TPU v7x, 32 devices: a whole 2x2x4 slice. The times are simulated.
32 devices in a mesh: dp: 8 (over y, x, core), mp: 4 (over z).
Axes of the slice: x: 2, y: 2, z: 4, core: 2. Of those that a mesh axis runs over, the one named last changes fastest.
Arguments:
- queries: bfloat16 [2048, 4096], P('dp', 'mp'), may hold values from -6 to 6
- enc_rows: bfloat16 [1024, 4096], P('dp', 'mp'), may hold values from -6 to 6
- key_weight: bfloat16 [4096, 4096], P(None, 'mp'), may hold values from -0.09375 to 0.09375
- value_weight: bfloat16 [4096, 4096], P(None, 'mp'), may hold values from -0.09375 to 0.09375
- enc_len: int32 [8, 8], P('dp'), may hold values from 1 to 64, 128 in all within a row
- dec_len: int32 [8, 8], P('dp'), may hold values from 1 to 128, 256 in all within a row
- route: int32 [8, 8], P('dp'), may hold values from 0 to 7, each once within a row
- out_grad: bfloat16 [2048, 4096], P('dp', 'mp'), may hold values from -6 to 6
Outputs:
- attended: bfloat16 [2048, 4096], P('dp', 'mp')
- query_grad: bfloat16 [2048, 4096], P('dp', 'mp')
- enc_grad: bfloat16 [1024, 4096], P('dp', 'mp')
- key_weight_grad: float32 [4096, 4096], P('dp', 'mp')
- value_weight_grad: float32 [4096, 4096], P('dp', 'mp')
Inputs may be any that keep to these rules, and one draw needn't show every extreme that they name: Every row of enc_len sums to 128, and its largest entry is exactly 64. Every row of dec_len sums to 256, and its largest entry is exactly 128. Every row of route is a permutation of the data shards, so each decoder shard receives exactly one example from each shard.
All inputs are finite; a program needn't handle non-finite values.
Results may differ from a plain program's by a relative error of at most 0.013.
Values may be sent and summed in bfloat16 or wider, within the bound.
No kernel may reach another device: no remote copies, remote signals or barrier semaphores. Data moves between devices by JAX's collectives and lax.ppermute only.
A program may use at most 128 MiB of HBM per device.

v0:
```python
import jax
import jax.numpy as jnp
from jax import lax
from jax.sharding import PartitionSpec as P

HD = 256


def attend(q_rows, g_rows, key_buf, val_buf, counts, dec_lens, slot_rows):
    rows = q_rows.shape[0]
    keys_n = key_buf.shape[0]
    heads = q_rows.shape[1] // HD
    scale = HD ** (-0.5)
    query_h = q_rows.reshape(rows, heads, HD)
    grad_h = g_rows.reshape(rows, heads, HD)
    key_h = key_buf.reshape(keys_n, heads, HD)
    val_h = val_buf.reshape(keys_n, heads, HD)
    dec_ends = jnp.cumsum(dec_lens, dtype=jnp.int32)
    dec_pos = jnp.arange(rows, dtype=jnp.int32)
    dec_source = jnp.sum(
        (dec_ends[None, :] <= dec_pos[:, None]).astype(jnp.int32), axis=1, dtype=jnp.int32
    )
    key_pos = jnp.arange(keys_n, dtype=jnp.int32)
    key_source = key_pos // slot_rows
    key_live = key_pos % slot_rows < counts[key_source]
    allowed = (dec_source[:, None] == key_source[None, :]) & key_live[None, :]
    scores = jnp.einsum("qhd,khd->hqk", query_h, key_h, preferred_element_type=jnp.float32) * scale
    scores = jnp.where(allowed[None], scores, -jnp.inf)
    top = jnp.max(scores, axis=-1, keepdims=True)
    expo = jnp.exp(scores - top)
    probs = expo / jnp.sum(expo, axis=-1, keepdims=True)
    weights = probs.astype(jnp.bfloat16)
    attended = jnp.einsum(
        "hqk,khd->qhd", weights, val_h, preferred_element_type=jnp.float32
    ).astype(jnp.bfloat16)
    dweights = jnp.einsum("qhd,khd->hqk", grad_h, val_h, preferred_element_type=jnp.float32)
    delta = jnp.sum(probs * dweights, axis=-1, keepdims=True)
    dscores = (probs * (dweights - delta) * scale).astype(jnp.bfloat16)
    query_grad = jnp.einsum(
        "hqk,khd->qhd", dscores, key_h, preferred_element_type=jnp.float32
    ).astype(jnp.bfloat16)
    key_grad = jnp.einsum(
        "hqk,qhd->khd", dscores, query_h, preferred_element_type=jnp.float32
    ).astype(jnp.bfloat16)
    value_grad = jnp.einsum(
        "hqk,qhd->khd", weights, grad_h, preferred_element_type=jnp.float32
    ).astype(jnp.bfloat16)
    width = heads * HD
    return (
        attended.reshape(rows, width),
        query_grad.reshape(rows, width),
        jnp.concatenate(
            [key_grad.reshape(keys_n, width), value_grad.reshape(keys_n, width)], axis=1
        ),
    )


def project_back(grads, key_weight, value_weight):
    width = key_weight.shape[1]
    contract_cols = (((1,), (1,)), ((), ()))
    return lax.dot_general(
        grads[:, :width], key_weight, contract_cols, preferred_element_type=jnp.float32
    ) + lax.dot_general(
        grads[:, width:], value_weight, contract_cols, preferred_element_type=jnp.float32
    )


def body(queries, enc_rows, key_weight, value_weight, enc_len, dec_len, route, out_grad):
    shards = lax.axis_size("dp")
    enc_dev = enc_rows.shape[0]
    slot_rows = 4 * enc_dev // shards
    width = key_weight.shape[1]
    model_width = key_weight.shape[0]
    lens = enc_len[0]
    targets = route[0]
    ends = jnp.cumsum(lens, dtype=jnp.int32)
    starts = ends - lens
    slots = jnp.arange(shards, dtype=jnp.int32)
    pick = targets[:, None] == slots[None, :]
    start_dest = jnp.sum(jnp.where(pick, starts[:, None], 0), axis=0, dtype=jnp.int32)
    len_dest = jnp.sum(jnp.where(pick, lens[:, None], 0), axis=0, dtype=jnp.int32)
    offsets = jnp.arange(slot_rows, dtype=jnp.int32)
    live = offsets[None, :] < len_dest[:, None]
    pack_index = jnp.where(live, start_dest[:, None] + offsets[None, :], 0).reshape(-1)
    live_flat = live.reshape(-1, 1)
    positions = jnp.arange(enc_dev, dtype=jnp.int32)
    owner = jnp.sum(
        (ends[None, :] <= positions[:, None]).astype(jnp.int32), axis=1, dtype=jnp.int32
    )
    own_pick = owner[:, None] == slots[None, :]
    dest_row = jnp.sum(jnp.where(own_pick, targets[None, :], 0), axis=1, dtype=jnp.int32)
    start_row = jnp.sum(jnp.where(own_pick, starts[None, :], 0), axis=1, dtype=jnp.int32)
    unpack_index = dest_row * slot_rows + positions - start_row
    zero_bf = jnp.zeros((), jnp.bfloat16)
    length_col = len_dest.reshape(shards, 1)
    contract_rows = (((0,), (0,)), ((), ()))
    row_buf = jnp.where(live_flat, enc_rows[pack_index], zero_bf).reshape(shards, slot_rows, -1)
    got, counts = (
        lax.all_to_all(row_buf, "dp", split_axis=0, concat_axis=0, tiled=True),
        lax.all_to_all(length_col, "dp", split_axis=0, concat_axis=0, tiled=True),
    )
    full_buf = lax.all_gather(got, "mp", axis=2, tiled=True).reshape(
        shards * slot_rows, model_width
    )
    key_buf = jnp.dot(full_buf, key_weight, preferred_element_type=jnp.float32).astype(jnp.bfloat16)
    val_buf = jnp.dot(full_buf, value_weight, preferred_element_type=jnp.float32).astype(
        jnp.bfloat16
    )
    counts = counts.reshape(shards)
    attended, query_grad, slot_grads = attend(
        queries, out_grad, key_buf, val_buf, counts, dec_len[0], slot_rows
    )
    slot_dx = project_back(slot_grads, key_weight, value_weight)
    slot_sum = lax.psum_scatter(slot_dx, "mp", scatter_dimension=1, tiled=True).astype(jnp.bfloat16)
    returned = lax.all_to_all(
        slot_sum.reshape(shards, slot_rows, -1), "dp", split_axis=0, concat_axis=0, tiled=True
    )
    enc_grad = returned.reshape(shards * slot_rows, -1)[unpack_index]
    weight_grad = lax.psum_scatter(
        lax.dot_general(full_buf, slot_grads, contract_rows, preferred_element_type=jnp.float32),
        "dp",
        scatter_dimension=0,
        tiled=True,
    )
    return (attended, query_grad, enc_grad, weight_grad[:, :width], weight_grad[:, width:])


def solution(mesh):
    in_specs = (
        P("dp", "mp"),
        P("dp", "mp"),
        P(None, "mp"),
        P(None, "mp"),
        P("dp", None),
        P("dp", None),
        P("dp", None),
        P("dp", "mp"),
    )
    out_specs = (P("dp", "mp"), P("dp", "mp"), P("dp", "mp"), P("dp", "mp"), P("dp", "mp"))
    return jax.shard_map(body, mesh=mesh, in_specs=in_specs, out_specs=out_specs, check_vma=False)
```

profile of v0, /device:TPU:0, one launch (start us, length us, event | category | flops | bytes accessed | tf_op | source)
XLA Modules:
  0.0 526.5 jit_solution(16006657597312556272)
XLA Ops:
  9.8 2.1 gather_fusion
  12.0 20.6 %all_to_all.19 = bf16[8,64,1024]{2,1,0:T(8,128)(2,1)} all-to-all(bf16[8,64,1024]{2,1,0:T(8,128)(2,1)S(1)} %broadcast_select_fusion), channel_id=1, replica_groups=mesh['dp'=8,'mp'=4] {'dp'}, dimensions={0} | all-to-all | bytes 2097152 | tf_op jit(solution)/shard_map/all_to_all | solution.py:99
  33.3 3.3 all-to-all-start.1
  37.4 3.7 all-to-all-done.1
  41.7 4.5 compare_select_fusion.2
  47.1 65.8 %all-gather.2.cloned.1.call-done = bf16[8,64,4096]{2,1,0:T(8,128)(2,1)} async-done(((bf16[8,64,1024]{2,1,0:T(8,128)(2,1)}), bf16[8,64,4096]{2,1,0:T(8,128)(2,1)}) %all-gather.2.cloned.1.call-update) | async-done | bytes 4194320 | tf_op jit(solution)/shard_map/all_gather | solution.py:102
  112.9 9.1 %convolution_convert_fusion = bf16[512,1024]{1,0:T(8,128)(2,1)S(1)} fusion(bf16[512,4096]{1,0:T(8,128)(2,1)} %bitcast.120, bf16[4096,1024]{1,0:T(8,128)(2,1)} %param.10), kind=kOutput, calls=%fused_computation.17 | convolution fusion | flops 4295491584 | bytes 13631488 | tf_op jit(solution)/shard_map/dot_general | solution.py:105
  123.4 9.1 %convolution_convert_fusion.1 = bf16[512,1024]{1,0:T(8,128)(2,1)S(1)} fusion(bf16[512,4096]{1,0:T(8,128)(2,1)} %bitcast.121, bf16[4096,1024]{1,0:T(8,128)(2,1)} %param.11), kind=kOutput, calls=%fused_computation.18 | convolution fusion | flops 4295491584 | bytes 13631488 | tf_op jit(solution)/shard_map/dot_general | solution.py:106
  133.9 3.4 fusion.42
  137.4 3.1 convolution_convert_fusion.2
  140.4 4.1 convolution_convert_fusion.3
  144.5 7.4 %fusion.43 = f32[512,4096]{1,0:T(8,128)S(1)} fusion(bf16[512,1024]{0,1:T(8,128)(2,1)} %bitcast.126, bf16[4096,1024]{1,0:T(8,128)(2,1)} %param.10), kind=kOutput, calls=%fused_computation.94 | convolution fusion | flops 4294967296 | bytes 17825792 | tf_op jit(solution)/shard_map/dot_general | solution.py:61
  151.9 10.5 %convolution_add_fusion = f32[512,4096]{1,0:T(8,128)} fusion(f32[512,4096]{1,0:T(8,128)S(1)} %fusion.43, bf16[512,1024]{0,1:T(8,128)(2,1)S(1)} %bitcast.124, bf16[4096,1024]{1,0:T(8,128)(2,1)} %param.11), kind=kOutput, calls=%fused_computation.4 | convolution fusion | flops 4297064448 | bytes 26214400 | tf_op jit(solution)/shard_map/dot_general | solution.py:63
  162.5 17.3 %fusion.2 = f32[4096,2048]{1,0:T(8,128)} fusion(bf16[512,4096]{1,0:T(8,128)(2,1)} %bitcast.122, bf16[512,1024]{0,1:T(8,128)(2,1)S(1)} %bitcast.125, bf16[512,1024]{0,1:T(8,128)(2,1)} %bitcast.127), kind=kOutput, calls=%fused_computation.5 | convolution fusion | flops 8594128896 | bytes 39845888 | tf_op jit(solution)/shard_map/dot_general | solution.py:120
  180.5 125.1 %reduce-scatter.3.cloned.1.call-done = f32[512,1024]{1,0:T(8,128)} async-done(((f32[512,4096]{1,0:T(8,128)}), f32[512,1024]{1,0:T(8,128)}) %reduce-scatter.3.cloned.1.call-update) | async-done | bytes 2097168 | tf_op jit(solution)/shard_map/reduce_scatter | solution.py:114
  305.6 2.7 convert_element_type.58
  308.3 3.7 all-to-all-start.2
  312.0 3.3 convolution_convert_fusion.5
  315.2 2.1 copy.55
  317.3 5.3 %convolution_convert_fusion.4 = bf16[4,256,256]{2,1,0:T(8,128)(2,1)} fusion(bf16[512,4,256]{0,2,1:T(8,128)(2,1)} %bitcast.108, f32[4,512,256]{2,1,0:T(8,128)S(1)} %fusion.11, f32[4,256,512]{1,2,0:T(8,128)} %get-tuple-element.35, f32[4,256]{1,0:T(4,128)S(1)} %get-tuple-element.34), kind=kOutput, calls=%fused_computation.21 | convolution fusion | flops 272369152 | bytes 5771264 | tf_op jit(solution)/shard_map/hqk,khd->qhd/dot_general | solution.py:39
  322.6 2.1 copy.56
  324.7 2.7 all-to-all-done.2
  328.9 186.2 %reduce-scatter.5.cloned.1.call-done = f32[512,2048]{1,0:T(8,128)} async-done(((f32[4096,2048]{1,0:T(8,128)}), f32[512,2048]{1,0:T(8,128)}) %reduce-scatter.5.cloned.1.call-update) | async-done | bytes 4194320 | tf_op jit(solution)/shard_map/reduce_scatter | solution.py:119
  515.1 4.9 fusion.40
  (51 shorter events, 10.8 us)
Async XLA Ops:
  7.2 2.6 copy-start
  7.2 105.7 %all-gather.2.cloned.1.call-start = ((), (), s32[]{:S(2)}) async-start(), calls=%async_computation.5 | async-start | bytes 5242880 | tf_op jit(solution)/shard_map/all_gather | solution.py:102
  12.0 24.7 %copy-start.7 = (s32[1,8]{1,0:T(1,128)S(1)}, s32[1,8]{1,0:T(1,128)}, u32[]{:S(2)}) copy-start(s32[1,8]{1,0:T(1,128)} %param.13) | copy-start | bytes 100
  12.0 24.9 %copy-start.3 = (bf16[256,1024]{1,0:T(8,128)(2,1)S(1)}, bf16[256,1024]{1,0:T(8,128)(2,1)}, u32[]{:S(2)}) copy-start(bf16[256,1024]{1,0:T(8,128)(2,1)} %param.8) | copy-start | bytes 1572868
  12.0 25.1 %copy-start.4 = (bf16[256,1024]{1,0:T(8,128)(2,1)S(1)}, bf16[256,1024]{1,0:T(8,128)(2,1)}, u32[]{:S(2)}) copy-start(bf16[256,1024]{1,0:T(8,128)(2,1)} %param.15) | copy-start | bytes 1572868
  33.3 7.8 %all-to-all-start.1 = ((s32[8,1,1]{2,1,0:T(1,128)}), s32[8,1,1]{2,1,0:T(1,128)S(1)}, u32[]{:S(2)}, u32[]{:S(2)}) async-start(s32[8,1,1]{2,1,0:T(1,128)} %copy.42), calls=%async_computation.1 | async-start | bytes 8192 | tf_op jit(solution)/shard_map/all_to_all | solution.py:100
  36.6 269.0 %reduce-scatter.3.cloned.1.call-start = ((), (), s32[]{:S(2)}) async-start(), calls=%async_computation.6 | async-start | bytes 10485760 | tf_op jit(solution)/shard_map/reduce_scatter | solution.py:114
  132.5 1.0 copy-start.2
  144.5 7.4 %copy-start.8 = (bf16[4,512,256]{1,2,0:T(8,128)(2,1)S(1)}, bf16[4,512,256]{1,2,0:T(8,128)(2,1)}, u32[]{:S(2)}) copy-start(bf16[4,512,256]{1,2,0:T(8,128)(2,1)} %convolution_convert_fusion.2) | copy-start | bytes 3145732
  162.4 352.7 %reduce-scatter.5.cloned.1.call-start = ((), (), s32[]{:S(2)}) async-start(), calls=%async_computation.7 | async-start | bytes 37748736 | tf_op jit(solution)/shard_map/reduce_scatter | solution.py:119
  179.7 0.7 copy-start.6
  179.7 0.7 copy-start.5
  308.3 19.1 %all-to-all-start.2 = ((bf16[8,64,1024]{2,1,0:T(8,128)(2,1)}), bf16[8,64,1024]{2,1,0:T(8,128)(2,1)S(1)}, u32[]{:S(2)}, u32[]{:S(2)}) async-start(bf16[8,64,1024]{2,1,0:T(8,128)(2,1)} %bitcast.29), calls=%async_computation.3 | async-start | bytes 2097152 | tf_op jit(solution)/shard_map/all_to_all | solution.py:115
  515.1 4.9 copy-start.1
Sparse Core Ops, SparseCore 0:
  32.7 80.1 all-gather.1
  162.5 142.9 reduce-scatter.2
  309.1 205.9 reduce-scatter.4
where the time goes:
time: 527 us
  waiting for transfers between devices  384 us (73%)
  matrix products  73 us (14%)
  blocking collectives  20.6 us (4%)
  local copies, waits for them, and re-layouts  17.3 us (3%)
  between operations  13.9 us (3%)
  other arithmetic  11.2 us (2%)
  starting transfers between devices  7.09 us (1%)
    reduce_scatter x1, waiting for transfers between devices, body(): lax.psum_scatter(lax.dot_general(full_buf, slot_grads, contract_rows, pre...  186 us
    reduce_scatter x1, waiting for transfers between devices, body(): lax.psum_scatter(slot_dx, 'mp', scatter_dimension=1, tiled=True)  125 us
    all_gather x1, waiting for transfers between devices, body(): lax.all_gather(got, 'mp', axis=2, tiled=True)  65.8 us
    all_to_all x1, blocking collectives, body(): lax.all_to_all(row_buf, 'dp', split_axis=0, concat_axis=0, tiled=True)  20.6 us
    dot_general x1, matrix products, body(): lax.dot_general(full_buf, slot_grads, contract_rows, preferred_element_ty...  17.3 us
  transfers between devices with their start and end apart: 5, of which 5 were waited for; matrix products, arithmetic and copies ran while one was open for 8% of the time, Pallas kernels for 0%

commit v1 on v0

v1 whole, which is shorter than its diff:
```python
import functools

import jax
import jax.numpy as jnp
from jax import lax
from jax.experimental import pallas as pl
from jax.experimental.pallas import tpu as pltpu
from jax.sharding import PartitionSpec as P

HD = 256
NT = (((1,), (1,)), ((), ()))
NN = (((1,), (0,)), ((), ()))
TN = (((0,), (0,)), ((), ()))


def mm(a, b, dims):
    return lax.dot_general(a, b, dims, preferred_element_type=jnp.float32)


def attend_kernel(enc_dev, table, dec_len, q_ref, g_ref, k_ref, v_ref, att_ref, qg_ref, kg_ref, vg_ref, open_ref):
    rows = q_ref.shape[0]
    keys_n = k_ref.shape[0]
    shards = dec_len.shape[1]
    scale = HD ** (-0.5)

    @pl.when(pl.program_id(0) == 0)
    def _():
        row = lax.broadcasted_iota(jnp.int32, (rows, 128), 0)
        low = jnp.zeros((rows, 128), jnp.int32)
        high = jnp.zeros((rows, 128), jnp.int32)
        begin = jnp.int32(0)
        for s in range(shards):
            low = jnp.where(row >= begin, table[0, s], low)
            high = jnp.where(row >= begin, table[1, s], high)
            begin = begin + dec_len[0, s]
        for c in range(0, keys_n, 128):
            col = lax.broadcasted_iota(jnp.int32, (rows, 128), 1) + c
            inside = (col >= low) & (col < high)
            open_ref[:, c : c + 128] = jnp.where(inside, 0.0, -jnp.inf)

    q = q_ref[...]
    g = g_ref[...]
    k = k_ref[...]
    v = v_ref[...]
    scores = mm(q, k, NT) * scale + open_ref[...]
    top = jnp.max(scores, axis=1, keepdims=True)
    expo = jnp.exp(scores - top)
    probs = expo * (1.0 / jnp.sum(expo, axis=1, keepdims=True))
    weights = probs.astype(jnp.bfloat16)
    att_ref[...] = mm(weights, v, NN).astype(jnp.bfloat16)
    vg_ref[...] = mm(weights, g, TN).astype(jnp.bfloat16)
    dweights = mm(g, v, NT)
    delta = jnp.sum(probs * dweights, axis=1, keepdims=True)
    dscores = (probs * (dweights - delta) * scale).astype(jnp.bfloat16)
    qg_ref[...] = mm(dscores, k, NN).astype(jnp.bfloat16)
    kg_ref[...] = mm(dscores, q, TN).astype(jnp.bfloat16)


def attend(queries, out_grad, keys, values, table, dec_len, enc_dev):
    rows, width = queries.shape
    keys_n = keys.shape[0]
    heads = width // HD
    row_spec = pl.BlockSpec((rows, HD), lambda h, *_: (0, h))
    key_spec = pl.BlockSpec((keys_n, HD), lambda h, *_: (0, h))
    row_out = jax.ShapeDtypeStruct((rows, width), jnp.bfloat16)
    key_out = jax.ShapeDtypeStruct((keys_n, width), jnp.bfloat16)
    return pl.pallas_call(
        functools.partial(attend_kernel, enc_dev),
        grid_spec=pltpu.PrefetchScalarGridSpec(
            num_scalar_prefetch=2,
            grid=(heads,),
            in_specs=[row_spec, row_spec, key_spec, key_spec],
            out_specs=[row_spec, row_spec, key_spec, key_spec],
            scratch_shapes=[pltpu.VMEM((rows, keys_n), jnp.float32)],
        ),
        out_shape=[row_out, row_out, key_out, key_out],
        compiler_params=pltpu.CompilerParams(vmem_limit_bytes=56 * 2**20),
        cost_estimate=pl.CostEstimate(
            flops=12 * rows * keys_n * width,
            bytes_accessed=2 * (4 * rows * width + 4 * keys_n * width),
            transcendentals=rows * keys_n * heads,
        ),
    )(table, dec_len, queries, out_grad, keys, values)


def body(queries, enc_rows, key_weight, value_weight, enc_len, dec_len, route, out_grad):
    shards = lax.axis_size("dp")
    enc_dev = enc_rows.shape[0]
    me = lax.axis_index("dp")
    lens = enc_len[0]
    targets = route[0]
    order = jnp.arange(shards, dtype=jnp.int32)
    before = order[None, :] < order[:, None]
    starts = jnp.sum(jnp.where(before, lens[None, :], 0), axis=1, dtype=jnp.int32)
    pick = targets[:, None] == order[None, :]
    bounds = me * enc_dev + jnp.stack([starts, starts + lens], axis=1)
    to_dest = jnp.sum(jnp.where(pick[:, :, None], bounds[:, None, :], 0), axis=0, dtype=jnp.int32)
    table = lax.all_to_all(to_dest.reshape(shards, 2), "dp", split_axis=0, concat_axis=0, tiled=True).T

    full = lax.all_gather(enc_rows, "mp", axis=1, tiled=True)
    own_keys = mm(full, key_weight, NN).astype(jnp.bfloat16)
    keys = lax.all_gather(own_keys, "dp", axis=0, tiled=True)
    own_values = mm(full, value_weight, NN).astype(jnp.bfloat16)
    values = lax.all_gather(own_values, "dp", axis=0, tiled=True)
    columns = lax.all_to_all(full, "dp", split_axis=1, concat_axis=0, tiled=True)

    attended, query_grad, key_part, value_part = attend(
        queries, out_grad, keys, values, table, dec_len, enc_dev
    )
    own_vg = lax.psum_scatter(value_part, "dp", scatter_dimension=0, tiled=True)
    own_kg = lax.psum_scatter(key_part, "dp", scatter_dimension=0, tiled=True)
    value_grad = lax.all_gather(own_vg, "dp", axis=0, tiled=True)
    key_grad = lax.all_gather(own_kg, "dp", axis=0, tiled=True)
    part = mm(own_kg, key_weight, NT) + mm(own_vg, value_weight, NT)
    enc_grad = lax.psum_scatter(part.astype(jnp.bfloat16), "mp", scatter_dimension=1, tiled=True)
    value_weight_grad = mm(columns, value_grad, TN)
    key_weight_grad = mm(columns, key_grad, TN)
    return (attended, query_grad, enc_grad, key_weight_grad, value_weight_grad)


def solution(mesh):
    in_specs = (
        P("dp", "mp"),
        P("dp", "mp"),
        P(None, "mp"),
        P(None, "mp"),
        P("dp", None),
        P("dp", None),
        P("dp", None),
        P("dp", "mp"),
    )
    out_specs = (P("dp", "mp"), P("dp", "mp"), P("dp", "mp"), P("dp", "mp"), P("dp", "mp"))
    return jax.shard_map(body, mesh=mesh, in_specs=in_specs, out_specs=out_specs, check_vma=False)
```

time: 527 us -> 306 us (0.58)
  waiting for transfers between devices: 384 us -> 212 us
  matrix products: 73 us -> 30.7 us
  other arithmetic: 11.2 us -> 0.3 us
  blocking collectives: 20.6 us -> 31.5 us
  local copies, waits for them, and re-layouts: 17.3 us -> 6.69 us
  Pallas kernels: 0 us -> 9.99 us
  starting transfers between devices: 7.09 us -> 0.32 us
    reduce_scatter x2 -> x3, waiting for transfers between devices: 311 us -> 111 us  [the longest x1 45.2 us: body(): own_vg = lax.psum_scatter(value_part, 'dp', scatter_dimension=0, tiled=True)]
    dot_general x10 -> x6, matrix products: 69.6 us -> 30.7 us  [mm(): return lax.dot_general(a, b, dims, preferred_element_type=jnp.float32)]
    all_gather x1 -> x5, waiting for transfers between devices: 65.8 us -> 100 us  [the longest x1 31.7 us: body(): full = lax.all_gather(enc_rows, 'mp', axis=1, tiled=True)]
    all_to_all x1 -> x2, blocking collectives: 20.6 us -> 31.5 us  [the longest x1 23.4 us: body(): lax.all_to_all(full, 'dp', split_axis=1, concat_axis=0, tiled=True)]
    pallas_call x0 -> x1, Pallas kernels: none -> 9.99 us  [attend(): pl.pallas_call(functools.partial(attend_kernel, enc_dev), grid_spec=pltpu...]
    all_to_all x2 -> x0, starting transfers between devices: 6.96 us -> none  [the longest x1 3.65 us: body(): lax.all_to_all(slot_sum.reshape(shards, slot_rows, -1), 'dp', split_axis=...]
    all_to_all x2 -> x0, waiting for transfers between devices: 6.37 us -> none  [the longest x1 3.72 us: body(): lax.all_to_all(length_col, 'dp', split_axis=0, concat_axis=0, tiled=True)]
  transfers between devices with their start and end apart: 5 -> 8, of which waited for: 5 -> 7; matrix products, arithmetic and copies ran while one was open for 8% -> 10% of each run, Pallas kernels for 0% -> 0%
where the time goes in v1:
time: 306 us
  waiting for transfers between devices  212 us (69%)
  blocking collectives  31.5 us (10%)
  matrix products  30.7 us (10%)
  between operations  14.2 us (5%)
  Pallas kernels  9.99 us (3%)
  local copies, waits for them, and re-layouts  6.69 us (2%)
    reduce_scatter x1, waiting for transfers between devices, body(): own_vg = lax.psum_scatter(value_part, 'dp', scatter_dimension=0, tiled=True)  45.2 us
    reduce_scatter x1, waiting for transfers between devices, body(): own_kg = lax.psum_scatter(key_part, 'dp', scatter_dimension=0, tiled=True)  40.8 us
    all_gather x1, waiting for transfers between devices, body(): full = lax.all_gather(enc_rows, 'mp', axis=1, tiled=True)  31.7 us
    dot_general x6, matrix products, mm(): return lax.dot_general(a, b, dims, preferred_element_type=jnp.float32)  30.7 us
    all_gather x1, waiting for transfers between devices, body(): values = lax.all_gather(own_values, 'dp', axis=0, tiled=True)  30.4 us
    reduce_scatter x1, waiting for transfers between devices, body(): lax.psum_scatter(part.astype(jnp.bfloat16), 'mp', scatter_dimension=1, ti...  25.4 us
    all_gather x1, waiting for transfers between devices, body(): value_grad = lax.all_gather(own_vg, 'dp', axis=0, tiled=True)  25.3 us
    all_to_all x1, blocking collectives, body(): lax.all_to_all(full, 'dp', split_axis=1, concat_axis=0, tiled=True)  23.4 us
  transfers between devices with their start and end apart: 8, of which 7 were waited for; matrix products, arithmetic and copies ran while one was open for 10% of the time, Pallas kernels for 0%

profile of v1, /device:TPU:0, one launch (start us, length us, event | category | flops | bytes accessed | tf_op | source)
XLA Modules:
  0.0 306.1 jit_solution(13651561590257695765)
XLA Ops:
  7.2 1.8 copy.33
  9.1 31.7 %all-gather.6.cloned.1.call-done = bf16[128,4096]{0,1:T(8,128)(2,1)} async-done(((bf16[128,1024]{0,1:T(8,128)(2,1)}), bf16[128,4096]{0,1:T(8,128)(2,1)}) %all-gather.6.cloned.1.call-update) | async-done | bytes 1048592 | tf_op jit(solution)/shard_map/all_gather | solution.py:100
  40.8 5.8 %convolution_convert_fusion.1 = bf16[128,1024]{1,0:T(8,128)(2,1)} fusion(bf16[128,4096]{0,1:T(8,128)(2,1)} %all-gather.6.cloned.1.call-done, bf16[4096,1024]{1,0:T(8,128)(2,1)} %param.10), kind=kOutput, calls=%fused_computation.5 | convolution fusion | flops 1073872896 | bytes 9699328 | tf_op jit(solution)/shard_map/dot_general | solution.py:17
  46.7 5.4 %convolution_convert_fusion = bf16[128,1024]{1,0:T(8,128)(2,1)} fusion(bf16[128,4096]{0,1:T(8,128)(2,1)S(1)} %copy-done, bf16[4096,1024]{1,0:T(8,128)(2,1)} %param.11), kind=kOutput, calls=%fused_computation.4 | convolution fusion | flops 1073872896 | bytes 9699328 | tf_op jit(solution)/shard_map/dot_general | solution.py:17
  52.1 0.1 select_reduce_fusion.1
  52.4 0.1 select_reduce_fusion
  52.5 8.1 %all_to_all.31 = s32[8,1,2]{2,1,0:T(1,128)S(1)} all-to-all(s32[8,1,2]{2,1,0:T(1,128)S(1)} %copy.31), channel_id=1, replica_groups=mesh['dp'=8,'mp'=4] {'dp'}, dimensions={0} | all-to-all | bytes 128 | tf_op jit(solution)/shard_map/all_to_all | solution.py:98
  60.6 0.6 copy.32
  61.3 12.9 %all-gather.8.cloned.1.call-done.k_ref = bf16[1024,1024]{1,0:T(8,128)(2,1)} async-done(((bf16[128,1024]{1,0:T(8,128)(2,1)}), bf16[1024,1024]{1,0:T(8,128)(2,1)}) %all-gather.8.cloned.1.call-update) | async-done | bytes 2097168 | tf_op jit(solution)/shard_map/all_gather | solution.py:102
  74.2 30.4 %all-gather.10.cloned.1.call-done.v_ref = bf16[1024,1024]{1,0:T(8,128)(2,1)} async-done(((bf16[128,1024]{1,0:T(8,128)(2,1)}), bf16[1024,1024]{1,0:T(8,128)(2,1)}) %all-gather.10.cloned.1.call-update) | async-done | bytes 2097168 | tf_op jit(solution)/shard_map/all_gather | solution.py:104
  104.6 10.0 %shard_map.119 = (bf16[256,1024]{1,0:T(8,128)(2,1)}, bf16[256,1024]{1,0:T(8,128)(2,1)}, bf16[1024,1024]{1,0:T(8,128)(2,1)}, bf16[1024,1024]{1,0:T(8,128)(2,1)}) custom-call(s32[2,8]{1,0:T(2,128)} %bitcast.34, s32[1,8]{1,0:T(1,128)} %dec_len.1, bf16[256,1024]{1,0:T(8,128)(2,1)} %q_ref.1, bf16[256,1024]{1,0:T(8,128)(2,1)} %g_ref.1, ...), custom_call_target="tpu_custom_call" | custom-call | flops 3221225472 | bytes 10485760 | tf_op jit(solution)/shard_map/pallas_call | solution.py:67
  114.7 0.5 reduce-scatter.6.cloned.1.call-update
  115.2 40.8 %reduce-scatter.4.cloned.1.call-done = bf16[128,1024]{1,0:T(8,128)(2,1)} async-done(((bf16[1024,1024]{1,0:T(8,128)(2,1)}), bf16[128,1024]{1,0:T(8,128)(2,1)}) %reduce-scatter.4.cloned.1.call-update) | async-done | bytes 262160 | tf_op jit(solution)/shard_map/reduce_scatter | solution.py:111
  156.1 45.2 %reduce-scatter.6.cloned.1.call-done = bf16[128,1024]{1,0:T(8,128)(2,1)} async-done(((bf16[1024,1024]{1,0:T(8,128)(2,1)}), bf16[128,1024]{1,0:T(8,128)(2,1)}) %reduce-scatter.6.cloned.1.call-update) | async-done | bytes 262160 | tf_op jit(solution)/shard_map/reduce_scatter | solution.py:110
  201.4 6.4 %fusion.1 = f32[128,4096]{1,0:T(8,128)S(1)} fusion(bf16[128,1024]{1,0:T(8,128)(2,1)} %reduce-scatter.4.cloned.1.call-done, bf16[4096,1024]{1,0:T(8,128)(2,1)} %param.10), kind=kOutput, calls=%fused_computation.12 | convolution fusion | flops 1073741824 | bytes 10747904 | tf_op jit(solution)/shard_map/dot_general | solution.py:17
  207.8 7.4 %fusion = bf16[128,4096]{1,0:T(8,128)(2,1)} fusion(f32[128,4096]{1,0:T(8,128)S(1)} %fusion.1, bf16[128,1024]{1,0:T(8,128)(2,1)S(1)} %copy-done.1, bf16[4096,1024]{1,0:T(8,128)(2,1)} %param.11), kind=kOutput, calls=%fused_computation.1 | convolution fusion | flops 1074790400 | bytes 11796480 | tf_op jit(solution)/shard_map/dot_general | solution.py:17
  215.2 23.4 %all_to_all.32 = bf16[128,8,512]{0,2,1:T(8,128)(2,1)S(1)} all-to-all(bf16[128,8,512]{0,2,1:T(8,128)(2,1)S(1)} %bitcast.29), channel_id=1, replica_groups=mesh['dp'=8,'mp'=4] {'dp'}, dimensions={1} | all-to-all | bytes 2097152 | tf_op jit(solution)/shard_map/all_to_all | solution.py:105
  238.7 0.5 copy.34
  239.2 2.9 convolution_bitcast_fusion.1
  242.1 1.8 copy.35
  243.9 25.3 %all-gather.14.cloned.1.call-done = bf16[1024,1024]{1,0:T(8,128)(2,1)} async-done(((bf16[128,1024]{1,0:T(8,128)(2,1)}), bf16[1024,1024]{1,0:T(8,128)(2,1)}) %all-gather.14.cloned.1.call-update) | async-done | bytes 2097168 | tf_op jit(solution)/shard_map/all_gather | solution.py:112
  269.2 2.9 convolution_bitcast_fusion
  272.1 1.8 copy.36
  273.9 25.4 %reduce-scatter.8.cloned.1.call-done = bf16[128,1024]{1,0:T(8,128)(2,1)} async-done(((bf16[128,4096]{1,0:T(8,128)(2,1)}), bf16[128,1024]{1,0:T(8,128)(2,1)}) %reduce-scatter.8.cloned.1.call-update) | async-done | bytes 262160 | tf_op jit(solution)/shard_map/reduce_scatter | solution.py:115
  (28 shorter events, 0.7 us)
Async XLA Ops:
  7.2 33.6 %all-gather.6.cloned.1.call-start = ((), (), s32[]{:S(2)}) async-start(), calls=%async_computation.5 | async-start | bytes 1310720 | tf_op jit(solution)/shard_map/all_gather | solution.py:100
  9.0 65.2 %all-gather.8.cloned.1.call-start = ((), (), s32[]{:S(2)}) async-start(), calls=%async_computation.6 | async-start | bytes 2359296 | tf_op jit(solution)/shard_map/all_gather | solution.py:102
  40.8 5.9 %copy-start = (bf16[128,4096]{0,1:T(8,128)(2,1)S(1)}, bf16[128,4096]{0,1:T(8,128)(2,1)}, u32[]{:S(2)}) copy-start(bf16[128,4096]{0,1:T(8,128)(2,1)} %all-gather.6.cloned.1.call-done) | copy-start | bytes 3145732
  46.6 5.5 %copy-start.2 = (s32[1,8]{1,0:T(1,128)S(1)}, s32[1,8]{1,0:T(1,128)}, u32[]{:S(2)}) copy-start(s32[1,8]{1,0:T(1,128)} %param.12) | copy-start | bytes 100
  46.6 5.7 %copy-start.3 = (s32[1,8]{1,0:T(1,128)S(1)}, s32[1,8]{1,0:T(1,128)}, u32[]{:S(2)}) copy-start(s32[1,8]{1,0:T(1,128)} %param.14) | copy-start | bytes 100
  46.6 58.0 %all-gather.10.cloned.1.call-start = ((), (), s32[]{:S(2)}) async-start(), calls=%async_computation.7 | async-start | bytes 2359296 | tf_op jit(solution)/shard_map/all_gather | solution.py:104
  52.1 103.9 %reduce-scatter.4.cloned.1.call-start = ((), (), s32[]{:S(2)}) async-start(), calls=%async_computation.8 | async-start | bytes 2359296 | tf_op jit(solution)/shard_map/reduce_scatter | solution.py:111
  114.6 86.7 %reduce-scatter.6.cloned.1.call-start = ((), (), s32[]{:S(2)}) async-start(), calls=%async_computation.9 | async-start | bytes 2359296 | tf_op jit(solution)/shard_map/reduce_scatter | solution.py:110
  115.2 124.0 %all-gather.12.cloned.1.call-start = ((), (), s32[]{:S(2)}) async-start(), calls=%async_computation.11 | async-start | bytes 2359296 | tf_op jit(solution)/shard_map/all_gather | solution.py:113
  156.0 113.2 %all-gather.14.cloned.1.call-start = ((), (), s32[]{:S(2)}) async-start(), calls=%async_computation.12 | async-start | bytes 2359296 | tf_op jit(solution)/shard_map/all_gather | solution.py:112
  201.3 6.4 %copy-start.1 = (bf16[128,1024]{1,0:T(8,128)(2,1)S(1)}, bf16[128,1024]{1,0:T(8,128)(2,1)}, u32[]{:S(2)}) copy-start(bf16[128,1024]{1,0:T(8,128)(2,1)} %reduce-scatter.6.cloned.1.call-done) | copy-start | bytes 786436
  201.3 97.9 %reduce-scatter.8.cloned.1.call-start = ((), (), s32[]{:S(2)}) async-start(), calls=%async_computation.10 | async-start | bytes 1310720 | tf_op jit(solution)/shard_map/reduce_scatter | solution.py:115
Sparse Core Ops, SparseCore 0:
  10.1 30.6 all-gather.5
  46.7 27.4 all-gather.7
  76.7 27.8 all-gather.9
  114.7 41.2 reduce-scatter.3
  160.1 41.2 reduce-scatter.5
  203.1 35.1 all-gather.11
  240.1 29.0 all-gather.13
  272.1 27.1 reduce-scatter.7

commit v2 on v1

v2 whole, which is shorter than its diff:
```python
import functools

import jax
import jax.numpy as jnp
from jax import lax
from jax.experimental import pallas as pl
from jax.experimental.pallas import tpu as pltpu
from jax.sharding import PartitionSpec as P

HD = 256
GROUPS = 2
NT = (((1,), (1,)), ((), ()))
NN = (((1,), (0,)), ((), ()))
TN = (((0,), (0,)), ((), ()))
SMEM = pl.BlockSpec(memory_space=pltpu.SMEM)
BF16 = jnp.bfloat16
F32 = jnp.float32


def mm(a, b, dims):
    return lax.dot_general(a, b, dims, preferred_element_type=F32)


def params(mib):
    return pltpu.CompilerParams(vmem_limit_bytes=mib * 2**20)


def cost(flops, nbytes, exps=0):
    return pl.CostEstimate(flops=flops, bytes_accessed=nbytes, transcendentals=exps)


def whole(shape):
    return pl.BlockSpec(shape, lambda *_: (0,) * len(shape))


def build_select(sel_ref, me, lens, route, slot):
    shards = lens.shape[1]
    packed = sel_ref.shape[1]
    i = lax.broadcasted_iota(jnp.int32, (slot, packed), 0)
    row = lax.broadcasted_iota(jnp.int32, (slot, packed), 1)
    for r in range(shards):
        target = me ^ r
        start, length, total = jnp.int32(0), jnp.int32(0), jnp.int32(0)
        for j in range(shards):
            hit = route[0, j] == target
            start = jnp.where(hit, total, start)
            length = jnp.where(hit, lens[0, j], length)
            total = total + lens[0, j]
        picked = (row == i + start) & (i < length)
        sel_ref[pl.ds(r * slot, slot), :] = jnp.where(picked, 1.0, 0.0).astype(BF16)


def first_kernel(at, enc_ref, kw_ref, vw_ref, out_ref):
    gw = kw_ref.shape[1]
    enc = enc_ref[...]
    out_ref[:, :gw] = mm(enc, kw_ref[...], NN)
    out_ref[:, gw:] = mm(enc, vw_ref[...], NN)


def first_block(at, enc, key_weight, value_weight):
    rows, depth = enc.shape
    width = key_weight.shape[1]
    gw = width // GROUPS
    w_spec = pl.BlockSpec((depth, gw), lambda g, at: (at[1], g))
    return pl.pallas_call(
        first_kernel,
        grid_spec=pltpu.PrefetchScalarGridSpec(
            num_scalar_prefetch=1,
            grid=(GROUPS,),
            in_specs=[whole((rows, depth)), w_spec, w_spec],
            out_specs=pl.BlockSpec((rows, 2 * gw), lambda g, at: (0, g)),
        ),
        out_shape=jax.ShapeDtypeStruct((rows, 2 * width), F32),
        compiler_params=params(24),
        cost_estimate=cost(4 * rows * depth * width, 4 * depth * width),
    )(at, enc, key_weight, value_weight)


def project_kernel(others, slot, at, lens, route, part_ref, kw_ref, vw_ref, *refs):
    encs = refs[:others]
    outs = refs[others:-2]
    acc_ref, sel_ref = refs[-2:]
    step = pl.program_id(0)
    gw = kw_ref.shape[1]

    @pl.when(step == 0)
    def _():
        acc_ref[...] = part_ref[...]
        build_select(sel_ref, at[0], lens, route, slot)

    for n in range(others):

        @pl.when(step == n)
        def _():
            enc = encs[n][...]
            acc_ref[:, :gw] += mm(enc, kw_ref[...], NN)
            acc_ref[:, gw:] += mm(enc, vw_ref[...], NN)

    @pl.when(step == others - 1)
    def _():
        slots = mm(sel_ref[...], acc_ref[...].astype(BF16), NN).astype(BF16)
        for r, out in enumerate(outs):
            out[...] = slots[r * slot : (r + 1) * slot]


def project(g, slot, at, enc_len, route, part, key_weight, value_weight, encs):
    rows, depth = encs[0].shape
    shards = enc_len.shape[1]
    others = len(encs)
    gw = key_weight.shape[1] // GROUPS
    w_spec = pl.BlockSpec((depth, gw), lambda n, at, *_: ((at[1] + others - n) % (others + 1), g))
    return pl.pallas_call(
        functools.partial(project_kernel, others, slot),
        grid_spec=pltpu.PrefetchScalarGridSpec(
            num_scalar_prefetch=3,
            grid=(others,),
            in_specs=[pl.BlockSpec((rows, 2 * gw), lambda *_: (0, g)), w_spec, w_spec]
            + [whole((rows, depth))] * others,
            out_specs=[whole((slot, 2 * gw))] * shards,
            scratch_shapes=[pltpu.VMEM((rows, 2 * gw), F32), pltpu.VMEM((shards * slot, rows), BF16)],
        ),
        out_shape=[jax.ShapeDtypeStruct((slot, 2 * gw), BF16)] * shards,
        compiler_params=params(24),
        cost_estimate=cost(4 * others * rows * depth * gw, 4 * others * depth * gw),
    )(at, enc_len, route, part, key_weight, value_weight, *encs)


def split_kernel(blocks, shards, at, *refs):
    encs, outs, all_ref = refs[:blocks], refs[blocks:-1], refs[-1]
    size = outs[0].shape[1]
    per = encs[0].shape[1] // size
    for n, enc in enumerate(encs):
        for c in range(per):
            all_ref[n * per + c] = enc[:, c * size : (c + 1) * size]
    for r, out in enumerate(outs):
        target = at[0] ^ r
        n = lax.rem(at[1] + blocks - lax.div(target, per), blocks)
        out[...] = all_ref[n * per + lax.rem(target, per)]


def split_columns(at, encs, shards):
    rows, depth = encs[0].shape
    blocks = len(encs)
    size = blocks * depth // shards
    return pl.pallas_call(
        functools.partial(split_kernel, blocks, shards),
        grid_spec=pltpu.PrefetchScalarGridSpec(
            num_scalar_prefetch=1,
            grid=(1,),
            in_specs=[whole((rows, depth))] * blocks,
            out_specs=[whole((rows, size))] * shards,
            scratch_shapes=[pltpu.VMEM((shards, rows, size), BF16)],
        ),
        out_shape=[jax.ShapeDtypeStruct((rows, size), BF16)] * shards,
        compiler_params=params(16),
        cost_estimate=cost(0, 4 * blocks * rows * depth),
    )(at, *encs)


def attend_kernel(shards, slot, at, counts, dec_len, q_ref, g_ref, *refs):
    msgs = refs[:shards]
    refs = refs[-(2 + shards) - 3 :]
    att_ref, qg_ref = refs[:2]
    outs = refs[2 : 2 + shards]
    open_ref, key_ref, grad_ref = refs[2 + shards :]
    rows, gw = q_ref.shape
    keys_n = shards * slot
    scale = HD ** (-0.5)
    row = lax.broadcasted_iota(jnp.int32, (rows, 128), 0)
    low = jnp.zeros((rows, 128), jnp.int32)
    high = jnp.zeros((rows, 128), jnp.int32)
    begin = jnp.int32(0)
    for s in range(shards):
        place = (at[0] ^ s) * slot
        low = jnp.where(row >= begin, place, low)
        high = jnp.where(row >= begin, place + counts[s, 0], high)
        begin = begin + dec_len[0, s]
    for c in range(0, keys_n, 128):
        col = lax.broadcasted_iota(jnp.int32, (rows, 128), 1) + c
        open_ref[:, c : c + 128] = jnp.where((col >= low) & (col < high), 0.0, -jnp.inf)
    for r, msg in enumerate(msgs):
        key_ref[r * slot : (r + 1) * slot, :] = msg[...]
    for h in range(gw // HD):
        mine = slice(h * HD, (h + 1) * HD)
        theirs = slice(gw + h * HD, gw + (h + 1) * HD)
        q, g, k, v = q_ref[:, mine], g_ref[:, mine], key_ref[:, mine], key_ref[:, theirs]
        scores = mm(q, k, NT) * scale + open_ref[...]
        top = jnp.max(scores, axis=1, keepdims=True)
        expo = jnp.exp(scores - top)
        probs = expo * (1.0 / jnp.sum(expo, axis=1, keepdims=True))
        weights = probs.astype(BF16)
        att_ref[:, mine] = mm(weights, v, NN).astype(BF16)
        grad_ref[:, theirs] = mm(weights, g, TN).astype(BF16)
        dweights = mm(g, v, NT)
        delta = jnp.sum(probs * dweights, axis=1, keepdims=True)
        dscores = (probs * (dweights - delta) * scale).astype(BF16)
        qg_ref[:, mine] = mm(dscores, k, NN).astype(BF16)
        grad_ref[:, mine] = mm(dscores, q, TN).astype(BF16)
    for r, out in enumerate(outs):
        out[...] = grad_ref[r * slot : (r + 1) * slot, :]


def attend(g, slot, at, counts, dec_len, queries, out_grad, msgs, before):
    rows, width = queries.shape
    gw = width // GROUPS
    shards = len(msgs)
    keys_n = shards * slot
    row_spec = pl.BlockSpec((rows, gw), lambda *_: (0, g))
    row_out = jax.ShapeDtypeStruct((rows, width), BF16)
    return pl.pallas_call(
        functools.partial(attend_kernel, shards, slot),
        grid_spec=pltpu.PrefetchScalarGridSpec(
            num_scalar_prefetch=3,
            grid=(1,),
            in_specs=[row_spec] * 2
            + [whole((slot, 2 * gw))] * shards
            + [pl.BlockSpec(memory_space=pl.ANY)] * len(before),
            out_specs=[row_spec] * 2 + [whole((slot, 2 * gw))] * shards,
            scratch_shapes=[
                pltpu.VMEM((rows, keys_n), F32),
                pltpu.VMEM((keys_n, 2 * gw), BF16),
                pltpu.VMEM((keys_n, 2 * gw), BF16),
            ],
        ),
        out_shape=[row_out] * 2 + [jax.ShapeDtypeStruct((slot, 2 * gw), BF16)] * shards,
        input_output_aliases={5 + shards + n: n for n in range(len(before))},
        compiler_params=params(32),
        cost_estimate=cost(12 * rows * keys_n * gw, 8 * (rows + keys_n) * gw, rows * keys_n * (gw // HD)),
    )(at, counts, dec_len, queries, out_grad, *msgs, *before)


def unpack_kernel(shards, slot, at, lens, route, *refs):
    msgs, out_ref, sel_ref, all_ref = refs[:shards], refs[shards], refs[-2], refs[-1]
    build_select(sel_ref, at[0], lens, route, slot)
    for r, msg in enumerate(msgs):
        all_ref[r * slot : (r + 1) * slot, :] = msg[...]
    out_ref[...] = mm(sel_ref[...], all_ref[...], TN).astype(BF16)


def unpack(slot, at, enc_len, route, msgs):
    shards = len(msgs)
    rows = shards * slot // 4
    cols = msgs[0].shape[1]
    return pl.pallas_call(
        functools.partial(unpack_kernel, shards, slot),
        grid_spec=pltpu.PrefetchScalarGridSpec(
            num_scalar_prefetch=3,
            grid=(1,),
            in_specs=[whole((slot, cols))] * shards,
            out_specs=whole((rows, cols)),
            scratch_shapes=[pltpu.VMEM((shards * slot, rows), BF16), pltpu.VMEM((shards * slot, cols), BF16)],
        ),
        out_shape=jax.ShapeDtypeStruct((rows, cols), BF16),
        compiler_params=params(16),
        cost_estimate=cost(2 * shards * slot * rows * cols, 2 * shards * slot * cols),
    )(at, enc_len, route, *msgs)


def back_kernel(chunks, final, at, grad_ref, kw_ref, vw_ref, *refs):
    gw = kw_ref.shape[1]
    step = pl.program_id(0)
    total = mm(grad_ref[:, :gw], kw_ref[...], NT) + mm(grad_ref[:, gw:], vw_ref[...], NT)
    if not final:
        refs[0][0] = total
        return
    total = (total + refs[0][0]).astype(BF16)
    for n, out in enumerate(refs[1:]):

        @pl.when(step == n)
        def _():
            out[...] = total


def project_back(g, chunks, at, grads, key_weight, value_weight, part):
    rows, cols = grads.shape
    gw = cols // 2
    depth = key_weight.shape[0] // chunks
    final = part is not None
    w_spec = pl.BlockSpec((depth, gw), lambda n, at: ((at[1] + n) % chunks, g))
    part_spec = pl.BlockSpec((1, rows, depth), lambda n, at: (n, 0, 0))
    return pl.pallas_call(
        functools.partial(back_kernel, chunks, final),
        grid_spec=pltpu.PrefetchScalarGridSpec(
            num_scalar_prefetch=1,
            grid=(chunks,),
            in_specs=[whole((rows, cols)), w_spec, w_spec] + [part_spec] * final,
            out_specs=[whole((rows, depth))] * chunks if final else part_spec,
        ),
        out_shape=[jax.ShapeDtypeStruct((rows, depth), BF16)] * chunks
        if final
        else jax.ShapeDtypeStruct((chunks, rows, depth), F32),
        compiler_params=params(24),
        cost_estimate=cost(2 * rows * cols * depth * chunks, 2 * cols * depth * chunks),
    )(at, grads, key_weight, value_weight, *([part] if final else []))


def weight_grad_kernel(shards, *refs):
    cols, grads = refs[:shards], refs[shards : 2 * shards]
    kout, vout, col_ref, grad_ref = refs[-4:]
    gw = kout.shape[1]
    rows = cols[0].shape[0]
    for r in range(shards):
        col_ref[r * rows : (r + 1) * rows, :] = cols[r][...]
        grad_ref[r * rows : (r + 1) * rows, :] = grads[r][...]
    kout[...] = mm(col_ref[...], grad_ref[:, :gw], TN)
    vout[...] = mm(col_ref[...], grad_ref[:, gw:], TN)


def weight_grads(g, cols, grads, width, before):
    shards = len(cols)
    rows, size = cols[0].shape
    gw = width // GROUPS
    out_spec = pl.BlockSpec((size, gw), lambda *_: (0, g))
    return pl.pallas_call(
        functools.partial(weight_grad_kernel, shards),
        grid=(1,),
        in_specs=[whole((rows, size))] * shards
        + [whole((rows, 2 * gw))] * shards
        + [pl.BlockSpec(memory_space=pl.ANY)] * len(before),
        out_specs=[out_spec] * 2,
        scratch_shapes=[pltpu.VMEM((shards * rows, size), BF16), pltpu.VMEM((shards * rows, 2 * gw), BF16)],
        out_shape=[jax.ShapeDtypeStruct((size, width), F32)] * 2,
        input_output_aliases={2 * shards + n: n for n in range(len(before))},
        compiler_params=params(40),
        cost_estimate=cost(4 * shards * rows * size * gw, 2 * shards * rows * (size + 2 * gw) + 8 * size * gw),
    )(*cols, *grads, *before)


def body(queries, enc_rows, key_weight, value_weight, enc_len, dec_len, route, out_grad):
    shards = lax.axis_size("dp")
    peers = lax.axis_size("mp")
    enc_dev = enc_rows.shape[0]
    slot = 4 * enc_dev // shards
    width = key_weight.shape[1]
    at = jnp.stack([lax.axis_index("dp"), lax.axis_index("mp")]).astype(jnp.int32)

    def flip(x, r):
        return lax.ppermute(x, "dp", [(i, i ^ r) for i in range(shards)])

    def shift(x, r):
        return lax.ppermute(x, "mp", [(i, (i + r) % peers) for i in range(peers)])

    encs = [shift(enc_rows, r) for r in range(1, peers)]
    order = jnp.arange(shards, dtype=jnp.int32)
    pick = route[0][:, None] == order[None, :]
    sends = jnp.sum(jnp.where(pick, enc_len[0][:, None], 0), axis=0, dtype=jnp.int32)
    counts = lax.all_to_all(sends.reshape(shards, 1), "dp", split_axis=0, concat_axis=0, tiled=True)

    part = first_block(at, enc_rows, key_weight, value_weight)
    back_part = None
    rows_out = []
    weight_out = []
    held = []
    for g in range(GROUPS):
        slots = project(g, slot, at, enc_len, route, part, key_weight, value_weight, encs)
        held.append([slots[0]] + [flip(slots[r], r) for r in range(1, shards)])
    cols = split_columns(at, [enc_rows] + encs, shards)
    cols = [cols[0]] + [flip(cols[r], r) for r in range(1, shards)]
    for g in range(GROUPS):
        out = attend(g, slot, at, counts, dec_len, queries, out_grad, held[g], rows_out)
        rows_out = out[:2]
        msgs = [out[2]] + [flip(out[2 + r], r) for r in range(1, shards)]
        own = unpack(slot, at, enc_len, route, msgs)
        back_part = project_back(g, peers, at, own, key_weight, value_weight, back_part)
        grads = [own] + [None] * (shards - 1)
        for r in range(2, shards, 2):
            grads[r] = flip(own, r)
        for r in range(1, shards, 2):
            grads[r] = flip(grads[r - 1], 1)
        weight_out = weight_grads(g, cols, grads, width, weight_out)
    total = back_part[0].astype(F32)
    for r in range(1, peers):
        total = total + shift(back_part[r], r).astype(F32)
    return (rows_out[0], rows_out[1], total.astype(BF16), weight_out[0], weight_out[1])


def solution(mesh):
    in_specs = (
        P("dp", "mp"),
        P("dp", "mp"),
        P(None, "mp"),
        P(None, "mp"),
        P("dp", None),
        P("dp", None),
        P("dp", None),
        P("dp", "mp"),
    )
    out_specs = (P("dp", "mp"), P("dp", "mp"), P("dp", "mp"), P("dp", "mp"), P("dp", "mp"))
    return jax.shard_map(body, mesh=mesh, in_specs=in_specs, out_specs=out_specs, check_vma=False)
```

time: 306 us -> 174 us (0.57)
  the two profiles are of different devices: /device:TPU:0 before, /device:TPU:25 now
where the time goes in v2:
time: 174 us
  starting transfers between devices  63.3 us (36%)
  waiting for transfers between devices  52 us (30%)
  Pallas kernels  33.3 us (19%)
  local copies, waits for them, and re-layouts  23.4 us (13%)
    ppermute x49, starting transfers between devices, flip(): return lax.ppermute(x, 'dp', [(i, i ^ r) for i in range(shards)])  49.9 us
    ppermute x6, waiting for transfers between devices, shift(): return lax.ppermute(x, 'mp', [(i, (i + r) % peers) for i in range(peers)])  27.5 us
    unnamed x48, local copies, waits for them, and re-layouts  22.7 us
    ppermute x49, waiting for transfers between devices, flip(): return lax.ppermute(x, 'dp', [(i, i ^ r) for i in range(shards)])  22.2 us
    ppermute x6, starting transfers between devices, shift(): return lax.ppermute(x, 'mp', [(i, (i + r) % peers) for i in range(peers)])  9.3 us
    pallas_call x2, Pallas kernels, project_back(): pl.pallas_call(functools.partial(back_kernel, chunks, final), grid_spec=p...  9.01 us
    pallas_call x2, Pallas kernels, attend(): pl.pallas_call(functools.partial(attend_kernel, shards, slot), grid_spec=...  8.14 us
    pallas_call x2, Pallas kernels, project(): pl.pallas_call(functools.partial(project_kernel, others, slot), grid_spec...  6.4 us
  transfers between devices with their start and end apart: 56, of which 11 were waited for; matrix products, arithmetic and copies ran while one was open for 1% of the time, Pallas kernels for 16%

profile of v2, /device:TPU:25, one launch (start us, length us, event | category | flops | bytes accessed | tf_op | source)
XLA Modules:
  0.0 173.8 jit_solution(2742225210583234884)
XLA Ops:
  3.0 3.4 %copy-done = bf16[4096,1024]{1,0:T(8,128)(2,1)S(1)} copy-done((bf16[4096,1024]{1,0:T(8,128)(2,1)S(1)}, bf16[4096,1024]{1,0:T(8,128)(2,1)}, u32[]{:S(2)}) %copy-start) | copy-done | bytes 8388632
  6.4 3.4 %copy-done.3 = bf16[4096,1024]{1,0:T(8,128)(2,1)S(1)} copy-done((bf16[4096,1024]{1,0:T(8,128)(2,1)S(1)}, bf16[4096,1024]{1,0:T(8,128)(2,1)}, u32[]{:S(2)}) %copy-start.3) | copy-done | bytes 8388632
  12.6 3.9 %collective-permute-done.1.refs_1_.refs_2_ = bf16[128,1024]{1,0:T(8,128)(2,1)S(1)} collective-permute-done((bf16[128,1024]{1,0:T(8,128)(2,1)}, bf16[128,1024]{1,0:T(8,128)(2,1)S(1)}, u32[]{:S(2)}, u32[]{:S(2)}) %collective-permute-start.1) | collective-permute-done | bytes 262176 | tf_op jit(solution)/shard_map/ppermute | solution.py:341
  16.5 3.6 %collective-permute-done.2.refs_2_.refs_3_ = bf16[128,1024]{1,0:T(8,128)(2,1)S(1)} collective-permute-done((bf16[128,1024]{1,0:T(8,128)(2,1)}, bf16[128,1024]{1,0:T(8,128)(2,1)S(1)}, u32[]{:S(2)}, u32[]{:S(2)}) %collective-permute-start.2) | collective-permute-done | bytes 262176 | tf_op jit(solution)/shard_map/ppermute | solution.py:341
  20.2 2.9 %shard_map.120 = (bf16[64,1024]{1,0:T(8,128)(2,1)S(1)}, bf16[64,1024]{1,0:T(8,128)(2,1)S(1)}, bf16[64,1024]{1,0:T(8,128)(2,1)S(1)}, bf16[64,1024]{1,0:T(8,128)(2...) custom-call(s32[2]{0:T(128)S(1)} %pad_add_fusion.at, ...), custom_call_target="tpu_custom_call" | custom-call | flops 805306368 | bytes 6291456 | tf_op jit(solution)/shard_map/pallas_call | solution.py:112
  30.5 2.7 %collective-permute-start.9 = (bf16[64,1024]{1,0:T(8,128)(2,1)S(1)}, bf16[64,1024]{1,0:T(8,128)(2,1)S(1)}, u32[]{:S(2)}, u32[]{:S(2)}) collective-permute-start(bf16[64,1024]{1,0:T(8,128)(2,1)S(1)} %get-tuple-element.64), channel_id=1, source_target_pairs={{0,28},{4,24},{8,20},{12,16},{16,12},{20,8},{24,4},{28,0},{1,29},{... | collective-permute-start | bytes 393224 | tf_op jit(solution)/shard_map/ppermute | solution.py:338
  33.2 3.5 %shard_map.121 = (bf16[64,1024]{1,0:T(8,128)(2,1)S(1)}, bf16[64,1024]{1,0:T(8,128)(2,1)S(1)}, bf16[64,1024]{1,0:T(8,128)(2,1)S(1)}, bf16[64,1024]{1,0:T(8,128)(2...) custom-call(s32[2]{0:T(128)S(1)} %pad_add_fusion.at, ...), custom_call_target="tpu_custom_call" | custom-call | flops 805306368 | bytes 6291456 | tf_op jit(solution)/shard_map/pallas_call | solution.py:112
  37.0 3.1 %collective-permute-done.7.refs_5_ = bf16[64,1024]{1,0:T(8,128)(2,1)S(1)} collective-permute-done((bf16[64,1024]{1,0:T(8,128)(2,1)S(1)}, bf16[64,1024]{1,0:T(8,128)(2,1)S(1)}, u32[]{:S(2)}, u32[]{:S(2)}) %collective-permute-start.7) | collective-permute-done | bytes 131104 | tf_op jit(solution)/shard_map/ppermute | solution.py:338
  51.8 3.0 %collective-permute-done.14.refs_5_ = bf16[64,1024]{1,0:T(8,128)(2,1)S(1)} collective-permute-done((bf16[64,1024]{1,0:T(8,128)(2,1)S(1)}, bf16[64,1024]{1,0:T(8,128)(2,1)S(1)}, u32[]{:S(2)}, u32[]{:S(2)}) %collective-permute-start.14) | collective-permute-done | bytes 131104 | tf_op jit(solution)/shard_map/ppermute | solution.py:338
  56.6 4.1 %all-to-all-start = ((s32[8,1,1]{2,1,0:T(1,128)}), s32[8,1,1]{2,1,0:T(1,128)S(1)}, u32[]{:S(2)}, u32[]{:S(2)}) async-start(s32[8,1,1]{2,1,0:T(1,128)} %copy.25), calls=%async_computation | async-start | bytes 8192 | tf_op jit(solution)/shard_map/all_to_all | solution.py:347
  68.4 4.6 %shard_map.122 = (bf16[256,1024]{1,0:T(8,128)(2,1)}, bf16[256,1024]{1,0:T(8,128)(2,1)}, bf16[64,1024]{1,0:T(8,128)(2,1)S(1)}, bf16[64,1024]{1,0:T(8,128)(2,1)S(1...) custom-call(s32[2]{0:T(128)S(1)} %pad_add_fusion.at, ...), custom_call_target="tpu_custom_call" | custom-call | flops 805306368 | bytes 3145728 | tf_op jit(solution)/shard_map/pallas_call | solution.py:210
  78.2 2.9 %collective-permute-start.28 = (bf16[64,1024]{1,0:T(8,128)(2,1)S(1)}, bf16[64,1024]{1,0:T(8,128)(2,1)S(1)}, u32[]{:S(2)}, u32[]{:S(2)}) collective-permute-start(bf16[64,1024]{1,0:T(8,128)(2,1)S(1)} %get-tuple-element.90), channel_id=1, source_target_pairs={{0,20},{4,16},{8,28},{12,24},{16,4},{20,0},{24,12},{28,8},{1,21},{... | collective-permute-start | bytes 393224 | tf_op jit(solution)/shard_map/ppermute | solution.py:338
  83.6 3.6 %shard_map.123 = (bf16[256,1024]{1,0:T(8,128)(2,1)}, bf16[256,1024]{1,0:T(8,128)(2,1)}, bf16[64,1024]{1,0:T(8,128)(2,1)S(1)}, bf16[64,1024]{1,0:T(8,128)(2,1)S(1...) custom-call(s32[2]{0:T(128)S(1)} %pad_add_fusion.at, ...), custom_call_target="tpu_custom_call", output_to_operand_aliasing={{0}: (13, {}), {1}: (14, {})} | custom-call | flops 805306368 | bytes 3145728 | tf_op jit(solution)/shard_map/pallas_call | solution.py:210
  94.1 2.4 %collective-permute-start.53 = (bf16[128,1024]{1,0:T(8,128)(2,1)S(1)}, bf16[128,1024]{1,0:T(8,128)(2,1)S(1)}, u32[]{:S(2)}, u32[]{:S(2)}) collective-permute-start(bf16[128,1024]{1,0:T(8,128)(2,1)S(1)} %shard_map.125.grad_ref.refs_8_), channel_id=1, source_target_pairs={{0,24},{4,28},{8,16},{12,20},{16,8},{20,12},{24,0},{28,4},{1,25},{... | collective-permute-start | bytes 786440 | tf_op jit(solution)/shard_map/ppermute | solution.py:338
  100.1 11.1 %collective-permute-done.21.refs_5_ = bf16[64,1024]{1,0:T(8,128)(2,1)S(1)} collective-permute-done((bf16[64,1024]{1,0:T(8,128)(2,1)S(1)}, bf16[64,1024]{1,0:T(8,128)(2,1)S(1)}, u32[]{:S(2)}, u32[]{:S(2)}) %collective-permute-start.21) | collective-permute-done | bytes 131104 | tf_op jit(solution)/shard_map/ppermute | solution.py:338
  115.2 2.7 %collective-permute-done.40.refs_7_ = bf16[128,512]{1,0:T(8,128)(2,1)S(1)} collective-permute-done((bf16[128,512]{1,0:T(8,128)(2,1)S(1)}, bf16[128,512]{1,0:T(8,128)(2,1)S(1)}, u32[]{:S(2)}, u32[]{:S(2)}) %collective-permute-start.40) | collective-permute-done | bytes 131104 | tf_op jit(solution)/shard_map/ppermute | solution.py:338
  117.8 2.4 %collective-permute-start.46 = (bf16[128,1024]{1,0:T(8,128)(2,1)S(1)}, bf16[128,1024]{1,0:T(8,128)(2,1)S(1)}, u32[]{:S(2)}, u32[]{:S(2)}) collective-permute-start(bf16[128,1024]{1,0:T(8,128)(2,1)S(1)} %shard_map.124.grad_ref.refs_8_), channel_id=1, source_target_pairs={{0,24},{4,28},{8,16},{12,20},{16,8},{20,12},{24,0},{28,4},{1,25},{... | collective-permute-start | bytes 786440 | tf_op jit(solution)/shard_map/ppermute | solution.py:338
  120.9 3.4 %copy-done.2 = bf16[4096,1024]{1,0:T(8,128)(2,1)S(1)} copy-done((bf16[4096,1024]{1,0:T(8,128)(2,1)S(1)}, bf16[4096,1024]{1,0:T(8,128)(2,1)}, u32[]{:S(2)}) %copy-start.2) | copy-done | bytes 8388632
  124.2 3.4 %copy-done.5 = bf16[4096,1024]{1,0:T(8,128)(2,1)S(1)} copy-done((bf16[4096,1024]{1,0:T(8,128)(2,1)S(1)}, bf16[4096,1024]{1,0:T(8,128)(2,1)}, u32[]{:S(2)}) %copy-start.5) | copy-done | bytes 8388632
  127.6 4.4 %shard_map.126.refs_0_ = f32[4,128,1024]{2,1,0:T(8,128)S(1)} custom-call(s32[2]{0:T(128)S(1)} %pad_add_fusion.at, bf16[128,1024]{1,0:T(8,128)(2,1)S(1)} %shard_map.125.grad_ref.refs_8_, bf16[4096,1024]{1,0:T(8,128)(2,1)S(1)} %copy-done.2, bf16[4096,1024]{1,0:T(8,128)(2,1)S(1)} %copy-done.5), custom_call_target="tpu_custom_call" | custom-call | flops 1073741824 | bytes 8388608 | tf_op jit(solution)/shard_map/pallas_call | solution.py:281
  132.0 4.6 %shard_map.127 = (bf16[128,1024]{1,0:T(8,128)(2,1)S(1)}, bf16[128,1024]{1,0:T(8,128)(2,1)S(1)}, bf16[128,1024]{1,0:T(8,128)(2,1)S(1)}, bf16[128,1024]{1,0:T(8,128)(2,1)S(1)}) custom-call(s32[2]{0:T(128)S(1)} %pad_add_fusion.at, bf16[128,1024]{1,0:T(8,128)(2,1)S(1)} %shard_map.124.grad_ref.refs_8_, bf16[4096,1024]{1,0:T(8,128)(2,1)S(1)} %copy-done.2, ...), custom_call_target="tpu_custom_call" | custom-call | flops 1073741824 | bytes 8388608 | tf_op jit(solution)/shard_map/pallas_call | solution.py:281
  138.2 5.4 %collective-permute-start.32 = (bf16[128,1024]{1,0:T(8,128)(2,1)S(1)}, bf16[128,1024]{1,0:T(8,128)(2,1)S(1)}, u32[]{:S(2)}, u32[]{:S(2)}) collective-permute-start(bf16[128,1024]{1,0:T(8,128)(2,1)S(1)} %get-tuple-element.95), channel_id=1, source_target_pairs={{0,2},{1,3},{2,0},{3,1},{4,6},{5,7},{6,4},{7,5},{8,10},{9,11},{10,... | collective-permute-start | bytes 786440 | tf_op jit(solution)/shard_map/ppermute | solution.py:341
  145.0 3.4 %collective-permute-done.31 = bf16[128,1024]{1,0:T(8,128)(2,1)S(1)} collective-permute-done((bf16[128,1024]{1,0:T(8,128)(2,1)S(1)}, bf16[128,1024]{1,0:T(8,128)(2,1)S(1)}, u32[]{:S(2)}, u32[]{:S(2)}) %collective-permute-start.31) | collective-permute-done | bytes 262176 | tf_op jit(solution)/shard_map/ppermute | solution.py:341
  149.7 16.5 %collective-permute-done.32 = bf16[128,1024]{1,0:T(8,128)(2,1)S(1)} collective-permute-done((bf16[128,1024]{1,0:T(8,128)(2,1)S(1)}, bf16[128,1024]{1,0:T(8,128)(2,1)S(1)}, u32[]{:S(2)}, u32[]{:S(2)}) %collective-permute-start.32) | collective-permute-done | bytes 262176 | tf_op jit(solution)/shard_map/ppermute | solution.py:341
  (152 shorter events, 68.5 us)
Async XLA Ops:
  0.6 15.9 %collective-permute-start.1 = (bf16[128,1024]{1,0:T(8,128)(2,1)}, bf16[128,1024]{1,0:T(8,128)(2,1)S(1)}, u32[]{:S(2)}, u32[]{:S(2)}) collective-permute-start(bf16[128,1024]{1,0:T(8,128)(2,1)} %refs_0_.1), channel_id=1, source_target_pairs={{0,2},{1,3},{2,0},{3,1},{4,6},{5,7},{6,4},{7,5},{8,10},{9,11},{10,... | collective-permute-start | bytes 786440 | tf_op jit(solution)/shard_map/ppermute | solution.py:341
  0.8 15.8 %collective-permute-start = (bf16[128,1024]{1,0:T(8,128)(2,1)}, bf16[128,1024]{1,0:T(8,128)(2,1)S(1)}, u32[]{:S(2)}, u32[]{:S(2)}) collective-permute-start(bf16[128,1024]{1,0:T(8,128)(2,1)} %refs_0_.1), channel_id=1, source_target_pairs={{0,1},{1,2},{2,3},{3,0},{4,5},{5,6},{6,7},{7,4},{8,9},{9,10},{10,1... | collective-permute-start | bytes 786440 | tf_op jit(solution)/shard_map/ppermute | solution.py:341
  2.9 17.2 %collective-permute-start.2 = (bf16[128,1024]{1,0:T(8,128)(2,1)}, bf16[128,1024]{1,0:T(8,128)(2,1)S(1)}, u32[]{:S(2)}, u32[]{:S(2)}) collective-permute-start(bf16[128,1024]{1,0:T(8,128)(2,1)} %refs_0_.1), channel_id=1, source_target_pairs={{0,3},{1,0},{2,1},{3,2},{4,7},{5,4},{6,5},{7,6},{8,11},{9,8},{10,9... | collective-permute-start | bytes 786440 | tf_op jit(solution)/shard_map/ppermute | solution.py:341
  43.6 17.1 %collective-permute-start.15 = (bf16[64,1024]{1,0:T(8,128)(2,1)}, bf16[64,1024]{1,0:T(8,128)(2,1)}, u32[]{:S(2)}, u32[]{:S(2)}) collective-permute-start(bf16[64,1024]{1,0:T(8,128)(2,1)} %get-tuple-element.71), channel_id=1, source_target_pairs={{0,24},{4,28},{8,16},{12,20},{16,8},{20,12},{24,0},{28,4},{1,25},{... | collective-permute-start | bytes 393224 | tf_op jit(solution)/shard_map/ppermute | solution.py:338
  45.5 17.0 %collective-permute-start.16 = (bf16[64,1024]{1,0:T(8,128)(2,1)}, bf16[64,1024]{1,0:T(8,128)(2,1)}, u32[]{:S(2)}, u32[]{:S(2)}) collective-permute-start(bf16[64,1024]{1,0:T(8,128)(2,1)} %get-tuple-element.72), channel_id=1, source_target_pairs={{0,28},{4,24},{8,20},{12,16},{16,12},{20,8},{24,4},{28,0},{1,29},{... | collective-permute-start | bytes 393224 | tf_op jit(solution)/shard_map/ppermute | solution.py:338
  50.8 22.1 %collective-permute-start.34 = (bf16[128,512]{1,0:T(8,128)(2,1)}, bf16[128,512]{1,0:T(8,128)(2,1)S(1)}, u32[]{:S(2)}, u32[]{:S(2)}) collective-permute-start(bf16[128,512]{1,0:T(8,128)(2,1)} %get-tuple-element.98), channel_id=1, source_target_pairs={{0,4},{4,0},{8,12},{12,8},{16,20},{20,16},{24,28},{28,24},{1,5},{5... | collective-permute-start | bytes 393224 | tf_op jit(solution)/shard_map/ppermute | solution.py:338
  51.7 21.6 %collective-permute-start.35 = (bf16[128,512]{1,0:T(8,128)(2,1)}, bf16[128,512]{1,0:T(8,128)(2,1)S(1)}, u32[]{:S(2)}, u32[]{:S(2)}) collective-permute-start(bf16[128,512]{1,0:T(8,128)(2,1)} %get-tuple-element.99), channel_id=1, source_target_pairs={{0,8},{4,12},{8,0},{12,4},{16,24},{20,28},{24,16},{28,20},{1,9},{5... | collective-permute-start | bytes 393224 | tf_op jit(solution)/shard_map/ppermute | solution.py:338
  55.4 18.8 %collective-permute-start.36 = (bf16[128,512]{1,0:T(8,128)(2,1)}, bf16[128,512]{1,0:T(8,128)(2,1)S(1)}, u32[]{:S(2)}, u32[]{:S(2)}) collective-permute-start(bf16[128,512]{1,0:T(8,128)(2,1)} %get-tuple-element.100), channel_id=1, source_target_pairs={{0,12},{4,8},{8,4},{12,0},{16,28},{20,24},{24,20},{28,16},{1,13},{... | collective-permute-start | bytes 393224 | tf_op jit(solution)/shard_map/ppermute | solution.py:338
  60.8 14.7 %collective-permute-start.37 = (bf16[128,512]{1,0:T(8,128)(2,1)}, bf16[128,512]{1,0:T(8,128)(2,1)S(1)}, u32[]{:S(2)}, u32[]{:S(2)}) collective-permute-start(bf16[128,512]{1,0:T(8,128)(2,1)} %copy-done.21), channel_id=1, source_target_pairs={{0,16},{4,20},{8,24},{12,28},{16,0},{20,4},{24,8},{28,12},{1,17},{... | collective-permute-start | bytes 393224 | tf_op jit(solution)/shard_map/ppermute | solution.py:338
  92.5 18.7 %collective-permute-start.21 = (bf16[64,1024]{1,0:T(8,128)(2,1)S(1)}, bf16[64,1024]{1,0:T(8,128)(2,1)S(1)}, u32[]{:S(2)}, u32[]{:S(2)}) collective-permute-start(bf16[64,1024]{1,0:T(8,128)(2,1)S(1)} %get-tuple-element.82), channel_id=1, source_target_pairs={{0,20},{4,16},{8,28},{12,24},{16,4},{20,0},{24,12},{28,8},{1,21},{... | collective-permute-start | bytes 393224 | tf_op jit(solution)/shard_map/ppermute | solution.py:338
  94.1 26.1 %collective-permute-start.53 = (bf16[128,1024]{1,0:T(8,128)(2,1)S(1)}, bf16[128,1024]{1,0:T(8,128)(2,1)S(1)}, u32[]{:S(2)}, u32[]{:S(2)}) collective-permute-start(bf16[128,1024]{1,0:T(8,128)(2,1)S(1)} %shard_map.125.grad_ref.refs_8_), channel_id=1, source_target_pairs={{0,24},{4,28},{8,16},{12,20},{16,8},{20,12},{24,0},{28,4},{1,25},{... | collective-permute-start | bytes 786440 | tf_op jit(solution)/shard_map/ppermute | solution.py:338
  96.6 23.8 %collective-permute-start.51 = (bf16[128,1024]{1,0:T(8,128)(2,1)S(1)}, bf16[128,1024]{1,0:T(8,128)(2,1)S(1)}, u32[]{:S(2)}, u32[]{:S(2)}) collective-permute-start(bf16[128,1024]{1,0:T(8,128)(2,1)S(1)} %shard_map.125.grad_ref.refs_8_), channel_id=1, source_target_pairs={{0,16},{4,20},{8,24},{12,28},{16,0},{20,4},{24,8},{28,12},{1,17},{... | collective-permute-start | bytes 786440 | tf_op jit(solution)/shard_map/ppermute | solution.py:338
  96.6 16.4 %collective-permute-start.22 = (bf16[64,1024]{1,0:T(8,128)(2,1)S(1)}, bf16[64,1024]{1,0:T(8,128)(2,1)S(1)}, u32[]{:S(2)}, u32[]{:S(2)}) collective-permute-start(bf16[64,1024]{1,0:T(8,128)(2,1)S(1)} %get-tuple-element.83), channel_id=1, source_target_pairs={{0,24},{4,28},{8,16},{12,20},{16,8},{20,12},{24,0},{28,4},{1,25},{... | collective-permute-start | bytes 393224 | tf_op jit(solution)/shard_map/ppermute | solution.py:338
  97.7 15.3 %collective-permute-start.23 = (bf16[64,1024]{1,0:T(8,128)(2,1)S(1)}, bf16[64,1024]{1,0:T(8,128)(2,1)S(1)}, u32[]{:S(2)}, u32[]{:S(2)}) collective-permute-start(bf16[64,1024]{1,0:T(8,128)(2,1)S(1)} %get-tuple-element.84), channel_id=1, source_target_pairs={{0,28},{4,24},{8,20},{12,16},{16,12},{20,8},{24,4},{28,0},{1,29},{... | collective-permute-start | bytes 393224 | tf_op jit(solution)/shard_map/ppermute | solution.py:338
  113.0 23.6 %collective-permute-start.49 = (bf16[128,1024]{1,0:T(8,128)(2,1)S(1)}, bf16[128,1024]{1,0:T(8,128)(2,1)S(1)}, u32[]{:S(2)}, u32[]{:S(2)}) collective-permute-start(bf16[128,1024]{1,0:T(8,128)(2,1)S(1)} %shard_map.125.grad_ref.refs_8_), channel_id=1, source_target_pairs={{0,8},{4,12},{8,0},{12,4},{16,24},{20,28},{24,16},{28,20},{1,9},{5... | collective-permute-start | bytes 786440 | tf_op jit(solution)/shard_map/ppermute | solution.py:338
  113.0 25.2 %collective-permute-start.48 = (bf16[128,1024]{1,0:T(8,128)(2,1)S(1)}, bf16[128,1024]{1,0:T(8,128)(2,1)S(1)}, u32[]{:S(2)}, u32[]{:S(2)}) collective-permute-start(bf16[128,1024]{1,0:T(8,128)(2,1)S(1)} %shard_map.125.grad_ref.refs_8_), channel_id=1, source_target_pairs={{0,4},{4,0},{8,12},{12,8},{16,20},{20,16},{24,28},{28,24},{1,5},{5... | collective-permute-start | bytes 786440 | tf_op jit(solution)/shard_map/ppermute | solution.py:338
  117.8 25.8 %collective-permute-start.46 = (bf16[128,1024]{1,0:T(8,128)(2,1)S(1)}, bf16[128,1024]{1,0:T(8,128)(2,1)S(1)}, u32[]{:S(2)}, u32[]{:S(2)}) collective-permute-start(bf16[128,1024]{1,0:T(8,128)(2,1)S(1)} %shard_map.124.grad_ref.refs_8_), channel_id=1, source_target_pairs={{0,24},{4,28},{8,16},{12,20},{16,8},{20,12},{24,0},{28,4},{1,25},{... | collective-permute-start | bytes 786440 | tf_op jit(solution)/shard_map/ppermute | solution.py:338
  120.3 23.4 %collective-permute-start.44 = (bf16[128,1024]{1,0:T(8,128)(2,1)S(1)}, bf16[128,1024]{1,0:T(8,128)(2,1)S(1)}, u32[]{:S(2)}, u32[]{:S(2)}) collective-permute-start(bf16[128,1024]{1,0:T(8,128)(2,1)S(1)} %shard_map.124.grad_ref.refs_8_), channel_id=1, source_target_pairs={{0,16},{4,20},{8,24},{12,28},{16,0},{20,4},{24,8},{28,12},{1,17},{... | collective-permute-start | bytes 786440 | tf_op jit(solution)/shard_map/ppermute | solution.py:338
  120.3 24.6 %collective-permute-start.42 = (bf16[128,1024]{1,0:T(8,128)(2,1)S(1)}, bf16[128,1024]{1,0:T(8,128)(2,1)S(1)}, u32[]{:S(2)}, u32[]{:S(2)}) collective-permute-start(bf16[128,1024]{1,0:T(8,128)(2,1)S(1)} %shard_map.124.grad_ref.refs_8_), channel_id=1, source_target_pairs={{0,8},{4,12},{8,0},{12,4},{16,24},{20,28},{24,16},{28,20},{1,9},{5... | collective-permute-start | bytes 786440 | tf_op jit(solution)/shard_map/ppermute | solution.py:338
  138.2 28.0 %collective-permute-start.32 = (bf16[128,1024]{1,0:T(8,128)(2,1)S(1)}, bf16[128,1024]{1,0:T(8,128)(2,1)S(1)}, u32[]{:S(2)}, u32[]{:S(2)}) collective-permute-start(bf16[128,1024]{1,0:T(8,128)(2,1)S(1)} %get-tuple-element.95), channel_id=1, source_target_pairs={{0,2},{1,3},{2,0},{3,1},{4,6},{5,7},{6,4},{7,5},{8,10},{9,11},{10,... | collective-permute-start | bytes 786440 | tf_op jit(solution)/shard_map/ppermute | solution.py:341
  143.6 24.1 %collective-permute-start.33 = (bf16[128,1024]{1,0:T(8,128)(2,1)S(1)}, bf16[128,1024]{1,0:T(8,128)(2,1)S(1)}, u32[]{:S(2)}, u32[]{:S(2)}) collective-permute-start(bf16[128,1024]{1,0:T(8,128)(2,1)S(1)} %get-tuple-element.96), channel_id=1, source_target_pairs={{0,3},{1,0},{2,1},{3,2},{4,7},{5,4},{6,5},{7,6},{8,11},{9,8},{10,9... | collective-permute-start | bytes 786440 | tf_op jit(solution)/shard_map/ppermute | solution.py:341
  143.6 24.1 %collective-permute-start.54 = (bf16[128,1024]{1,0:T(8,128)(2,1)S(1)}, bf16[128,1024]{1,0:T(8,128)(2,1)S(1)}, u32[]{:S(2)}, u32[]{:S(2)}) collective-permute-start(bf16[128,1024]{1,0:T(8,128)(2,1)S(1)} %collective-permute-done.53.refs_14_), channel_id=1, source_target_pairs={{0,4},{4,0},{8,12},{12,8},{16,20},{20,16},{24,28},{28,24},{1,5},{5... | collective-permute-start | bytes 786440 | tf_op jit(solution)/shard_map/ppermute | solution.py:338
  144.9 23.3 %collective-permute-start.52 = (bf16[128,1024]{1,0:T(8,128)(2,1)S(1)}, bf16[128,1024]{1,0:T(8,128)(2,1)S(1)}, u32[]{:S(2)}, u32[]{:S(2)}) collective-permute-start(bf16[128,1024]{1,0:T(8,128)(2,1)S(1)} %collective-permute-done.51.refs_12_), channel_id=1, source_target_pairs={{0,4},{4,0},{8,12},{12,8},{16,20},{20,16},{24,28},{28,24},{1,5},{5... | collective-permute-start | bytes 786440 | tf_op jit(solution)/shard_map/ppermute | solution.py:338
  148.5 20.7 %collective-permute-start.50 = (bf16[128,1024]{1,0:T(8,128)(2,1)S(1)}, bf16[128,1024]{1,0:T(8,128)(2,1)S(1)}, u32[]{:S(2)}, u32[]{:S(2)}) collective-permute-start(bf16[128,1024]{1,0:T(8,128)(2,1)S(1)} %collective-permute-done.49.refs_10_), channel_id=1, source_target_pairs={{0,4},{4,0},{8,12},{12,8},{16,20},{20,16},{24,28},{28,24},{1,5},{5... | collective-permute-start | bytes 786440 | tf_op jit(solution)/shard_map/ppermute | solution.py:338
  (56 other events, 446.1 us)

commit v3 on v1

v3 whole, which is shorter than its diff:
```python
import functools

import jax
import jax.numpy as jnp
from jax import lax
from jax.experimental import pallas as pl
from jax.experimental.pallas import tpu as pltpu
from jax.sharding import PartitionSpec as P

HD = 256
TILE = 256
NT = (((1,), (1,)), ((), ()))
NN = (((1,), (0,)), ((), ()))
TN = (((0,), (0,)), ((), ()))
SMEM = pl.BlockSpec(memory_space=pltpu.SMEM)
BF16 = jnp.bfloat16
F32 = jnp.float32


def mm(a, b, dims):
    return lax.dot_general(a, b, dims, preferred_element_type=F32)


def params(mib=60):
    return pltpu.CompilerParams(vmem_limit_bytes=mib * 2**20)


def cost(flops, nbytes, exps=0):
    return pl.CostEstimate(flops=flops, bytes_accessed=nbytes, transcendentals=exps)


def whole(shape):
    return pl.BlockSpec(shape, lambda *_: (0,) * len(shape))


def pair_rows(ref, core, own, partner):
    rows = own.shape[0]
    ref[pl.ds(pl.multiple_of(core * rows, rows), rows), :] = own
    ref[pl.ds(pl.multiple_of((1 - core) * rows, rows), rows), :] = partner


def project_kernel(first, blocks, cuts, final, at, kw_ref, vw_ref, *refs):
    owns, partners = refs[:blocks], refs[blocks : 2 * blocks]
    enc_ref, acc_ref, w_ref, sems = refs[-4:]
    _, steps, tile, gw = w_ref.shape
    peers = kw_ref.shape[0] // (cuts * tile)
    core = at[0] & 1
    copies = []
    for n in range(steps):
        block = lax.rem(at[1] + 2 * peers - first - n // cuts, peers)
        rows = pl.ds(pl.multiple_of((block * cuts + n % cuts) * tile, tile), tile)
        cols = pl.ds(pl.multiple_of(core * gw, gw), gw)
        for m, ref in enumerate((kw_ref, vw_ref)):
            copies.append(pltpu.make_async_copy(ref.at[rows, cols], w_ref.at[m, n], sems.at[m, n]))
            copies[-1].start()
    for n in range(steps):
        place = slice(n % cuts * tile, (n % cuts + 1) * tile)
        pair_rows(enc_ref.at[n], core, owns[n // cuts][:, place], partners[n // cuts][:, place])
    acc_ref[...] = refs[2 * blocks][...] if final else jnp.zeros_like(acc_ref)
    for n in range(steps):
        copies[2 * n].wait()
        copies[2 * n + 1].wait()
        acc_ref[:, :gw] += mm(enc_ref[n], w_ref[0, n], NN)
        acc_ref[:, gw:] += mm(enc_ref[n], w_ref[1, n], NN)
    if final:
        refs[-6][...] = acc_ref[:, :gw].astype(BF16)
        refs[-5][...] = acc_ref[:, gw:].astype(BF16)
    else:
        refs[-5][...] = acc_ref[...]


def project(first, at, key_weight, value_weight, owns, partners, sums=None):
    rows, depth = owns[0].shape
    gw = key_weight.shape[1] // 2
    blocks = len(owns)
    final = sums is not None
    cuts = 2
    tile = depth // cuts
    out_shape = (2 * rows, 2 * gw)
    half = (2 * rows, gw)
    return pl.pallas_call(
        functools.partial(project_kernel, first, blocks, cuts, final),
        grid_spec=pltpu.PrefetchScalarGridSpec(
            num_scalar_prefetch=1,
            grid=(1,),
            in_specs=[pl.BlockSpec(memory_space=pltpu.HBM)] * 2
            + [whole((rows, depth))] * (2 * blocks)
            + [whole(out_shape)] * final,
            out_specs=[whole(half)] * 2 if final else whole(out_shape),
            scratch_shapes=[
                pltpu.VMEM((blocks * cuts, 2 * rows, tile), BF16),
                pltpu.VMEM(out_shape, F32),
                pltpu.VMEM((2, blocks * cuts, tile, gw), BF16),
                pltpu.SemaphoreType.DMA((2, blocks * cuts)),
            ],
        ),
        out_shape=[jax.ShapeDtypeStruct(half, BF16)] * 2 if final else jax.ShapeDtypeStruct(out_shape, F32),
        compiler_params=params(22),
        cost_estimate=cost(8 * blocks * rows * depth * gw, 4 * blocks * depth * gw),
    )(at, key_weight, value_weight, *owns, *partners, *([sums] if final else []))


def split_kernel(peers, at, *refs):
    owns, partners = refs[:peers], refs[peers : 2 * peers]
    outs, all_ref = refs[2 * peers : -1], refs[-1]
    size = outs[0].shape[1]
    per = owns[0].shape[1] // size
    for r in range(peers):
        for c in range(per):
            place = slice(c * size, (c + 1) * size)
            pair_rows(all_ref.at[r * per + c], at[0] & 1, owns[r][:, place], partners[r][:, place])
    for j, out in enumerate(outs):
        target = at[0] ^ (2 * j)
        r = lax.rem(at[1] + peers - lax.div(target, per), peers)
        out[...] = all_ref[r * per + lax.rem(target, per)]


def split_columns(chips, at, owns, partners):
    rows, depth = owns[0].shape
    peers = len(owns)
    size = peers * depth // (2 * chips)
    return pl.pallas_call(
        functools.partial(split_kernel, peers),
        grid_spec=pltpu.PrefetchScalarGridSpec(
            num_scalar_prefetch=1,
            grid=(1,),
            in_specs=[whole((rows, depth))] * (2 * peers),
            out_specs=[whole((2 * rows, size))] * chips,
            scratch_shapes=[pltpu.VMEM((2 * chips, 2 * rows, size), BF16)],
        ),
        out_shape=[jax.ShapeDtypeStruct((2 * rows, size), BF16)] * chips,
        compiler_params=params(16),
        cost_estimate=cost(0, 8 * peers * rows * depth),
    )(at, *owns, *partners)


def attend_kernel(chips, window, at, table, q_ref, g_ref, pair_ref, *refs):
    keys, values = refs[:chips], refs[chips : 2 * chips]
    att_ref, qg_ref, back_ref = refs[2 * chips : 2 * chips + 3]
    outs = refs[2 * chips + 3 : -3]
    outs = (outs[:chips], outs[chips:])
    open_ref, key_ref, grad_ref = refs[-3:]
    rows, gw = q_ref.shape
    shards = 2 * chips
    packed = keys[0].shape[0] // 2
    keys_n = shards * window
    scale = HD ** (-0.5)
    for out in outs[0] + outs[1]:
        out[...] = jnp.zeros_like(out)
    for d in range(2):
        row = lax.broadcasted_iota(jnp.int32, (rows, 128), 0)
        low = jnp.zeros((rows, 128), jnp.int32)
        high = jnp.zeros((rows, 128), jnp.int32)
        for s in range(shards):
            place = (s ^ (at[0] & -2)) * window
            low = jnp.where(row >= table[3, d, s], place + table[1, d, s], low)
            high = jnp.where(row >= table[3, d, s], place + table[2, d, s], high)
        for c in range(0, keys_n, 128):
            col = lax.broadcasted_iota(jnp.int32, (rows, 128), 1) + c
            open_ref[d, :, c : c + 128] = jnp.where((col >= low) & (col < high), 0.0, -jnp.inf)
        bases = []
        for u in range(shards):
            bases.append(pl.multiple_of(u % 2 * packed + table[0, d, u ^ (at[0] & -2)], 16))
            key_ref[d, u * window : (u + 1) * window, :gw] = keys[u // 2][pl.ds(bases[u], window), :]
            key_ref[d, u * window : (u + 1) * window, gw:] = values[u // 2][pl.ds(bases[u], window), :]
        for h in range(gw // HD):
            mine = slice(h * HD, (h + 1) * HD)
            theirs = slice(gw + h * HD, gw + (h + 1) * HD)
            q, g = (pair_ref[:, mine], pair_ref[:, theirs]) if d else (q_ref[:, mine], g_ref[:, mine])
            k, v = key_ref[d, :, mine], key_ref[d, :, theirs]
            scores = mm(q, k, NT) * scale + open_ref[d]
            top = jnp.max(scores, axis=1, keepdims=True)
            expo = jnp.exp(scores - top)
            probs = expo * (1.0 / jnp.sum(expo, axis=1, keepdims=True))
            weights = probs.astype(BF16)
            attended = mm(weights, v, NN).astype(BF16)
            grad_ref[d, :, theirs] = mm(weights, g, TN).astype(BF16)
            dweights = mm(g, v, NT)
            delta = jnp.sum(probs * dweights, axis=1, keepdims=True)
            dscores = (probs * (dweights - delta) * scale).astype(BF16)
            query_grad = mm(dscores, k, NN).astype(BF16)
            grad_ref[d, :, mine] = mm(dscores, q, TN).astype(BF16)
            if d:
                back_ref[:, mine], back_ref[:, theirs] = attended, query_grad
            else:
                att_ref[:, mine], qg_ref[:, mine] = attended, query_grad
        for u in range(shards):
            for m in range(2):
                part = grad_ref[d, u * window : (u + 1) * window, m * gw : (m + 1) * gw]
                outs[m][u // 2][pl.ds(bases[u], window), :] += part


def attend(window, at, table, queries, out_grad, pair, keys, values):
    rows, width = queries.shape
    gw = width // 2
    chips = len(keys)
    keys_n = 2 * chips * window
    row_spec = pl.BlockSpec((rows, gw), lambda n, at, *_: (0, at[0] & 1))
    half = jax.ShapeDtypeStruct((rows, gw), BF16)
    both = jax.ShapeDtypeStruct((rows, width), BF16)
    block = keys[0].shape
    return pl.pallas_call(
        functools.partial(attend_kernel, chips, window),
        grid_spec=pltpu.PrefetchScalarGridSpec(
            num_scalar_prefetch=2,
            grid=(1,),
            in_specs=[row_spec] * 2 + [whole((rows, width))] + [whole(keys[0].shape)] * (2 * chips),
            out_specs=[whole((rows, gw))] * 2 + [whole((rows, width))] + [whole(block)] * (2 * chips),
            scratch_shapes=[
                pltpu.VMEM((2, rows, keys_n), F32),
                pltpu.VMEM((2, keys_n, width), BF16),
                pltpu.VMEM((2, keys_n, width), BF16),
            ],
        ),
        out_shape=[half, half, both] + [jax.ShapeDtypeStruct(block, BF16)] * (2 * chips),
        compiler_params=params(20 if keys_n <= 640 else 28),
        cost_estimate=cost(24 * rows * keys_n * gw, 8 * rows * width + 4 * keys_n * width, 4 * rows * keys_n),
    )(at, table, queries, out_grad, pair, *keys, *values)


def back_kernel(r, chunks, at, ko_ref, vo_ref, kp_ref, vp_ref, kw_ref, vw_ref, out_ref, w_ref, turned_ref, sems):
    depth, rows = out_ref.shape
    gw = ko_ref.shape[1]
    tile = min(TILE, depth)
    steps = depth // tile
    first = lax.rem(at[1] + r, chunks) * depth
    copies = []
    for n in range(steps):
        for m, ref in enumerate((kw_ref, vw_ref)):
            place = pl.ds(pl.multiple_of(first + n * tile, tile), tile)
            copies.append(pltpu.make_async_copy(ref.at[place, :], w_ref.at[m, n], sems.at[m, n]))
            copies[-1].start()
    for n, pair in enumerate(((ko_ref, vo_ref), (kp_ref, vp_ref))):
        start = pl.multiple_of(((at[0] & 1) ^ n) * gw, gw)
        for m, ref in enumerate(pair):
            turned_ref[m, pl.ds(start, gw), :] = ref[...].astype(F32).T.astype(BF16)
    for n in range(steps):
        copies[2 * n].wait()
        copies[2 * n + 1].wait()
        total = mm(w_ref[0, n], turned_ref[0], NN) + mm(w_ref[1, n], turned_ref[1], NN)
        out_ref[n * tile : (n + 1) * tile, :] = total.astype(BF16)


def project_back(r, chunks, at, own, other, key_weight, value_weight):
    rows, gw = own[0].shape
    rows = rows // 2
    depth = key_weight.shape[0] // chunks
    tile = min(TILE, depth)
    steps = depth // tile
    row_spec = pl.BlockSpec((rows, gw), lambda n, at: (at[0] & 1, 0))
    return pl.pallas_call(
        functools.partial(back_kernel, r, chunks),
        grid_spec=pltpu.PrefetchScalarGridSpec(
            num_scalar_prefetch=1,
            grid=(1,),
            in_specs=[row_spec] * 4 + [pl.BlockSpec(memory_space=pltpu.HBM)] * 2,
            out_specs=whole((depth, rows)),
            scratch_shapes=[
                pltpu.VMEM((2, steps, tile, 2 * gw), BF16),
                pltpu.VMEM((2, 2 * gw, rows), BF16),
                pltpu.SemaphoreType.DMA((2, steps)),
            ],
        ),
        out_shape=jax.ShapeDtypeStruct((depth, rows), BF16),
        compiler_params=params(16),
        cost_estimate=cost(8 * rows * gw * depth, 8 * gw * depth),
    )(at, *own, *other, key_weight, value_weight)


def weight_grad_kernel(chips, at, col_ref, *refs):
    grads = refs[: 4 * chips]
    outs = refs[4 * chips : -1]
    grad_ref = refs[-1]
    rows = grads[0].shape[0]
    half = pl.program_id(0) // (pl.num_programs(0) // 2)
    for m in range(2):

        @pl.when(half == m)
        def _():
            for n, out in enumerate(outs):
                for j in range(chips):
                    grad_ref[n, j * rows : (j + 1) * rows, :] = grads[(2 * m + n) * chips + j][...]
                out[...] = mm(col_ref[...], grad_ref[n], NN)


def weight_grads(at, cols, owns, others):
    chips = len(owns[0])
    rows, gw = owns[0][0].shape
    width = 2 * gw
    size = cols.shape[0]
    steps = gw // TILE
    own_spec = pl.BlockSpec((rows, TILE), lambda n, at: (0, jnp.minimum(n, steps - 1)))
    other_spec = pl.BlockSpec((rows, TILE), lambda n, at: (0, jnp.maximum(n - steps, 0)))
    out_spec = pl.BlockSpec((size, TILE), lambda n, at: (0, (n // steps ^ (at[0] & 1)) * steps + n % steps))
    return pl.pallas_call(
        functools.partial(weight_grad_kernel, chips),
        grid_spec=pltpu.PrefetchScalarGridSpec(
            num_scalar_prefetch=1,
            grid=(2 * steps,),
            in_specs=[whole(cols.shape)] + [own_spec] * (2 * chips) + [other_spec] * (2 * chips),
            out_specs=[out_spec] * 2,
            scratch_shapes=[pltpu.VMEM((2, chips * rows, TILE), BF16)],
        ),
        out_shape=[jax.ShapeDtypeStruct((size, width), F32)] * 2,
        compiler_params=params(16 if chips <= 4 else 28),
        cost_estimate=cost(4 * chips * rows * size * width, 2 * chips * rows * (size + 2 * width) + 8 * size * width),
    )(at, cols, *owns[0], *owns[1], *others[0], *others[1])


def window_table(dp, enc_len, route, dec_len, window):
    shards = enc_len.shape[1]
    packed_rows = jnp.concatenate([enc_len, route, dec_len], axis=1)
    everyone = lax.all_to_all(
        jnp.broadcast_to(packed_rows, (shards, 3 * shards)), "dp", split_axis=0, concat_axis=0, tiled=True
    )
    lens, targets, decs = everyone[:, :shards], everyone[:, shards : 2 * shards], everyone[:, 2 * shards :]
    order = jnp.arange(shards, dtype=jnp.int32)
    before = (order[None, :] < order[:, None])[None]
    starts = jnp.sum(jnp.where(before, lens[:, None, :], 0), axis=2, dtype=jnp.int32)
    here = dp ^ jnp.arange(2, dtype=jnp.int32)
    hit = targets[None] == here[:, None, None]
    start = jnp.sum(jnp.where(hit, starts[None], 0), axis=2, dtype=jnp.int32)
    length = jnp.sum(jnp.where(hit, lens[None], 0), axis=2, dtype=jnp.int32)
    mine = jnp.sum(jnp.where((order[None] == here[:, None])[:, :, None], decs[None], 0), axis=1, dtype=jnp.int32)
    begin = jnp.sum(jnp.where(before, mine[:, None, :], 0), axis=2, dtype=jnp.int32)
    return start, length, begin


def body(queries, enc_rows, key_weight, value_weight, enc_len, dec_len, route, out_grad):
    shards = lax.axis_size("dp")
    peers = lax.axis_size("mp")
    chips = shards // 2
    packed = enc_rows.shape[0]
    window = 4 * packed // shards + 16
    gw = key_weight.shape[1] // 2
    dp, mp = lax.axis_index("dp"), lax.axis_index("mp")
    core = dp & 1
    at = jnp.stack([dp, mp]).astype(jnp.int32)

    def flip(x, r):
        return lax.ppermute(x, "dp", [(i, i ^ r) for i in range(shards)])

    def shift(x, r):
        return lax.ppermute(x, "mp", [(i, (i + r) % peers) for i in range(peers)])

    low = 1 << ((chips.bit_length() - 1) // 2)
    lows, highs = range(1, low), range(low, chips, low)

    def spread(x, low_first):
        got = {0: x}
        first, second = (lows, highs) if low_first else (highs, lows)
        for a in first:
            got[a] = flip(x, 2 * a)
        for b in second:
            got[b] = flip(x, 2 * b)
        for a in first:
            for b in second:
                got[a + b] = flip(got[a], 2 * b)
        return [got[j] for j in range(chips)]

    def collect(parts, low_first):
        first, second = (lows, highs) if low_first else (highs, lows)
        sums = {}
        for b in [*second, 0]:
            sums[b] = functools.reduce(jnp.add, [parts[b]] + [flip(parts[a + b], 2 * a) for a in first])
        return functools.reduce(jnp.add, [flip(sums[b], 2 * b) for b in second] + [sums[0]])

    partner = flip(enc_rows, 1)
    owns = [enc_rows] + [shift(enc_rows, r) for r in range(1, peers)]
    sums = project(0, at, key_weight, value_weight, [enc_rows], [partner])
    sums, owns = lax.optimization_barrier((sums, owns))
    partners = [partner] + [flip(x, 1) for x in owns[1:]]
    keys, values = project(1, at, key_weight, value_weight, owns[1:], partners[1:], sums)
    keys, values, lens, targets, decs, *theirs = lax.optimization_barrier(
        (keys, values, enc_len, route, dec_len, queries, out_grad)
    )
    keys, values = spread(keys, True), spread(values, False)
    theirs = [lax.dynamic_slice_in_dim(x, (1 - core) * gw, gw, axis=1) for x in theirs]
    pair = flip(jnp.concatenate(theirs, axis=1), 1)
    start, length, begin = window_table(dp, lens, targets, decs, window)
    base = jnp.minimum(start // 16 * 16, packed - window)
    table = jnp.stack([base, start - base, start - base + length, begin])
    cols = split_columns(chips, at, owns, partners)
    keys, values, table, pair, cols = lax.optimization_barrier((keys, values, table, pair, list(cols)))
    cols = [cols[0]] + [flip(cols[j], 2 * j) for j in range(1, chips)]
    attended, query_grad, back, *parts = attend(window, at, table, queries, out_grad, pair, keys, values)
    parts, back, cols = lax.optimization_barrier((parts, back, cols))
    own = [collect(parts[:chips], False), collect(parts[chips:], True)]
    back = flip(back, 1)
    outs = []
    for mine, rest in ((attended, back[:, :gw]), (query_grad, back[:, gw:])):
        outs.append(jnp.where(core == 0, jnp.concatenate([mine, rest], 1), jnp.concatenate([rest, mine], 1)))
    cols = jnp.concatenate([x.T for x in cols], axis=1)
    own, cols, outs = lax.optimization_barrier((own, cols, outs))
    other = [flip(x, 1) for x in own]
    owns = [spread(own[0], True), spread(own[1], False)]
    middle = peers // 2
    order = [middle] + [r for r in range(1, peers) if r != middle] + [0]
    chunks = [project_back(r, peers, at, own, other, key_weight, value_weight) for r in order]
    arrived = [shift(x, r) for x, r in zip(chunks[:-1], order)]
    owns, arrived[0], _, chunk = lax.optimization_barrier((owns, arrived[0], chunks[:-1], chunks[-1]))
    others = [[other[n]] + [flip(x, 1) for x in owns[n][1:]] for n in range(2)]
    weight_out = weight_grads(at, cols, owns, others)
    arrived, weight_out = lax.optimization_barrier((arrived, weight_out))
    total = functools.reduce(jnp.add, [x.astype(F32) for x in [chunk, *arrived]])
    return (*outs, total.T.astype(BF16), *weight_out)


def solution(mesh):
    in_specs = (
        P("dp", "mp"),
        P("dp", "mp"),
        P(None, "mp"),
        P(None, "mp"),
        P("dp", None),
        P("dp", None),
        P("dp", None),
        P("dp", "mp"),
    )
    out_specs = (P("dp", "mp"), P("dp", "mp"), P("dp", "mp"), P("dp", "mp"), P("dp", "mp"))
    return jax.shard_map(body, mesh=mesh, in_specs=in_specs, out_specs=out_specs, check_vma=False)
```

time: 306 us -> 153 us (0.50)
  waiting for transfers between devices: 212 us -> 32.3 us
  starting transfers between devices: 0.32 us -> 48.8 us
  blocking collectives: 31.5 us -> 0 us
  matrix products: 30.7 us -> 0 us
  local copies, waits for them, and re-layouts: 6.69 us -> 31.5 us
  Pallas kernels: 9.99 us -> 31.6 us
  between operations: 14.2 us -> 0.94 us
  other arithmetic: 0.3 us -> 7.07 us
    reduce_scatter x3 -> x0, waiting for transfers between devices: 111 us -> none  [the longest x1 45.2 us: body(): own_vg = lax.psum_scatter(value_part, 'dp', scatter_dimension=0, tiled=True)]
    all_gather x5 -> x0, waiting for transfers between devices: 100 us -> none  [the longest x1 31.7 us: body(): full = lax.all_gather(enc_rows, 'mp', axis=1, tiled=True)]
    ppermute x0 -> x41, starting transfers between devices: none -> 45 us  [the longest x35 27.3 us: flip(): return lax.ppermute(x, 'dp', [(i, i ^ r) for i in range(shards)])]
    all_to_all x2 -> x0, blocking collectives: 31.5 us -> none  [the longest x1 23.4 us: body(): lax.all_to_all(full, 'dp', split_axis=1, concat_axis=0, tiled=True)]
    dot_general x6 -> x0, matrix products: 30.7 us -> none  [mm(): return lax.dot_general(a, b, dims, preferred_element_type=jnp.float32)]
    ppermute x0 -> x41, waiting for transfers between devices: none -> 28.4 us  [the longest x35 16.5 us: flip(): return lax.ppermute(x, 'dp', [(i, i ^ r) for i in range(shards)])]
    pallas_call x1 -> x9, Pallas kernels: 9.99 us -> 31.6 us  [the longest x4 11.5 us: project_back(): pl.pallas_call(functools.partial(back_kernel, r, chunks), grid_spec=pltpu...]
    unnamed x11 -> x37, local copies, waits for them, and re-layouts: 5.44 us -> 26.1 us
  transfers between devices with their start and end apart: 8 -> 42, of which waited for: 7 -> 15; matrix products, arithmetic and copies ran while one was open for 10% -> 6% of each run, Pallas kernels for 0% -> 18%
where the time goes in v3:
time: 153 us; the launch traced here: 152 us
  starting transfers between devices  48.8 us (32%)
  waiting for transfers between devices  32.3 us (21%)
  Pallas kernels  31.6 us (21%)
  local copies, waits for them, and re-layouts  31.5 us (21%)
  other arithmetic  7.07 us (5%)
    ppermute x35, starting transfers between devices, flip(): return lax.ppermute(x, 'dp', [(i, i ^ r) for i in range(shards)])  27.3 us
    unnamed x37, local copies, waits for them, and re-layouts  26.1 us
    ppermute x6, starting transfers between devices, shift(): return lax.ppermute(x, 'mp', [(i, (i + r) % peers) for i in range(peers)])  17.6 us
    ppermute x35, waiting for transfers between devices, flip(): return lax.ppermute(x, 'dp', [(i, i ^ r) for i in range(shards)])  16.5 us
    ppermute x6, waiting for transfers between devices, shift(): return lax.ppermute(x, 'mp', [(i, (i + r) % peers) for i in range(peers)])  11.8 us
    pallas_call x4, Pallas kernels, project_back(): pl.pallas_call(functools.partial(back_kernel, r, chunks), grid_spec=pltpu...  11.5 us
    pallas_call x1, Pallas kernels, attend(): pl.pallas_call(functools.partial(attend_kernel, chips, window), grid_spec...  7.85 us
    pallas_call x2, Pallas kernels, project(): pl.pallas_call(functools.partial(project_kernel, first, blocks, cuts, fin...  6.13 us
  transfers between devices with their start and end apart: 42, of which 15 were waited for; matrix products, arithmetic and copies ran while one was open for 6% of the time, Pallas kernels for 18%

profile of v3, /device:TPU:0, one launch (start us, length us, event | category | flops | bytes accessed | tf_op | source)
XLA Modules:
  0.0 152.1 jit_solution(5612868965736425821)
XLA Ops:
  1.1 3.7 %collective-permute-start.2 = (bf16[128,1024]{1,0:T(8,128)(2,1)}, bf16[128,1024]{1,0:T(8,128)(2,1)S(1)}, u32[]{:S(2)}, u32[]{:S(2)}) collective-permute-start(bf16[128,1024]{1,0:T(8,128)(2,1)} %refs_0_.2), channel_id=1, source_target_pairs={{0,2},{1,3},{2,0},{3,1},{4,6},{5,7},{6,4},{7,5},{8,10},{9,11},{10,... | collective-permute-start | bytes 786440 | tf_op jit(solution)/shard_map/ppermute | solution.py:344
  6.4 2.2 %collective-permute-start.3 = (bf16[128,1024]{1,0:T(8,128)(2,1)}, bf16[128,1024]{1,0:T(8,128)(2,1)S(1)}, u32[]{:S(2)}, u32[]{:S(2)}) collective-permute-start(bf16[128,1024]{1,0:T(8,128)(2,1)} %refs_0_.2), channel_id=1, source_target_pairs={{0,3},{1,0},{2,1},{3,2},{4,7},{5,4},{6,5},{7,6},{8,11},{9,8},{10,9... | collective-permute-start | bytes 786440 | tf_op jit(solution)/shard_map/ppermute | solution.py:344
  8.7 3.4 %copy-done = bf16[4096,1024]{1,0:T(8,128)(2,1)S(1)} copy-done((bf16[4096,1024]{1,0:T(8,128)(2,1)S(1)}, bf16[4096,1024]{1,0:T(8,128)(2,1)}, u32[]{:S(2)}) %copy-start) | copy-done | bytes 8388632
  12.1 3.4 %copy-done.3 = bf16[4096,1024]{1,0:T(8,128)(2,1)S(1)} copy-done((bf16[4096,1024]{1,0:T(8,128)(2,1)S(1)}, bf16[4096,1024]{1,0:T(8,128)(2,1)}, u32[]{:S(2)}) %copy-start.3) | copy-done | bytes 8388632
  18.1 5.3 %collective-permute-done.2.refs_1_.refs_2_ = bf16[128,1024]{1,0:T(8,128)(2,1)S(1)} collective-permute-done((bf16[128,1024]{1,0:T(8,128)(2,1)}, bf16[128,1024]{1,0:T(8,128)(2,1)S(1)}, u32[]{:S(2)}, u32[]{:S(2)}) %collective-permute-start.2) | collective-permute-done | bytes 262176 | tf_op jit(solution)/shard_map/ppermute | solution.py:344
  27.0 3.4 %copy-done.1 = bf16[4096,1024]{1,0:T(8,128)(2,1)S(1)} copy-done((bf16[4096,1024]{1,0:T(8,128)(2,1)S(1)}, bf16[4096,1024]{1,0:T(8,128)(2,1)}, u32[]{:S(2)}) %copy-start.1) | copy-done | bytes 8388632
  30.4 3.4 %copy-done.4 = bf16[4096,1024]{1,0:T(8,128)(2,1)S(1)} copy-done((bf16[4096,1024]{1,0:T(8,128)(2,1)S(1)}, bf16[4096,1024]{1,0:T(8,128)(2,1)}, u32[]{:S(2)}) %copy-start.4) | copy-done | bytes 8388632
  33.8 4.5 %shard_map.120 = (bf16[256,512]{1,0:T(8,128)(2,1)}, bf16[256,512]{1,0:T(8,128)(2,1)}) custom-call(s32[2]{0:T(128)S(1)} %pad_add_fusion.1.at, bf16[4096,1024]{1,0:T(8,128)(2,1)S(1)} %copy-done.1, bf16[4096,1024]{1,0:T(8,128)(2,1)S(1)} %copy-done.4, bf16[128,1024]{1,0:T(8,128)(2,1)S(1)} %collective-permute-done.1.refs_0_.refs_1_, ...), custom_call_target="tpu_custom_call" | custom-call | flops 1610612736 | bytes 6291456 | tf_op jit(solution)/shard_map/pallas_call | solution.py:81
  43.1 3.8 %all-to-all-start = ((s32[8,1,24]{2,1,0:T(1,128)}), s32[8,1,24]{2,1,0:T(1,128)S(1)}, u32[]{:S(2)}, u32[]{:S(2)}) async-start(s32[8,1,24]{2,1,0:T(1,128)} %broadcast_in_dim.92), calls=%async_computation | async-start | bytes 8192 | tf_op jit(solution)/shard_map/all_to_all | solution.py:313
  50.0 3.9 %all-to-all-done = s32[8,1,24]{2,1,0:T(1,128)S(1)} async-done(((s32[8,1,24]{2,1,0:T(1,128)}), s32[8,1,24]{2,1,0:T(1,128)S(1)}, u32[]{:S(2)}, u32[]{:S(2)}) %all-to-all-start) | async-done | bytes 800 | tf_op jit(solution)/shard_map/all_to_all | solution.py:313
  57.6 5.5 %collective-permute-done.9.refs_3_ = bf16[256,512]{1,0:T(8,128)(2,1)S(1)} collective-permute-done((bf16[256,512]{1,0:T(8,128)(2,1)}, bf16[256,512]{1,0:T(8,128)(2,1)S(1)}, u32[]{:S(2)}, u32[]{:S(2)}) %collective-permute-start.9) | collective-permute-done | bytes 262176 | tf_op jit(solution)/shard_map/ppermute | solution.py:341
  73.8 7.9 %shard_map.122 = (bf16[256,512]{1,0:T(8,128)(2,1)S(1)}, bf16[256,512]{1,0:T(8,128)(2,1)S(1)}, bf16[256,1024]{1,0:T(8,128)(2,1)S(1)}, bf16[256,512]{1,0:T(8,128)(...) custom-call(s32[2]{0:T(128)S(1)} %pad_add_fusion.1.at, ...), custom_call_target="tpu_custom_call" | custom-call | flops 2013265920 | bytes 4718592 | tf_op jit(solution)/shard_map/pallas_call | solution.py:202
  87.3 3.9 %collective-permute-done.17 = bf16[256,512]{1,0:T(8,128)(2,1)} collective-permute-done((bf16[256,512]{1,0:T(8,128)(2,1)}, bf16[256,512]{1,0:T(8,128)(2,1)}, u32[]{:S(2)}, u32[]{:S(2)}) %collective-permute-start.17) | collective-permute-done | bytes 262176 | tf_op jit(solution)/shard_map/ppermute | solution.py:341
  98.8 3.6 %collective-permute-done.18 = bf16[256,512]{1,0:T(8,128)(2,1)S(1)} collective-permute-done((bf16[256,512]{1,0:T(8,128)(2,1)S(1)}, bf16[256,512]{1,0:T(8,128)(2,1)S(1)}, u32[]{:S(2)}, u32[]{:S(2)}) %collective-permute-start.18) | collective-permute-done | bytes 262176 | tf_op jit(solution)/shard_map/ppermute | solution.py:341
  107.2 3.4 %copy-done.2 = bf16[4096,1024]{1,0:T(8,128)(2,1)S(1)} copy-done((bf16[4096,1024]{1,0:T(8,128)(2,1)S(1)}, bf16[4096,1024]{1,0:T(8,128)(2,1)}, u32[]{:S(2)}) %copy-start.2) | copy-done | bytes 8388632
  110.6 3.4 %copy-done.5 = bf16[4096,1024]{1,0:T(8,128)(2,1)S(1)} copy-done((bf16[4096,1024]{1,0:T(8,128)(2,1)S(1)}, bf16[4096,1024]{1,0:T(8,128)(2,1)}, u32[]{:S(2)}) %copy-start.5) | copy-done | bytes 8388632
  113.9 2.8 %shard_map.123 = bf16[1024,128]{1,0:T(8,128)(2,1)S(1)} custom-call(s32[2]{0:T(128)S(1)} %pad_add_fusion.1.at, bf16[256,512]{1,0:T(8,128)(2,1)S(1)} %add_add_fusion.1.ko_ref.refs_0_, bf16[256,512]{1,0:T(8,128)(2,1)S(1)} %add_add_fusion.vo_ref.refs_4_, bf16[256,512]{1,0:T(8,128)(2,1)S(1)} %collective-permute-done.30.kp_ref.refs_8_, ...), custom_call_target="tpu_custom_call" | custom-call | flops 536870912 | bytes 4194304 | tf_op jit(solution)/shard_map/pallas_call | solution.py:251
  116.8 6.7 %collective-permute-start.32 = (bf16[1024,128]{1,0:T(8,128)(2,1)S(1)}, bf16[1024,128]{1,0:T(8,128)(2,1)S(1)}, u32[]{:S(2)}, u32[]{:S(2)}) collective-permute-start(bf16[1024,128]{1,0:T(8,128)(2,1)S(1)} %shard_map.123), channel_id=1, source_target_pairs={{0,2},{1,3},{2,0},{3,1},{4,6},{5,7},{6,4},{7,5},{8,10},{9,11},{10,... | collective-permute-start | bytes 786440 | tf_op jit(solution)/shard_map/ppermute | solution.py:344
  126.0 2.8 %shard_map.125 = bf16[1024,128]{1,0:T(8,128)(2,1)S(1)} custom-call(s32[2]{0:T(128)S(1)} %pad_add_fusion.1.at, bf16[256,512]{1,0:T(8,128)(2,1)S(1)} %add_add_fusion.1.ko_ref.refs_0_, bf16[256,512]{1,0:T(8,128)(2,1)S(1)} %add_add_fusion.vo_ref.refs_4_, bf16[256,512]{1,0:T(8,128)(2,1)S(1)} %collective-permute-done.30.kp_ref.refs_8_, ...), custom_call_target="tpu_custom_call" | custom-call | flops 536870912 | bytes 4194304 | tf_op jit(solution)/shard_map/pallas_call | solution.py:251
  128.9 3.1 %shard_map.124 = bf16[1024,128]{1,0:T(8,128)(2,1)S(1)} custom-call(s32[2]{0:T(128)S(1)} %pad_add_fusion.1.at, bf16[256,512]{1,0:T(8,128)(2,1)S(1)} %add_add_fusion.1.ko_ref.refs_0_, bf16[256,512]{1,0:T(8,128)(2,1)S(1)} %add_add_fusion.vo_ref.refs_4_, bf16[256,512]{1,0:T(8,128)(2,1)S(1)} %collective-permute-done.30.kp_ref.refs_8_, ...), custom_call_target="tpu_custom_call" | custom-call | flops 536870912 | bytes 4194304 | tf_op jit(solution)/shard_map/pallas_call | solution.py:251
  131.9 2.8 %shard_map.126 = bf16[1024,128]{1,0:T(8,128)(2,1)S(1)} custom-call(s32[2]{0:T(128)S(1)} %pad_add_fusion.1.at, bf16[256,512]{1,0:T(8,128)(2,1)S(1)} %add_add_fusion.1.ko_ref.refs_0_, bf16[256,512]{1,0:T(8,128)(2,1)S(1)} %add_add_fusion.vo_ref.refs_4_, bf16[256,512]{1,0:T(8,128)(2,1)S(1)} %collective-permute-done.30.kp_ref.refs_8_, ...), custom_call_target="tpu_custom_call" | custom-call | flops 536870912 | bytes 4194304 | tf_op jit(solution)/shard_map/pallas_call | solution.py:251
  137.2 3.5 %collective-permute-start.34 = (bf16[1024,128]{1,0:T(8,128)(2,1)S(1)}, bf16[1024,128]{1,0:T(8,128)(2,1)S(1)}, u32[]{:S(2)}, u32[]{:S(2)}) collective-permute-start(bf16[1024,128]{1,0:T(8,128)(2,1)S(1)} %shard_map.125), channel_id=1, source_target_pairs={{0,3},{1,0},{2,1},{3,2},{4,7},{5,4},{6,5},{7,6},{8,11},{9,8},{10,9... | collective-permute-start | bytes 786440 | tf_op jit(solution)/shard_map/ppermute | solution.py:344
  140.6 5.3 %shard_map.127 = (f32[512,1024]{1,0:T(8,128)}, f32[512,1024]{1,0:T(8,128)}) custom-call(s32[2]{0:T(128)S(1)} %pad_add_fusion.1.at, bf16[512,1024]{1,0:T(8,128)(2,1)S(1)} %pad_maximum_fusion.col_ref, bf16[256,512]{1,0:T(8,128)(2,1)S(1)} %add_add_fusion.1.ko_ref.refs_0_, bf16[256,512]{1,0:T(8,128)(2,1)S(1)} %collective-permute-done.24.refs_1_, ...), custom_call_target="tpu_custom_call" | custom-call | flops 2147483648 | bytes 9437184 | tf_op jit(solution)/shard_map/pallas_call | solution.py:295
  147.8 3.3 %collective-permute-done.34 = bf16[1024,128]{1,0:T(8,128)(2,1)S(1)} collective-permute-done((bf16[1024,128]{1,0:T(8,128)(2,1)S(1)}, bf16[1024,128]{1,0:T(8,128)(2,1)S(1)}, u32[]{:S(2)}, u32[]{:S(2)}) %collective-permute-start.34) | collective-permute-done | bytes 262176 | tf_op jit(solution)/shard_map/ppermute | solution.py:344
  (133 shorter events, 56.3 us)
Async XLA Ops:
  1.1 22.3 %collective-permute-start.2 = (bf16[128,1024]{1,0:T(8,128)(2,1)}, bf16[128,1024]{1,0:T(8,128)(2,1)S(1)}, u32[]{:S(2)}, u32[]{:S(2)}) collective-permute-start(bf16[128,1024]{1,0:T(8,128)(2,1)} %refs_0_.2), channel_id=1, source_target_pairs={{0,2},{1,3},{2,0},{3,1},{4,6},{5,7},{6,4},{7,5},{8,10},{9,11},{10,... | collective-permute-start | bytes 786440 | tf_op jit(solution)/shard_map/ppermute | solution.py:344
  4.8 18.7 %collective-permute-start.1 = (bf16[128,1024]{1,0:T(8,128)(2,1)}, bf16[128,1024]{1,0:T(8,128)(2,1)S(1)}, u32[]{:S(2)}, u32[]{:S(2)}) collective-permute-start(bf16[128,1024]{1,0:T(8,128)(2,1)} %refs_0_.2), channel_id=1, source_target_pairs={{0,1},{1,2},{2,3},{3,0},{4,5},{5,6},{6,7},{7,4},{8,9},{9,10},{10,1... | collective-permute-start | bytes 786440 | tf_op jit(solution)/shard_map/ppermute | solution.py:344
  6.4 18.4 %collective-permute-start.3 = (bf16[128,1024]{1,0:T(8,128)(2,1)}, bf16[128,1024]{1,0:T(8,128)(2,1)S(1)}, u32[]{:S(2)}, u32[]{:S(2)}) collective-permute-start(bf16[128,1024]{1,0:T(8,128)(2,1)} %refs_0_.2), channel_id=1, source_target_pairs={{0,3},{1,0},{2,1},{3,2},{4,7},{5,4},{6,5},{7,6},{8,11},{9,8},{10,9... | collective-permute-start | bytes 786440 | tf_op jit(solution)/shard_map/ppermute | solution.py:344
  38.3 19.3 %collective-permute-start.8 = (bf16[256,512]{1,0:T(8,128)(2,1)}, bf16[256,512]{1,0:T(8,128)(2,1)}, u32[]{:S(2)}, u32[]{:S(2)}) collective-permute-start(bf16[256,512]{1,0:T(8,128)(2,1)} %get-tuple-element.103.refs_0_), channel_id=1, source_target_pairs={{0,16},{4,20},{8,24},{12,28},{16,0},{20,4},{24,8},{28,12},{1,17},{... | collective-permute-start | bytes 786440 | tf_op jit(solution)/shard_map/ppermute | solution.py:341
  39.9 14.5 %collective-permute-start.7 = (bf16[256,512]{1,0:T(8,128)(2,1)}, bf16[256,512]{1,0:T(8,128)(2,1)}, u32[]{:S(2)}, u32[]{:S(2)}) collective-permute-start(bf16[256,512]{1,0:T(8,128)(2,1)} %get-tuple-element.103.refs_0_), channel_id=1, source_target_pairs={{0,8},{4,12},{8,0},{12,4},{16,24},{20,28},{24,16},{28,20},{1,9},{5... | collective-permute-start | bytes 786440 | tf_op jit(solution)/shard_map/ppermute | solution.py:341
  41.4 14.5 %collective-permute-start.11 = (bf16[256,512]{1,0:T(8,128)(2,1)}, bf16[256,512]{1,0:T(8,128)(2,1)}, u32[]{:S(2)}, u32[]{:S(2)}) collective-permute-start(bf16[256,512]{1,0:T(8,128)(2,1)} %get-tuple-element.107.refs_4_), channel_id=1, source_target_pairs={{0,16},{4,20},{8,24},{12,28},{16,0},{20,4},{24,8},{28,12},{1,17},{... | collective-permute-start | bytes 786440 | tf_op jit(solution)/shard_map/ppermute | solution.py:341
  41.9 15.6 %collective-permute-start.10 = (bf16[256,512]{1,0:T(8,128)(2,1)}, bf16[256,512]{1,0:T(8,128)(2,1)}, u32[]{:S(2)}, u32[]{:S(2)}) collective-permute-start(bf16[256,512]{1,0:T(8,128)(2,1)} %get-tuple-element.107.refs_4_), channel_id=1, source_target_pairs={{0,8},{4,12},{8,0},{12,4},{16,24},{20,28},{24,16},{28,20},{1,9},{5... | collective-permute-start | bytes 786440 | tf_op jit(solution)/shard_map/ppermute | solution.py:341
  43.1 10.9 %all-to-all-start = ((s32[8,1,24]{2,1,0:T(1,128)}), s32[8,1,24]{2,1,0:T(1,128)S(1)}, u32[]{:S(2)}, u32[]{:S(2)}) async-start(s32[8,1,24]{2,1,0:T(1,128)} %broadcast_in_dim.92), calls=%async_computation | async-start | bytes 8192 | tf_op jit(solution)/shard_map/all_to_all | solution.py:313
  48.8 15.1 %collective-permute-start.13 = (bf16[256,1024]{1,0:T(8,128)(2,1)}, bf16[256,1024]{1,0:T(8,128)(2,1)}, u32[]{:S(2)}, u32[]{:S(2)}) collective-permute-start(bf16[256,1024]{1,0:T(8,128)(2,1)} %pad_maximum_fusion.1), channel_id=1, source_target_pairs={{0,4},{4,0},{8,12},{12,8},{16,20},{20,16},{24,28},{28,24},{1,5},{5... | collective-permute-start | bytes 1572872 | tf_op jit(solution)/shard_map/ppermute | solution.py:341
  66.3 15.3 %collective-permute-start.16 = (bf16[256,512]{0,1:T(8,128)(2,1)}, bf16[256,512]{0,1:T(8,128)(2,1)}, u32[]{:S(2)}, u32[]{:S(2)}) collective-permute-start(bf16[256,512]{0,1:T(8,128)(2,1)} %copy.25), channel_id=1, source_target_pairs={{0,24},{4,28},{8,16},{12,20},{16,8},{20,12},{24,0},{28,4},{1,25},{... | collective-permute-start | bytes 786440 | tf_op jit(solution)/shard_map/ppermute | solution.py:341
  68.2 13.5 %collective-permute-start.15 = (bf16[256,512]{0,1:T(8,128)(2,1)}, bf16[256,512]{0,1:T(8,128)(2,1)}, u32[]{:S(2)}, u32[]{:S(2)}) collective-permute-start(bf16[256,512]{0,1:T(8,128)(2,1)} %copy.24), channel_id=1, source_target_pairs={{0,16},{4,20},{8,24},{12,28},{16,0},{20,4},{24,8},{28,12},{1,17},{... | collective-permute-start | bytes 786440 | tf_op jit(solution)/shard_map/ppermute | solution.py:341
  69.3 12.4 %collective-permute-start.14 = (bf16[256,512]{0,1:T(8,128)(2,1)}, bf16[256,512]{0,1:T(8,128)(2,1)}, u32[]{:S(2)}, u32[]{:S(2)}) collective-permute-start(bf16[256,512]{0,1:T(8,128)(2,1)} %copy.23), channel_id=1, source_target_pairs={{0,8},{4,12},{8,0},{12,4},{16,24},{20,28},{24,16},{28,20},{1,9},{5... | collective-permute-start | bytes 786440 | tf_op jit(solution)/shard_map/ppermute | solution.py:341
  81.7 14.2 %collective-permute-start.23 = (bf16[256,1024]{1,0:T(8,128)(2,1)S(1)}, bf16[256,1024]{1,0:T(8,128)(2,1)}, u32[]{:S(2)}, u32[]{:S(2)}) collective-permute-start(bf16[256,1024]{1,0:T(8,128)(2,1)S(1)} %get-tuple-element.137), channel_id=1, source_target_pairs={{0,4},{4,0},{8,12},{12,8},{16,20},{20,16},{24,28},{28,24},{1,5},{5... | collective-permute-start | bytes 1572872 | tf_op jit(solution)/shard_map/ppermute | solution.py:341
  82.8 11.0 %collective-permute-start.20 = (bf16[256,512]{1,0:T(8,128)(2,1)S(1)}, bf16[256,512]{1,0:T(8,128)(2,1)}, u32[]{:S(2)}, u32[]{:S(2)}) collective-permute-start(bf16[256,512]{1,0:T(8,128)(2,1)S(1)} %get-tuple-element.129), channel_id=1, source_target_pairs={{0,8},{4,12},{8,0},{12,4},{16,24},{20,28},{24,16},{28,20},{1,9},{5... | collective-permute-start | bytes 786440 | tf_op jit(solution)/shard_map/ppermute | solution.py:341
  84.4 14.4 %collective-permute-start.19 = (bf16[256,512]{1,0:T(8,128)(2,1)S(1)}, bf16[256,512]{1,0:T(8,128)(2,1)S(1)}, u32[]{:S(2)}, u32[]{:S(2)}) collective-permute-start(bf16[256,512]{1,0:T(8,128)(2,1)S(1)} %get-tuple-element.127), channel_id=1, source_target_pairs={{0,16},{4,20},{8,24},{12,28},{16,0},{20,4},{24,8},{28,12},{1,17},{... | collective-permute-start | bytes 786440 | tf_op jit(solution)/shard_map/ppermute | solution.py:341
  85.6 16.9 %collective-permute-start.22 = (bf16[256,512]{1,0:T(8,128)(2,1)S(1)}, bf16[256,512]{1,0:T(8,128)(2,1)S(1)}, u32[]{:S(2)}, u32[]{:S(2)}) collective-permute-start(bf16[256,512]{1,0:T(8,128)(2,1)S(1)} %get-tuple-element.131), channel_id=1, source_target_pairs={{0,8},{4,12},{8,0},{12,4},{16,24},{20,28},{24,16},{28,20},{1,9},{5... | collective-permute-start | bytes 786440 | tf_op jit(solution)/shard_map/ppermute | solution.py:341
  103.1 20.4 %collective-permute-start.24 = (bf16[256,512]{1,0:T(8,128)(2,1)S(1)}, bf16[256,512]{1,0:T(8,128)(2,1)S(1)}, u32[]{:S(2)}, u32[]{:S(2)}) collective-permute-start(bf16[256,512]{1,0:T(8,128)(2,1)S(1)} %add_add_fusion.1.ko_ref.refs_0_), channel_id=1, source_target_pairs={{0,8},{4,12},{8,0},{12,4},{16,24},{20,28},{24,16},{28,20},{1,9},{5... | collective-permute-start | bytes 786440 | tf_op jit(solution)/shard_map/ppermute | solution.py:341
  104.6 19.9 %collective-permute-start.28 = (bf16[256,512]{1,0:T(8,128)(2,1)S(1)}, bf16[256,512]{1,0:T(8,128)(2,1)S(1)}, u32[]{:S(2)}, u32[]{:S(2)}) collective-permute-start(bf16[256,512]{1,0:T(8,128)(2,1)S(1)} %add_add_fusion.vo_ref.refs_4_), channel_id=1, source_target_pairs={{0,16},{4,20},{8,24},{12,28},{16,0},{20,4},{24,8},{28,12},{1,17},{... | collective-permute-start | bytes 786440 | tf_op jit(solution)/shard_map/ppermute | solution.py:341
  105.7 29.1 %collective-permute-start.25 = (bf16[256,512]{1,0:T(8,128)(2,1)S(1)}, bf16[256,512]{1,0:T(8,128)(2,1)S(1)}, u32[]{:S(2)}, u32[]{:S(2)}) collective-permute-start(bf16[256,512]{1,0:T(8,128)(2,1)S(1)} %add_add_fusion.1.ko_ref.refs_0_), channel_id=1, source_target_pairs={{0,16},{4,20},{8,24},{12,28},{16,0},{20,4},{24,8},{28,12},{1,17},{... | collective-permute-start | bytes 786440 | tf_op jit(solution)/shard_map/ppermute | solution.py:341
  106.6 28.1 %collective-permute-start.27 = (bf16[256,512]{1,0:T(8,128)(2,1)S(1)}, bf16[256,512]{1,0:T(8,128)(2,1)S(1)}, u32[]{:S(2)}, u32[]{:S(2)}) collective-permute-start(bf16[256,512]{1,0:T(8,128)(2,1)S(1)} %add_add_fusion.vo_ref.refs_4_), channel_id=1, source_target_pairs={{0,8},{4,12},{8,0},{12,4},{16,24},{20,28},{24,16},{28,20},{1,9},{5... | collective-permute-start | bytes 786440 | tf_op jit(solution)/shard_map/ppermute | solution.py:341
  116.8 18.0 %collective-permute-start.32 = (bf16[1024,128]{1,0:T(8,128)(2,1)S(1)}, bf16[1024,128]{1,0:T(8,128)(2,1)S(1)}, u32[]{:S(2)}, u32[]{:S(2)}) collective-permute-start(bf16[1024,128]{1,0:T(8,128)(2,1)S(1)} %shard_map.123), channel_id=1, source_target_pairs={{0,2},{1,3},{2,0},{3,1},{4,6},{5,7},{6,4},{7,5},{8,10},{9,11},{10,... | collective-permute-start | bytes 786440 | tf_op jit(solution)/shard_map/ppermute | solution.py:344
  123.5 11.3 %collective-permute-start.26 = (bf16[256,512]{1,0:T(8,128)(2,1)S(1)}, bf16[256,512]{1,0:T(8,128)(2,1)S(1)}, u32[]{:S(2)}, u32[]{:S(2)}) collective-permute-start(bf16[256,512]{1,0:T(8,128)(2,1)S(1)} %collective-permute-done.24.refs_1_), channel_id=1, source_target_pairs={{0,16},{4,20},{8,24},{12,28},{16,0},{20,4},{24,8},{28,12},{1,17},{... | collective-permute-start | bytes 786440 | tf_op jit(solution)/shard_map/ppermute | solution.py:341
  136.8 11.0 %collective-permute-start.33 = (bf16[1024,128]{1,0:T(8,128)(2,1)S(1)}, bf16[1024,128]{1,0:T(8,128)(2,1)S(1)}, u32[]{:S(2)}, u32[]{:S(2)}) collective-permute-start(bf16[1024,128]{1,0:T(8,128)(2,1)S(1)} %shard_map.124), channel_id=1, source_target_pairs={{0,1},{1,2},{2,3},{3,0},{4,5},{5,6},{6,7},{7,4},{8,9},{9,10},{10,1... | collective-permute-start | bytes 786440 | tf_op jit(solution)/shard_map/ppermute | solution.py:344
  137.2 14.0 %collective-permute-start.34 = (bf16[1024,128]{1,0:T(8,128)(2,1)S(1)}, bf16[1024,128]{1,0:T(8,128)(2,1)S(1)}, u32[]{:S(2)}, u32[]{:S(2)}) collective-permute-start(bf16[1024,128]{1,0:T(8,128)(2,1)S(1)} %shard_map.125), channel_id=1, source_target_pairs={{0,3},{1,0},{2,1},{3,2},{4,7},{5,4},{6,5},{7,6},{8,11},{9,8},{10,9... | collective-permute-start | bytes 786440 | tf_op jit(solution)/shard_map/ppermute | solution.py:344
  (36 other events, 207.7 us)

commit v4 on v3

--- a/solution.py
+++ b/solution.py
@@ -26,7 +26,7 @@
 
 
 def cost(flops, nbytes, exps=0):
-    return pl.CostEstimate(flops=flops, bytes_accessed=nbytes, transcendentals=exps)
+    return pl.CostEstimate(flops=flops // 1024, bytes_accessed=nbytes // 1024, transcendentals=exps // 1024)
 
 
 def whole(shape):
@@ -95,7 +95,7 @@
             ],
         ),
         out_shape=[jax.ShapeDtypeStruct(half, BF16)] * 2 if final else jax.ShapeDtypeStruct(out_shape, F32),
-        compiler_params=params(22),
+        compiler_params=params(48),
         cost_estimate=cost(8 * blocks * rows * depth * gw, 4 * blocks * depth * gw),
     )(at, key_weight, value_weight, *owns, *partners, *([sums] if final else []))
 
@@ -103,7 +103,7 @@
 def split_kernel(peers, at, *refs):
     owns, partners = refs[:peers], refs[peers : 2 * peers]
     outs, all_ref = refs[2 * peers : -1], refs[-1]
-    size = outs[0].shape[1]
+    size = outs[0].shape[0]
     per = owns[0].shape[1] // size
     for r in range(peers):
         for c in range(per):
@@ -112,7 +112,7 @@
     for j, out in enumerate(outs):
         target = at[0] ^ (2 * j)
         r = lax.rem(at[1] + peers - lax.div(target, per), peers)
-        out[...] = all_ref[r * per + lax.rem(target, per)]
+        out[...] = all_ref[r * per + lax.rem(target, per)].astype(F32).T.astype(BF16)
 
 
 def split_columns(chips, at, owns, partners):
@@ -125,22 +125,22 @@
             num_scalar_prefetch=1,
             grid=(1,),
             in_specs=[whole((rows, depth))] * (2 * peers),
-            out_specs=[whole((2 * rows, size))] * chips,
+            out_specs=[whole((size, 2 * rows))] * chips,
             scratch_shapes=[pltpu.VMEM((2 * chips, 2 * rows, size), BF16)],
         ),
-        out_shape=[jax.ShapeDtypeStruct((2 * rows, size), BF16)] * chips,
+        out_shape=[jax.ShapeDtypeStruct((size, 2 * rows), BF16)] * chips,
         compiler_params=params(16),
         cost_estimate=cost(0, 8 * peers * rows * depth),
     )(at, *owns, *partners)
 
 
-def attend_kernel(chips, window, at, table, q_ref, g_ref, pair_ref, *refs):
+def attend_kernel(chips, window, at, table, own_ref, pair_ref, *refs):
     keys, values = refs[:chips], refs[chips : 2 * chips]
     att_ref, qg_ref, back_ref = refs[2 * chips : 2 * chips + 3]
     outs = refs[2 * chips + 3 : -3]
     outs = (outs[:chips], outs[chips:])
     open_ref, key_ref, grad_ref = refs[-3:]
-    rows, gw = q_ref.shape
+    rows, gw = att_ref.shape
     shards = 2 * chips
     packed = keys[0].shape[0] // 2
     keys_n = shards * window
@@ -166,7 +166,7 @@
         for h in range(gw // HD):
             mine = slice(h * HD, (h + 1) * HD)
             theirs = slice(gw + h * HD, gw + (h + 1) * HD)
-            q, g = (pair_ref[:, mine], pair_ref[:, theirs]) if d else (q_ref[:, mine], g_ref[:, mine])
+            q, g = ((own_ref, pair_ref)[d][:, place] for place in (mine, theirs))
             k, v = key_ref[d, :, mine], key_ref[d, :, theirs]
             scores = mm(q, k, NT) * scale + open_ref[d]
             top = jnp.max(scores, axis=1, keepdims=True)
@@ -190,12 +190,11 @@
                 outs[m][u // 2][pl.ds(bases[u], window), :] += part
 
 
-def attend(window, at, table, queries, out_grad, pair, keys, values):
-    rows, width = queries.shape
+def attend(window, at, table, own, pair, keys, values):
+    rows, width = own.shape
     gw = width // 2
     chips = len(keys)
     keys_n = 2 * chips * window
-    row_spec = pl.BlockSpec((rows, gw), lambda n, at, *_: (0, at[0] & 1))
     half = jax.ShapeDtypeStruct((rows, gw), BF16)
     both = jax.ShapeDtypeStruct((rows, width), BF16)
     block = keys[0].shape
@@ -204,7 +203,7 @@
         grid_spec=pltpu.PrefetchScalarGridSpec(
             num_scalar_prefetch=2,
             grid=(1,),
-            in_specs=[row_spec] * 2 + [whole((rows, width))] + [whole(keys[0].shape)] * (2 * chips),
+            in_specs=[whole((rows, width))] * 2 + [whole(keys[0].shape)] * (2 * chips),
             out_specs=[whole((rows, gw))] * 2 + [whole((rows, width))] + [whole(block)] * (2 * chips),
             scratch_shapes=[
                 pltpu.VMEM((2, rows, keys_n), F32),
@@ -215,12 +214,12 @@
         out_shape=[half, half, both] + [jax.ShapeDtypeStruct(block, BF16)] * (2 * chips),
         compiler_params=params(20 if keys_n <= 640 else 28),
         cost_estimate=cost(24 * rows * keys_n * gw, 8 * rows * width + 4 * keys_n * width, 4 * rows * keys_n),
-    )(at, table, queries, out_grad, pair, *keys, *values)
-
-
-def back_kernel(r, chunks, at, ko_ref, vo_ref, kp_ref, vp_ref, kw_ref, vw_ref, out_ref, w_ref, turned_ref, sems):
+    )(at, table, own, pair, *keys, *values)
+
+
+def back_kernel(r, chunks, at, own_ref, other_ref, kw_ref, vw_ref, out_ref, w_ref, turned_ref, sems):
     depth, rows = out_ref.shape
-    gw = ko_ref.shape[1]
+    gw = own_ref.shape[1] // 2
     tile = min(TILE, depth)
     steps = depth // tile
     first = lax.rem(at[1] + r, chunks) * depth
@@ -230,10 +229,10 @@
             place = pl.ds(pl.multiple_of(first + n * tile, tile), tile)
             copies.append(pltpu.make_async_copy(ref.at[place, :], w_ref.at[m, n], sems.at[m, n]))
             copies[-1].start()
-    for n, pair in enumerate(((ko_ref, vo_ref), (kp_ref, vp_ref))):
+    for n, ref in enumerate((own_ref, other_ref)):
         start = pl.multiple_of(((at[0] & 1) ^ n) * gw, gw)
-        for m, ref in enumerate(pair):
-            turned_ref[m, pl.ds(start, gw), :] = ref[...].astype(F32).T.astype(BF16)
+        for m in range(2):
+            turned_ref[m, pl.ds(start, gw), :] = ref[:, m * gw : (m + 1) * gw].astype(F32).T.astype(BF16)
     for n in range(steps):
         copies[2 * n].wait()
         copies[2 * n + 1].wait()
@@ -242,18 +241,18 @@
 
 
 def project_back(r, chunks, at, own, other, key_weight, value_weight):
-    rows, gw = own[0].shape
-    rows = rows // 2
+    rows, width = own.shape
+    rows, gw = rows // 2, width // 2
     depth = key_weight.shape[0] // chunks
     tile = min(TILE, depth)
     steps = depth // tile
-    row_spec = pl.BlockSpec((rows, gw), lambda n, at: (at[0] & 1, 0))
+    row_spec = pl.BlockSpec((rows, width), lambda n, at: (at[0] & 1, 0))
     return pl.pallas_call(
         functools.partial(back_kernel, r, chunks),
         grid_spec=pltpu.PrefetchScalarGridSpec(
             num_scalar_prefetch=1,
             grid=(1,),
-            in_specs=[row_spec] * 4 + [pl.BlockSpec(memory_space=pltpu.HBM)] * 2,
+            in_specs=[row_spec] * 2 + [pl.BlockSpec(memory_space=pltpu.HBM)] * 2,
             out_specs=whole((depth, rows)),
             scratch_shapes=[
                 pltpu.VMEM((2, steps, tile, 2 * gw), BF16),
@@ -262,9 +261,9 @@
             ],
         ),
         out_shape=jax.ShapeDtypeStruct((depth, rows), BF16),
-        compiler_params=params(16),
+        compiler_params=params(48),
         cost_estimate=cost(8 * rows * gw * depth, 8 * gw * depth),
-    )(at, *own, *other, key_weight, value_weight)
+    )(at, own, other, key_weight, value_weight)
 
 
 def weight_grad_kernel(chips, at, col_ref, *refs):
@@ -284,27 +283,36 @@
 
 
 def weight_grads(at, cols, owns, others):
-    chips = len(owns[0])
-    rows, gw = owns[0][0].shape
-    width = 2 * gw
+    chips = len(owns)
+    rows, width = owns[0].shape
+    gw = width // 2
     size = cols.shape[0]
     steps = gw // TILE
-    own_spec = pl.BlockSpec((rows, TILE), lambda n, at: (0, jnp.minimum(n, steps - 1)))
-    other_spec = pl.BlockSpec((rows, TILE), lambda n, at: (0, jnp.maximum(n - steps, 0)))
+    arrays, specs = [], []
+    for blocks, column in (
+        (owns, lambda n: jnp.minimum(n, steps - 1)),
+        (others, lambda n: jnp.maximum(n - steps, 0)),
+    ):
+        for half in range(2):
+            for block in blocks:
+                split = isinstance(block, tuple)
+                first = 0 if split else half * steps
+                arrays.append(block[half] if split else block)
+                specs.append(pl.BlockSpec((rows, TILE), lambda n, at, f=first, c=column: (0, f + c(n))))
     out_spec = pl.BlockSpec((size, TILE), lambda n, at: (0, (n // steps ^ (at[0] & 1)) * steps + n % steps))
     return pl.pallas_call(
         functools.partial(weight_grad_kernel, chips),
         grid_spec=pltpu.PrefetchScalarGridSpec(
             num_scalar_prefetch=1,
             grid=(2 * steps,),
-            in_specs=[whole(cols.shape)] + [own_spec] * (2 * chips) + [other_spec] * (2 * chips),
+            in_specs=[whole(cols.shape)] + specs,
             out_specs=[out_spec] * 2,
             scratch_shapes=[pltpu.VMEM((2, chips * rows, TILE), BF16)],
         ),
         out_shape=[jax.ShapeDtypeStruct((size, width), F32)] * 2,
         compiler_params=params(16 if chips <= 4 else 28),
         cost_estimate=cost(4 * chips * rows * size * width, 2 * chips * rows * (size + 2 * width) + 8 * size * width),
-    )(at, cols, *owns[0], *owns[1], *others[0], *others[1])
+    )(at, cols, *arrays)
 
 
 def window_table(dp, enc_len, route, dec_len, window):
@@ -365,41 +373,48 @@
             sums[b] = functools.reduce(jnp.add, [parts[b]] + [flip(parts[a + b], 2 * a) for a in first])
         return functools.reduce(jnp.add, [flip(sums[b], 2 * b) for b in second] + [sums[0]])
 
+    def half_of(x, which):
+        return lax.dynamic_slice_in_dim(x, which * gw, gw, axis=1)
+
     partner = flip(enc_rows, 1)
     owns = [enc_rows] + [shift(enc_rows, r) for r in range(1, peers)]
+    mine, theirs = (jnp.concatenate([half_of(queries, c), half_of(out_grad, c)], axis=1) for c in (core, 1 - core))
+    pair = flip(theirs, 1)
+    start, length, begin = window_table(dp, enc_len, route, dec_len, window)
+    base = jnp.minimum(start // 16 * 16, packed - window)
+    table = jnp.stack([base, start - base, start - base + length, begin])
     sums = project(0, at, key_weight, value_weight, [enc_rows], [partner])
-    sums, owns = lax.optimization_barrier((sums, owns))
+    sums, table, mine, pair, owns = lax.optimization_barrier((sums, table, mine, pair, owns))
     partners = [partner] + [flip(x, 1) for x in owns[1:]]
     keys, values = project(1, at, key_weight, value_weight, owns[1:], partners[1:], sums)
-    keys, values, lens, targets, decs, *theirs = lax.optimization_barrier(
-        (keys, values, enc_len, route, dec_len, queries, out_grad)
-    )
     keys, values = spread(keys, True), spread(values, False)
-    theirs = [lax.dynamic_slice_in_dim(x, (1 - core) * gw, gw, axis=1) for x in theirs]
-    pair = flip(jnp.concatenate(theirs, axis=1), 1)
-    start, length, begin = window_table(dp, lens, targets, decs, window)
-    base = jnp.minimum(start // 16 * 16, packed - window)
-    table = jnp.stack([base, start - base, start - base + length, begin])
     cols = split_columns(chips, at, owns, partners)
-    keys, values, table, pair, cols = lax.optimization_barrier((keys, values, table, pair, list(cols)))
+    keys, values, cols = lax.optimization_barrier((keys, values, list(cols)))
     cols = [cols[0]] + [flip(cols[j], 2 * j) for j in range(1, chips)]
-    attended, query_grad, back, *parts = attend(window, at, table, queries, out_grad, pair, keys, values)
+    attended, query_grad, back, *parts = attend(window, at, table, mine, pair, keys, values)
     parts, back, cols = lax.optimization_barrier((parts, back, cols))
-    own = [collect(parts[:chips], False), collect(parts[chips:], True)]
+    own = jnp.concatenate([collect(parts[:chips], False), collect(parts[chips:], True)], axis=1)
     back = flip(back, 1)
     outs = []
-    for mine, rest in ((attended, back[:, :gw]), (query_grad, back[:, gw:])):
-        outs.append(jnp.where(core == 0, jnp.concatenate([mine, rest], 1), jnp.concatenate([rest, mine], 1)))
-    cols = jnp.concatenate([x.T for x in cols], axis=1)
-    own, cols, outs = lax.optimization_barrier((own, cols, outs))
-    other = [flip(x, 1) for x in own]
-    owns = [spread(own[0], True), spread(own[1], False)]
+    for here, rest in ((attended, back[:, :gw]), (query_grad, back[:, gw:])):
+        outs.append(jnp.where(core == 0, jnp.concatenate([here, rest], 1), jnp.concatenate([rest, here], 1)))
+    cols = jnp.concatenate(cols, axis=1)
+    own, cols = lax.optimization_barrier((own, cols))
+    other = flip(own, 1)
     middle = peers // 2
     order = [middle] + [r for r in range(1, peers) if r != middle] + [0]
     chunks = [project_back(r, peers, at, own, other, key_weight, value_weight) for r in order]
     arrived = [shift(x, r) for x, r in zip(chunks[:-1], order)]
-    owns, arrived[0], _, chunk = lax.optimization_barrier((owns, arrived[0], chunks[:-1], chunks[-1]))
-    others = [[other[n]] + [flip(x, 1) for x in owns[n][1:]] for n in range(2)]
+    owns = {0: own}
+    for j in [*lows, *highs]:
+        owns[j] = flip(own, 2 * j)
+    owns, _ = lax.optimization_barrier((owns, chunks[:-1]))
+    for a in lows:
+        for b in highs:
+            owns[a + b] = (flip(owns[a][:, :gw], 2 * b), flip(owns[b][:, gw:], 2 * a))
+    owns = [owns[j] for j in range(chips)]
+    owns, arrived[:2], chunk, outs = lax.optimization_barrier((owns, arrived[:2], chunks[-1], outs))
+    others = [other] + [tuple(flip(y, 1) for y in x) if isinstance(x, tuple) else flip(x, 1) for x in owns[1:]]
     weight_out = weight_grads(at, cols, owns, others)
     arrived, weight_out = lax.optimization_barrier((arrived, weight_out))
     total = functools.reduce(jnp.add, [x.astype(F32) for x in [chunk, *arrived]])

time: 153 us -> 126 us (0.82)
  local copies, waits for them, and re-layouts: 31.5 us -> 3.94 us
  waiting for transfers between devices: 32.3 us -> 40.6 us
  starting transfers between devices: 48.8 us -> 42 us
  other arithmetic: 7.07 us -> 4.06 us
  Pallas kernels: 31.6 us -> 33.8 us
    unnamed x37 -> x7, local copies, waits for them, and re-layouts: 26.1 us -> 0.86 us
    ppermute x35 -> x30, waiting for transfers between devices: 16.5 us -> 31.6 us  [flip(): return lax.ppermute(x, 'dp', [(i, i ^ r) for i in range(shards)])]
    ppermute x6, waiting for transfers between devices: 11.8 us -> 6.6 us  [shift(): return lax.ppermute(x, 'mp', [(i, (i + r) % peers) for i in range(peers)])]
    ppermute x35 -> x30, starting transfers between devices: 27.3 us -> 23.3 us  [flip(): return lax.ppermute(x, 'dp', [(i, i ^ r) for i in range(shards)])]
    pallas_call x4, Pallas kernels: 11.5 us -> 14.4 us  [project_back(): pl.pallas_call(functools.partial(back_kernel, r, chunks), grid_spec=pltpu...]
    ppermute x6, starting transfers between devices: 17.6 us -> 15 us  [shift(): return lax.ppermute(x, 'mp', [(i, (i + r) % peers) for i in range(peers)])]
    optimization_barrier x4 -> x0, local copies, waits for them, and re-layouts: 2.62 us -> none  [the longest x3 2.48 us: body(): lax.optimization_barrier((keys, values, table, pair, list(cols)))]
    add x2, other arithmetic: 2.03 us -> 0.13 us  [collect(): functools.reduce(jnp.add, [parts[b]] + [flip(parts[a + b], 2 * a) for a i...]
  transfers between devices with their start and end apart: 42 -> 37, of which waited for: 15 -> 19; matrix products, arithmetic and copies ran while one was open for 6% -> 5% of each run, Pallas kernels for 18% -> 24%
where the time goes in v4:
time: 126 us; the launch traced here: 125 us
  starting transfers between devices  42 us (33%)
  waiting for transfers between devices  40.6 us (32%)
  Pallas kernels  33.8 us (27%)
  other arithmetic  4.06 us (3%)
  local copies, waits for them, and re-layouts  3.94 us (3%)
    ppermute x30, waiting for transfers between devices, flip(): return lax.ppermute(x, 'dp', [(i, i ^ r) for i in range(shards)])  31.6 us
    ppermute x30, starting transfers between devices, flip(): return lax.ppermute(x, 'dp', [(i, i ^ r) for i in range(shards)])  23.3 us
    ppermute x6, starting transfers between devices, shift(): return lax.ppermute(x, 'mp', [(i, (i + r) % peers) for i in range(peers)])  15 us
    pallas_call x4, Pallas kernels, project_back(): pl.pallas_call(functools.partial(back_kernel, r, chunks), grid_spec=pltpu...  14.4 us
    ppermute x6, waiting for transfers between devices, shift(): return lax.ppermute(x, 'mp', [(i, (i + r) % peers) for i in range(peers)])  6.6 us
    pallas_call x2, Pallas kernels, project(): pl.pallas_call(functools.partial(project_kernel, first, blocks, cuts, fin...  6.47 us
    pallas_call x1, Pallas kernels, attend(): pl.pallas_call(functools.partial(attend_kernel, chips, window), grid_spec...  6.44 us
    pallas_call x1, Pallas kernels, weight_grads(): pl.pallas_call(functools.partial(weight_grad_kernel, chips), grid_spec=pl...  5.46 us
  transfers between devices with their start and end apart: 37, of which 19 were waited for; matrix products, arithmetic and copies ran while one was open for 5% of the time, Pallas kernels for 24%

profile of v4, /device:TPU:0, one launch (start us, length us, event | category | flops | bytes accessed | tf_op | source)
XLA Modules:
  0.0 125.4 jit_solution(3286896667688841817)
XLA Ops:
  0.6 4.1 %collective-permute-start.3 = (bf16[128,1024]{1,0:T(8,128)(2,1)}, bf16[128,1024]{1,0:T(8,128)(2,1)S(1)}, u32[]{:S(2)}, u32[]{:S(2)}) collective-permute-start(bf16[128,1024]{1,0:T(8,128)(2,1)} %refs_0_.2), channel_id=1, source_target_pairs={{0,2},{1,3},{2,0},{3,1},{4,6},{5,7},{6,4},{7,5},{8,10},{9,11},{10,... | collective-permute-start | bytes 786440 | tf_op jit(solution)/shard_map/ppermute | solution.py:352
  6.3 2.2 %collective-permute-start.4 = (bf16[128,1024]{1,0:T(8,128)(2,1)}, bf16[128,1024]{1,0:T(8,128)(2,1)S(1)}, u32[]{:S(2)}, u32[]{:S(2)}) collective-permute-start(bf16[128,1024]{1,0:T(8,128)(2,1)} %refs_0_.2), channel_id=1, source_target_pairs={{0,3},{1,0},{2,1},{3,2},{4,7},{5,4},{6,5},{7,6},{8,11},{9,8},{10,9... | collective-permute-start | bytes 786440 | tf_op jit(solution)/shard_map/ppermute | solution.py:352
  9.9 3.7 %all-to-all-start = ((s32[8,1,24]{2,1,0:T(1,128)}), s32[8,1,24]{2,1,0:T(1,128)S(1)}, u32[]{:S(2)}, u32[]{:S(2)}) async-start(s32[8,1,24]{2,1,0:T(1,128)} %broadcast_in_dim.92), calls=%async_computation | async-start | bytes 8192 | tf_op jit(solution)/shard_map/all_to_all | solution.py:321
  15.8 2.4 %all-to-all-done = s32[8,1,24]{2,1,0:T(1,128)S(1)} async-done(((s32[8,1,24]{2,1,0:T(1,128)}), s32[8,1,24]{2,1,0:T(1,128)S(1)}, u32[]{:S(2)}, u32[]{:S(2)}) %all-to-all-start) | async-done | bytes 800 | tf_op jit(solution)/shard_map/all_to_all | solution.py:321
  18.9 2.5 %shard_map.119.refs_6_ = f32[256,1024]{1,0:T(8,128)S(1)} custom-call(s32[2]{0:T(128)S(1)} %pad_add_fusion.1.at, bf16[4096,1024]{1,0:T(8,128)(2,1)} %kw_ref.11, bf16[4096,1024]{1,0:T(8,128)(2,1)} %vw_ref.11, bf16[128,1024]{1,0:T(8,128)(2,1)S(1)} %copy-done, bf16[128,1024]{1,0:T(8,128)(2,1)S(1)} %collective-permute-done.refs_1_.refs_4_), custom_call_target="tpu_custom_call" | custom-call | flops 524288 | bytes 2048 | tf_op jit(solution)/shard_map/pallas_call | solution.py:81
  21.5 1.9 %collective-permute-done.3.refs_1_.refs_2_ = bf16[128,1024]{1,0:T(8,128)(2,1)S(1)} collective-permute-done((bf16[128,1024]{1,0:T(8,128)(2,1)}, bf16[128,1024]{1,0:T(8,128)(2,1)S(1)}, u32[]{:S(2)}, u32[]{:S(2)}) %collective-permute-start.3) | collective-permute-done | bytes 262176 | tf_op jit(solution)/shard_map/ppermute | solution.py:352
  23.4 1.9 %collective-permute-done.4.refs_2_.refs_3_ = bf16[128,1024]{1,0:T(8,128)(2,1)S(1)} collective-permute-done((bf16[128,1024]{1,0:T(8,128)(2,1)}, bf16[128,1024]{1,0:T(8,128)(2,1)S(1)}, u32[]{:S(2)}, u32[]{:S(2)}) %collective-permute-start.4) | collective-permute-done | bytes 262176 | tf_op jit(solution)/shard_map/ppermute | solution.py:352
  27.6 3.9 %shard_map.120 = (bf16[256,512]{1,0:T(8,128)(2,1)S(1)}, bf16[256,512]{1,0:T(8,128)(2,1)S(1)}) custom-call(s32[2]{0:T(128)S(1)} %pad_add_fusion.1.at, bf16[4096,1024]{1,0:T(8,128)(2,1)} %kw_ref.11, bf16[4096,1024]{1,0:T(8,128)(2,1)} %vw_ref.11, bf16[128,1024]{1,0:T(8,128)(2,1)S(1)} %collective-permute-done.2.refs_0_.refs_1_, ...), custom_call_target="tpu_custom_call" | custom-call | flops 1572864 | bytes 6144 | tf_op jit(solution)/shard_map/pallas_call | solution.py:81
  35.7 5.1 %collective-permute-done.8.refs_1_ = bf16[256,512]{1,0:T(8,128)(2,1)S(1)} collective-permute-done((bf16[256,512]{1,0:T(8,128)(2,1)S(1)}, bf16[256,512]{1,0:T(8,128)(2,1)S(1)}, u32[]{:S(2)}, u32[]{:S(2)}) %collective-permute-start.8) | collective-permute-done | bytes 262176 | tf_op jit(solution)/shard_map/ppermute | solution.py:349
  44.8 3.1 %collective-permute-done.9.refs_2_ = bf16[256,512]{1,0:T(8,128)(2,1)S(1)} collective-permute-done((bf16[256,512]{1,0:T(8,128)(2,1)S(1)}, bf16[256,512]{1,0:T(8,128)(2,1)S(1)}, u32[]{:S(2)}, u32[]{:S(2)}) %collective-permute-start.9) | collective-permute-done | bytes 262176 | tf_op jit(solution)/shard_map/ppermute | solution.py:349
  48.0 4.5 %collective-permute-done.10.refs_3_ = bf16[256,512]{1,0:T(8,128)(2,1)S(1)} collective-permute-done((bf16[256,512]{1,0:T(8,128)(2,1)S(1)}, bf16[256,512]{1,0:T(8,128)(2,1)S(1)}, u32[]{:S(2)}, u32[]{:S(2)}) %collective-permute-start.10) | collective-permute-done | bytes 262176 | tf_op jit(solution)/shard_map/ppermute | solution.py:349
  55.9 6.4 %shard_map.122 = (bf16[256,512]{1,0:T(8,128)(2,1)S(1)}, bf16[256,512]{1,0:T(8,128)(2,1)S(1)}, bf16[256,1024]{1,0:T(8,128)(2,1)}, bf16[256,512]{1,0:T(8,128)(2,1)...) custom-call(s32[2]{0:T(128)S(1)} %pad_add_fusion.1.at, ...), custom_call_target="tpu_custom_call" | custom-call | flops 1966080 | bytes 4608 | tf_op jit(solution)/shard_map/pallas_call | solution.py:201
  62.4 2.3 %collective-permute-done.15 = bf16[512,256]{1,0:T(8,128)(2,1)S(1)} collective-permute-done((bf16[512,256]{1,0:T(8,128)(2,1)S(1)}, bf16[512,256]{1,0:T(8,128)(2,1)S(1)}, u32[]{:S(2)}, u32[]{:S(2)}) %collective-permute-start.15) | collective-permute-done | bytes 262176 | tf_op jit(solution)/shard_map/ppermute | solution.py:349
  67.1 1.8 %collective-permute-start.20 = (bf16[256,512]{1,0:T(8,128)(2,1)S(1)}, bf16[256,512]{1,0:T(8,128)(2,1)S(1)}, u32[]{:S(2)}, u32[]{:S(2)}) collective-permute-start(bf16[256,512]{1,0:T(8,128)(2,1)S(1)} %get-tuple-element.117), channel_id=1, source_target_pairs={{0,8},{4,12},{8,0},{12,4},{16,24},{20,28},{24,16},{28,20},{1,9},{5... | collective-permute-start | bytes 786440 | tf_op jit(solution)/shard_map/ppermute | solution.py:349
  69.0 6.4 %collective-permute-done.17 = bf16[256,512]{1,0:T(8,128)(2,1)S(1)} collective-permute-done((bf16[256,512]{1,0:T(8,128)(2,1)S(1)}, bf16[256,512]{1,0:T(8,128)(2,1)S(1)}, u32[]{:S(2)}, u32[]{:S(2)}) %collective-permute-start.17) | collective-permute-done | bytes 262176 | tf_op jit(solution)/shard_map/ppermute | solution.py:349
  78.8 2.1 %collective-permute-done.19 = bf16[256,512]{1,0:T(8,128)(2,1)S(1)} collective-permute-done((bf16[256,512]{1,0:T(8,128)(2,1)S(1)}, bf16[256,512]{1,0:T(8,128)(2,1)S(1)}, u32[]{:S(2)}, u32[]{:S(2)}) %collective-permute-start.19) | collective-permute-done | bytes 262176 | tf_op jit(solution)/shard_map/ppermute | solution.py:349
  82.0 2.7 %collective-permute-done.22 = bf16[256,512]{1,0:T(8,128)(2,1)S(1)} collective-permute-done((bf16[256,512]{1,0:T(8,128)(2,1)S(1)}, bf16[256,512]{1,0:T(8,128)(2,1)S(1)}, u32[]{:S(2)}, u32[]{:S(2)}) %collective-permute-start.22) | collective-permute-done | bytes 262176 | tf_op jit(solution)/shard_map/ppermute | solution.py:349
  87.7 3.6 %shard_map.123 = bf16[1024,128]{1,0:T(8,128)(2,1)S(1)} custom-call(s32[2]{0:T(128)S(1)} %pad_add_fusion.1.at, bf16[256,1024]{1,0:T(8,128)(2,1)S(1)} %pad_maximum_fusion.3.own_ref.refs_0_.refs_4_, bf16[256,1024]{1,0:T(8,128)(2,1)S(1)} %collective-permute-done.25.other_ref.refs_8_.refs_12_, bf16[4096,1024]{1,0:T(8,128)(2,1)} %kw_ref.11, bf16[4096,1024]{1,0:T(8,128)(2,1)} %vw_ref.11), custom_call_target="tpu_custom_call" | custom-call | flops 524288 | bytes 4096 | tf_op jit(solution)/shard_map/pallas_call | solution.py:250
  91.3 5.5 %collective-permute-start.28 = (bf16[1024,128]{1,0:T(8,128)(2,1)S(1)}, bf16[1024,128]{1,0:T(8,128)(2,1)S(1)}, u32[]{:S(2)}, u32[]{:S(2)}) collective-permute-start(bf16[1024,128]{1,0:T(8,128)(2,1)S(1)} %shard_map.123), channel_id=1, source_target_pairs={{0,2},{1,3},{2,0},{3,1},{4,6},{5,7},{6,4},{7,5},{8,10},{9,11},{10,... | collective-permute-start | bytes 786440 | tf_op jit(solution)/shard_map/ppermute | solution.py:352
  96.8 3.7 %shard_map.124 = bf16[1024,128]{1,0:T(8,128)(2,1)S(1)} custom-call(s32[2]{0:T(128)S(1)} %pad_add_fusion.1.at, bf16[256,1024]{1,0:T(8,128)(2,1)S(1)} %pad_maximum_fusion.3.own_ref.refs_0_.refs_4_, bf16[256,1024]{1,0:T(8,128)(2,1)S(1)} %collective-permute-done.25.other_ref.refs_8_.refs_12_, bf16[4096,1024]{1,0:T(8,128)(2,1)} %kw_ref.11, bf16[4096,1024]{1,0:T(8,128)(2,1)} %vw_ref.11), custom_call_target="tpu_custom_call" | custom-call | flops 524288 | bytes 4096 | tf_op jit(solution)/shard_map/pallas_call | solution.py:250
  100.6 3.6 %shard_map.125 = bf16[1024,128]{1,0:T(8,128)(2,1)S(1)} custom-call(s32[2]{0:T(128)S(1)} %pad_add_fusion.1.at, bf16[256,1024]{1,0:T(8,128)(2,1)S(1)} %pad_maximum_fusion.3.own_ref.refs_0_.refs_4_, bf16[256,1024]{1,0:T(8,128)(2,1)S(1)} %collective-permute-done.25.other_ref.refs_8_.refs_12_, bf16[4096,1024]{1,0:T(8,128)(2,1)} %kw_ref.11, bf16[4096,1024]{1,0:T(8,128)(2,1)} %vw_ref.11), custom_call_target="tpu_custom_call" | custom-call | flops 524288 | bytes 4096 | tf_op jit(solution)/shard_map/pallas_call | solution.py:250
  109.1 3.6 %shard_map.126 = bf16[1024,128]{1,0:T(8,128)(2,1)S(1)} custom-call(s32[2]{0:T(128)S(1)} %pad_add_fusion.1.at, bf16[256,1024]{1,0:T(8,128)(2,1)S(1)} %pad_maximum_fusion.3.own_ref.refs_0_.refs_4_, bf16[256,1024]{1,0:T(8,128)(2,1)S(1)} %collective-permute-done.25.other_ref.refs_8_.refs_12_, bf16[4096,1024]{1,0:T(8,128)(2,1)} %kw_ref.11, bf16[4096,1024]{1,0:T(8,128)(2,1)} %vw_ref.11), custom_call_target="tpu_custom_call" | custom-call | flops 524288 | bytes 4096 | tf_op jit(solution)/shard_map/pallas_call | solution.py:250
  112.6 2.3 %collective-permute-done.28 = bf16[1024,128]{1,0:T(8,128)(2,1)S(1)} collective-permute-done((bf16[1024,128]{1,0:T(8,128)(2,1)S(1)}, bf16[1024,128]{1,0:T(8,128)(2,1)S(1)}, u32[]{:S(2)}, u32[]{:S(2)}) %collective-permute-start.28) | collective-permute-done | bytes 262176 | tf_op jit(solution)/shard_map/ppermute | solution.py:352
  118.5 5.5 %shard_map.127 = (f32[512,1024]{1,0:T(8,128)}, f32[512,1024]{1,0:T(8,128)}) custom-call(s32[2]{0:T(128)S(1)} %pad_add_fusion.1.at, bf16[512,1024]{1,0:T(8,128)(2,1)S(1)} %pad_maximum_fusion.col_ref, bf16[256,1024]{1,0:T(8,128)(2,1)S(1)} %pad_maximum_fusion.3.own_ref.refs_0_.refs_4_, bf16[256,1024]{1,0:T(8,128)(2,1)S(1)} %collective-permute-done.23.refs_1_.refs_5_, ...), custom_call_target="tpu_custom_call" | custom-call | flops 2097152 | bytes 9216 | tf_op jit(solution)/shard_map/pallas_call | solution.py:303
  (93 shorter events, 39.5 us)
Async XLA Ops:
  0.6 22.7 %collective-permute-start.3 = (bf16[128,1024]{1,0:T(8,128)(2,1)}, bf16[128,1024]{1,0:T(8,128)(2,1)S(1)}, u32[]{:S(2)}, u32[]{:S(2)}) collective-permute-start(bf16[128,1024]{1,0:T(8,128)(2,1)} %refs_0_.2), channel_id=1, source_target_pairs={{0,2},{1,3},{2,0},{3,1},{4,6},{5,7},{6,4},{7,5},{8,10},{9,11},{10,... | collective-permute-start | bytes 786440 | tf_op jit(solution)/shard_map/ppermute | solution.py:352
  4.7 18.6 %collective-permute-start.2 = (bf16[128,1024]{1,0:T(8,128)(2,1)}, bf16[128,1024]{1,0:T(8,128)(2,1)S(1)}, u32[]{:S(2)}, u32[]{:S(2)}) collective-permute-start(bf16[128,1024]{1,0:T(8,128)(2,1)} %refs_0_.2), channel_id=1, source_target_pairs={{0,1},{1,2},{2,3},{3,0},{4,5},{5,6},{6,7},{7,4},{8,9},{9,10},{10,1... | collective-permute-start | bytes 786440 | tf_op jit(solution)/shard_map/ppermute | solution.py:352
  6.3 12.6 %collective-permute-start = (bf16[128,1024]{1,0:T(8,128)(2,1)}, bf16[128,1024]{1,0:T(8,128)(2,1)S(1)}, u32[]{:S(2)}, u32[]{:S(2)}) collective-permute-start(bf16[128,1024]{1,0:T(8,128)(2,1)} %refs_0_.2), channel_id=1, source_target_pairs={{0,4},{4,0},{8,12},{12,8},{16,20},{20,16},{24,28},{28,24},{1,5},{5... | collective-permute-start | bytes 786440 | tf_op jit(solution)/shard_map/ppermute | solution.py:349
  6.3 19.0 %collective-permute-start.4 = (bf16[128,1024]{1,0:T(8,128)(2,1)}, bf16[128,1024]{1,0:T(8,128)(2,1)S(1)}, u32[]{:S(2)}, u32[]{:S(2)}) collective-permute-start(bf16[128,1024]{1,0:T(8,128)(2,1)} %refs_0_.2), channel_id=1, source_target_pairs={{0,3},{1,0},{2,1},{3,2},{4,7},{5,4},{6,5},{7,6},{8,11},{9,8},{10,9... | collective-permute-start | bytes 786440 | tf_op jit(solution)/shard_map/ppermute | solution.py:352
  15.0 10.3 %collective-permute-start.1 = (bf16[256,1024]{1,0:T(8,128)(2,1)S(1)}, bf16[256,1024]{1,0:T(8,128)(2,1)S(1)}, u32[]{:S(2)}, u32[]{:S(2)}) collective-permute-start(bf16[256,1024]{1,0:T(8,128)(2,1)S(1)} %pad_maximum_fusion.2), channel_id=1, source_target_pairs={{0,4},{4,0},{8,12},{12,8},{16,20},{20,16},{24,28},{28,24},{1,5},{5... | collective-permute-start | bytes 1572872 | tf_op jit(solution)/shard_map/ppermute | solution.py:349
  31.5 9.2 %collective-permute-start.8 = (bf16[256,512]{1,0:T(8,128)(2,1)S(1)}, bf16[256,512]{1,0:T(8,128)(2,1)S(1)}, u32[]{:S(2)}, u32[]{:S(2)}) collective-permute-start(bf16[256,512]{1,0:T(8,128)(2,1)S(1)} %get-tuple-element.91.refs_0_), channel_id=1, source_target_pairs={{0,8},{4,12},{8,0},{12,4},{16,24},{20,28},{24,16},{28,20},{1,9},{5... | collective-permute-start | bytes 786440 | tf_op jit(solution)/shard_map/ppermute | solution.py:349
  33.1 9.2 %collective-permute-start.12 = (bf16[256,512]{1,0:T(8,128)(2,1)S(1)}, bf16[256,512]{1,0:T(8,128)(2,1)S(1)}, u32[]{:S(2)}, u32[]{:S(2)}) collective-permute-start(bf16[256,512]{1,0:T(8,128)(2,1)S(1)} %get-tuple-element.95.refs_4_), channel_id=1, source_target_pairs={{0,16},{4,20},{8,24},{12,28},{16,0},{20,4},{24,8},{28,12},{1,17},{... | collective-permute-start | bytes 786440 | tf_op jit(solution)/shard_map/ppermute | solution.py:349
  34.7 13.3 %collective-permute-start.9 = (bf16[256,512]{1,0:T(8,128)(2,1)S(1)}, bf16[256,512]{1,0:T(8,128)(2,1)S(1)}, u32[]{:S(2)}, u32[]{:S(2)}) collective-permute-start(bf16[256,512]{1,0:T(8,128)(2,1)S(1)} %get-tuple-element.91.refs_0_), channel_id=1, source_target_pairs={{0,16},{4,20},{8,24},{12,28},{16,0},{20,4},{24,8},{28,12},{1,17},{... | collective-permute-start | bytes 786440 | tf_op jit(solution)/shard_map/ppermute | solution.py:349
  35.2 12.8 %collective-permute-start.11 = (bf16[256,512]{1,0:T(8,128)(2,1)S(1)}, bf16[256,512]{1,0:T(8,128)(2,1)S(1)}, u32[]{:S(2)}, u32[]{:S(2)}) collective-permute-start(bf16[256,512]{1,0:T(8,128)(2,1)S(1)} %get-tuple-element.95.refs_4_), channel_id=1, source_target_pairs={{0,8},{4,12},{8,0},{12,4},{16,24},{20,28},{24,16},{28,20},{1,9},{5... | collective-permute-start | bytes 786440 | tf_op jit(solution)/shard_map/ppermute | solution.py:349
  40.8 11.7 %collective-permute-start.10 = (bf16[256,512]{1,0:T(8,128)(2,1)S(1)}, bf16[256,512]{1,0:T(8,128)(2,1)S(1)}, u32[]{:S(2)}, u32[]{:S(2)}) collective-permute-start(bf16[256,512]{1,0:T(8,128)(2,1)S(1)} %collective-permute-done.8.refs_1_), channel_id=1, source_target_pairs={{0,16},{4,20},{8,24},{12,28},{16,0},{20,4},{24,8},{28,12},{1,17},{... | collective-permute-start | bytes 786440 | tf_op jit(solution)/shard_map/ppermute | solution.py:349
  42.3 10.1 %collective-permute-start.13 = (bf16[256,512]{1,0:T(8,128)(2,1)S(1)}, bf16[256,512]{1,0:T(8,128)(2,1)S(1)}, u32[]{:S(2)}, u32[]{:S(2)}) collective-permute-start(bf16[256,512]{1,0:T(8,128)(2,1)S(1)} %collective-permute-done.12.refs_6_), channel_id=1, source_target_pairs={{0,8},{4,12},{8,0},{12,4},{16,24},{20,28},{24,16},{28,20},{1,9},{5... | collective-permute-start | bytes 786440 | tf_op jit(solution)/shard_map/ppermute | solution.py:349
  52.4 9.9 %collective-permute-start.14 = (bf16[512,256]{1,0:T(8,128)(2,1)S(1)}, bf16[512,256]{1,0:T(8,128)(2,1)S(1)}, u32[]{:S(2)}, u32[]{:S(2)}) collective-permute-start(bf16[512,256]{1,0:T(8,128)(2,1)S(1)} %get-tuple-element.109), channel_id=1, source_target_pairs={{0,8},{4,12},{8,0},{12,4},{16,24},{20,28},{24,16},{28,20},{1,9},{5... | collective-permute-start | bytes 786440 | tf_op jit(solution)/shard_map/ppermute | solution.py:349
  52.9 11.7 %collective-permute-start.15 = (bf16[512,256]{1,0:T(8,128)(2,1)S(1)}, bf16[512,256]{1,0:T(8,128)(2,1)S(1)}, u32[]{:S(2)}, u32[]{:S(2)}) collective-permute-start(bf16[512,256]{1,0:T(8,128)(2,1)S(1)} %get-tuple-element.110), channel_id=1, source_target_pairs={{0,16},{4,20},{8,24},{12,28},{16,0},{20,4},{24,8},{28,12},{1,17},{... | collective-permute-start | bytes 786440 | tf_op jit(solution)/shard_map/ppermute | solution.py:349
  54.5 11.7 %collective-permute-start.16 = (bf16[512,256]{1,0:T(8,128)(2,1)S(1)}, bf16[512,256]{1,0:T(8,128)(2,1)S(1)}, u32[]{:S(2)}, u32[]{:S(2)}) collective-permute-start(bf16[512,256]{1,0:T(8,128)(2,1)S(1)} %get-tuple-element.111), channel_id=1, source_target_pairs={{0,24},{4,28},{8,16},{12,20},{16,8},{20,12},{24,0},{28,4},{1,25},{... | collective-permute-start | bytes 786440 | tf_op jit(solution)/shard_map/ppermute | solution.py:349
  66.2 9.2 %collective-permute-start.17 = (bf16[256,512]{1,0:T(8,128)(2,1)S(1)}, bf16[256,512]{1,0:T(8,128)(2,1)S(1)}, u32[]{:S(2)}, u32[]{:S(2)}) collective-permute-start(bf16[256,512]{1,0:T(8,128)(2,1)S(1)} %get-tuple-element.113), channel_id=1, source_target_pairs={{0,16},{4,20},{8,24},{12,28},{16,0},{20,4},{24,8},{28,12},{1,17},{... | collective-permute-start | bytes 786440 | tf_op jit(solution)/shard_map/ppermute | solution.py:349
  67.1 10.5 %collective-permute-start.20 = (bf16[256,512]{1,0:T(8,128)(2,1)S(1)}, bf16[256,512]{1,0:T(8,128)(2,1)S(1)}, u32[]{:S(2)}, u32[]{:S(2)}) collective-permute-start(bf16[256,512]{1,0:T(8,128)(2,1)S(1)} %get-tuple-element.117), channel_id=1, source_target_pairs={{0,8},{4,12},{8,0},{12,4},{16,24},{20,28},{24,16},{28,20},{1,9},{5... | collective-permute-start | bytes 786440 | tf_op jit(solution)/shard_map/ppermute | solution.py:349
  68.9 12.1 %collective-permute-start.19 = (bf16[256,512]{1,0:T(8,128)(2,1)S(1)}, bf16[256,512]{1,0:T(8,128)(2,1)S(1)}, u32[]{:S(2)}, u32[]{:S(2)}) collective-permute-start(bf16[256,512]{1,0:T(8,128)(2,1)S(1)} %get-tuple-element.115), channel_id=1, source_target_pairs={{0,16},{4,20},{8,24},{12,28},{16,0},{20,4},{24,8},{28,12},{1,17},{... | collective-permute-start | bytes 786440 | tf_op jit(solution)/shard_map/ppermute | solution.py:349
  85.0 19.2 %collective-permute-start.24 = (bf16[256,1024]{1,0:T(8,128)(2,1)S(1)}, bf16[256,1024]{1,0:T(8,128)(2,1)S(1)}, u32[]{:S(2)}, u32[]{:S(2)}) collective-permute-start(bf16[256,1024]{1,0:T(8,128)(2,1)S(1)} %pad_maximum_fusion.3.own_ref.refs_0_.refs_4_), channel_id=1, source_target_pairs={{0,16},{4,20},{8,24},{12,28},{16,0},{20,4},{24,8},{28,12},{1,17},{... | collective-permute-start | bytes 1572872 | tf_op jit(solution)/shard_map/ppermute | solution.py:349
  86.1 18.0 %collective-permute-start.23 = (bf16[256,1024]{1,0:T(8,128)(2,1)S(1)}, bf16[256,1024]{1,0:T(8,128)(2,1)S(1)}, u32[]{:S(2)}, u32[]{:S(2)}) collective-permute-start(bf16[256,1024]{1,0:T(8,128)(2,1)S(1)} %pad_maximum_fusion.3.own_ref.refs_0_.refs_4_), channel_id=1, source_target_pairs={{0,8},{4,12},{8,0},{12,4},{16,24},{20,28},{24,16},{28,20},{1,9},{5... | collective-permute-start | bytes 1572872 | tf_op jit(solution)/shard_map/ppermute | solution.py:349
  87.7 18.4 %collective-permute-start.30 = (bf16[256,1024]{1,0:T(8,128)(2,1)}, bf16[256,1024]{1,0:T(8,128)(2,1)}, u32[]{:S(2)}, u32[]{:S(2)}) collective-permute-start(bf16[256,1024]{1,0:T(8,128)(2,1)} %get-tuple-element.129), channel_id=1, source_target_pairs={{0,4},{4,0},{8,12},{12,8},{16,20},{20,16},{24,28},{28,24},{1,5},{5... | collective-permute-start | bytes 1572872 | tf_op jit(solution)/shard_map/ppermute | solution.py:349
  91.3 23.7 %collective-permute-start.28 = (bf16[1024,128]{1,0:T(8,128)(2,1)S(1)}, bf16[1024,128]{1,0:T(8,128)(2,1)S(1)}, u32[]{:S(2)}, u32[]{:S(2)}) collective-permute-start(bf16[1024,128]{1,0:T(8,128)(2,1)S(1)} %shard_map.123), channel_id=1, source_target_pairs={{0,2},{1,3},{2,0},{3,1},{4,6},{5,7},{6,4},{7,5},{8,10},{9,11},{10,... | collective-permute-start | bytes 786440 | tf_op jit(solution)/shard_map/ppermute | solution.py:352
  100.5 14.5 %collective-permute-start.29 = (bf16[1024,128]{1,0:T(8,128)(2,1)S(1)}, bf16[1024,128]{1,0:T(8,128)(2,1)S(1)}, u32[]{:S(2)}, u32[]{:S(2)}) collective-permute-start(bf16[1024,128]{1,0:T(8,128)(2,1)S(1)} %shard_map.124), channel_id=1, source_target_pairs={{0,1},{1,2},{2,3},{3,0},{4,5},{5,6},{6,7},{7,4},{8,9},{9,10},{10,1... | collective-permute-start | bytes 786440 | tf_op jit(solution)/shard_map/ppermute | solution.py:352
  104.2 10.8 %collective-permute-start.27 = (bf16[256,512]{1,0:T(8,128)(2,1)S(1)}, bf16[256,512]{1,0:T(8,128)(2,1)S(1)}, u32[]{:S(2)}, u32[]{:S(2)}) collective-permute-start(bf16[256,512]{1,0:T(8,128)(2,1)S(1)} %slice.25), channel_id=1, source_target_pairs={{0,8},{4,12},{8,0},{12,4},{16,24},{20,28},{24,16},{28,20},{1,9},{5... | collective-permute-start | bytes 786440 | tf_op jit(solution)/shard_map/ppermute | solution.py:349
  105.2 9.8 %collective-permute-start.26 = (bf16[256,512]{1,0:T(8,128)(2,1)S(1)}, bf16[256,512]{1,0:T(8,128)(2,1)S(1)}, u32[]{:S(2)}, u32[]{:S(2)}) collective-permute-start(bf16[256,512]{1,0:T(8,128)(2,1)S(1)} %slice.24), channel_id=1, source_target_pairs={{0,16},{4,20},{8,24},{12,28},{16,0},{20,4},{24,8},{28,12},{1,17},{... | collective-permute-start | bytes 786440 | tf_op jit(solution)/shard_map/ppermute | solution.py:349
  (16 other events, 86.7 us)

commit v5 on v4

--- a/solution.py
+++ b/solution.py
@@ -217,50 +217,55 @@
     )(at, table, own, pair, *keys, *values)
 
 
-def back_kernel(r, chunks, at, own_ref, other_ref, kw_ref, vw_ref, out_ref, w_ref, turned_ref, sems):
-    depth, rows = out_ref.shape
+def back_kernel(places, chunks, at, own_ref, other_ref, kw_ref, vw_ref, *refs):
+    outs = refs[: len(places)]
+    w_ref, turned_ref, sems = refs[len(places) :]
+    depth, rows = outs[0].shape
     gw = own_ref.shape[1] // 2
     tile = min(TILE, depth)
     steps = depth // tile
-    first = lax.rem(at[1] + r, chunks) * depth
     copies = []
-    for n in range(steps):
-        for m, ref in enumerate((kw_ref, vw_ref)):
-            place = pl.ds(pl.multiple_of(first + n * tile, tile), tile)
-            copies.append(pltpu.make_async_copy(ref.at[place, :], w_ref.at[m, n], sems.at[m, n]))
-            copies[-1].start()
+    for c, r in enumerate(places):
+        first = lax.rem(at[1] + r, chunks) * depth
+        for n in range(steps):
+            for m, ref in enumerate((kw_ref, vw_ref)):
+                place = pl.ds(pl.multiple_of(first + n * tile, tile), tile)
+                step = c * steps + n
+                copies.append(pltpu.make_async_copy(ref.at[place, :], w_ref.at[m, step], sems.at[m, step]))
+                copies[-1].start()
     for n, ref in enumerate((own_ref, other_ref)):
         start = pl.multiple_of(((at[0] & 1) ^ n) * gw, gw)
         for m in range(2):
             turned_ref[m, pl.ds(start, gw), :] = ref[:, m * gw : (m + 1) * gw].astype(F32).T.astype(BF16)
-    for n in range(steps):
-        copies[2 * n].wait()
-        copies[2 * n + 1].wait()
-        total = mm(w_ref[0, n], turned_ref[0], NN) + mm(w_ref[1, n], turned_ref[1], NN)
-        out_ref[n * tile : (n + 1) * tile, :] = total.astype(BF16)
-
-
-def project_back(r, chunks, at, own, other, key_weight, value_weight):
+    for step in range(len(places) * steps):
+        copies[2 * step].wait()
+        copies[2 * step + 1].wait()
+        total = mm(w_ref[0, step], turned_ref[0], NN) + mm(w_ref[1, step], turned_ref[1], NN)
+        n = step % steps
+        outs[step // steps][n * tile : (n + 1) * tile, :] = total.astype(BF16)
+
+
+def project_back(places, chunks, at, own, other, key_weight, value_weight):
     rows, width = own.shape
     rows, gw = rows // 2, width // 2
     depth = key_weight.shape[0] // chunks
     tile = min(TILE, depth)
-    steps = depth // tile
+    steps = len(places) * (depth // tile)
     row_spec = pl.BlockSpec((rows, width), lambda n, at: (at[0] & 1, 0))
     return pl.pallas_call(
-        functools.partial(back_kernel, r, chunks),
+        functools.partial(back_kernel, places, chunks),
         grid_spec=pltpu.PrefetchScalarGridSpec(
             num_scalar_prefetch=1,
             grid=(1,),
             in_specs=[row_spec] * 2 + [pl.BlockSpec(memory_space=pltpu.HBM)] * 2,
-            out_specs=whole((depth, rows)),
+            out_specs=[whole((depth, rows))] * len(places),
             scratch_shapes=[
                 pltpu.VMEM((2, steps, tile, 2 * gw), BF16),
                 pltpu.VMEM((2, 2 * gw, rows), BF16),
                 pltpu.SemaphoreType.DMA((2, steps)),
             ],
         ),
-        out_shape=jax.ShapeDtypeStruct((depth, rows), BF16),
+        out_shape=[jax.ShapeDtypeStruct((depth, rows), BF16)] * len(places),
         compiler_params=params(48),
         cost_estimate=cost(8 * rows * gw * depth, 8 * gw * depth),
     )(at, own, other, key_weight, value_weight)
@@ -401,13 +406,15 @@
     cols = jnp.concatenate(cols, axis=1)
     own, cols = lax.optimization_barrier((own, cols))
     other = flip(own, 1)
-    middle = peers // 2
-    order = [middle] + [r for r in range(1, peers) if r != middle] + [0]
-    chunks = [project_back(r, peers, at, own, other, key_weight, value_weight) for r in order]
-    arrived = [shift(x, r) for x, r in zip(chunks[:-1], order)]
     owns = {0: own}
     for j in [*lows, *highs]:
         owns[j] = flip(own, 2 * j)
+    middle = peers // 2
+    rest = [r for r in range(1, peers) if r != middle]
+    chunks = list(project_back((middle,), peers, at, own, other, key_weight, value_weight))
+    arrived = [shift(chunks[0], middle)]
+    chunks += list(project_back((*rest, 0), peers, at, own, other, key_weight, value_weight))
+    arrived += [shift(x, r) for x, r in zip(chunks[1:-1], rest)]
     owns, _ = lax.optimization_barrier((owns, chunks[:-1]))
     for a in lows:
         for b in highs:

time: 126 us -> 126 us (level)
  waiting for transfers between devices: 40.6 us -> 44.3 us
  Pallas kernels: 33.8 us -> 30.2 us
    ppermute x6, waiting for transfers between devices: 6.6 us -> 10.2 us  [shift(): return lax.ppermute(x, 'mp', [(i, (i + r) % peers) for i in range(peers)])]
    pallas_call x4 -> x2, Pallas kernels: 14.4 us -> 10.8 us  [project_back(): pl.pallas_call(functools.partial(back_kernel, places, chunks), grid_spec=...]
  transfers between devices with their start and end apart: 37 -> 37, of which waited for: 19 -> 19; matrix products, arithmetic and copies ran while one was open for 5% -> 5% of each run, Pallas kernels for 24% -> 21%
where the time goes in v5:
time: 126 us; the launch traced here: 125 us
  waiting for transfers between devices  44.3 us (35%)
  starting transfers between devices  41.9 us (33%)
  Pallas kernels  30.2 us (24%)
  other arithmetic  4.06 us (3%)
  local copies, waits for them, and re-layouts  3.94 us (3%)
    ppermute x30, waiting for transfers between devices, flip(): return lax.ppermute(x, 'dp', [(i, i ^ r) for i in range(shards)])  31.7 us
    ppermute x30, starting transfers between devices, flip(): return lax.ppermute(x, 'dp', [(i, i ^ r) for i in range(shards)])  23.3 us
    ppermute x6, starting transfers between devices, shift(): return lax.ppermute(x, 'mp', [(i, (i + r) % peers) for i in range(peers)])  14.9 us
    pallas_call x2, Pallas kernels, project_back(): pl.pallas_call(functools.partial(back_kernel, places, chunks), grid_spec=...  10.8 us
    ppermute x6, waiting for transfers between devices, shift(): return lax.ppermute(x, 'mp', [(i, (i + r) % peers) for i in range(peers)])  10.2 us
    pallas_call x2, Pallas kernels, project(): pl.pallas_call(functools.partial(project_kernel, first, blocks, cuts, fin...  6.47 us
    pallas_call x1, Pallas kernels, attend(): pl.pallas_call(functools.partial(attend_kernel, chips, window), grid_spec...  6.44 us
    pallas_call x1, Pallas kernels, weight_grads(): pl.pallas_call(functools.partial(weight_grad_kernel, chips), grid_spec=pl...  5.46 us
  transfers between devices with their start and end apart: 37, of which 19 were waited for; matrix products, arithmetic and copies ran while one was open for 5% of the time, Pallas kernels for 21%

profile of v5, /device:TPU:0, one launch (start us, length us, event | category | flops | bytes accessed | tf_op | source)
XLA Modules:
  0.0 125.4 jit_solution(2048250107346654819)
XLA Ops:
  0.6 4.1 %collective-permute-start.3 = (bf16[128,1024]{1,0:T(8,128)(2,1)}, bf16[128,1024]{1,0:T(8,128)(2,1)S(1)}, u32[]{:S(2)}, u32[]{:S(2)}) collective-permute-start(bf16[128,1024]{1,0:T(8,128)(2,1)} %refs_0_.2), channel_id=1, source_target_pairs={{0,2},{1,3},{2,0},{3,1},{4,6},{5,7},{6,4},{7,5},{8,10},{9,11},{10,... | collective-permute-start | bytes 786440 | tf_op jit(solution)/shard_map/ppermute | solution.py:357
  6.3 2.2 %collective-permute-start.4 = (bf16[128,1024]{1,0:T(8,128)(2,1)}, bf16[128,1024]{1,0:T(8,128)(2,1)S(1)}, u32[]{:S(2)}, u32[]{:S(2)}) collective-permute-start(bf16[128,1024]{1,0:T(8,128)(2,1)} %refs_0_.2), channel_id=1, source_target_pairs={{0,3},{1,0},{2,1},{3,2},{4,7},{5,4},{6,5},{7,6},{8,11},{9,8},{10,9... | collective-permute-start | bytes 786440 | tf_op jit(solution)/shard_map/ppermute | solution.py:357
  9.9 3.7 %all-to-all-start = ((s32[8,1,24]{2,1,0:T(1,128)}), s32[8,1,24]{2,1,0:T(1,128)S(1)}, u32[]{:S(2)}, u32[]{:S(2)}) async-start(s32[8,1,24]{2,1,0:T(1,128)} %broadcast_in_dim.92), calls=%async_computation | async-start | bytes 8192 | tf_op jit(solution)/shard_map/all_to_all | solution.py:326
  15.8 2.4 %all-to-all-done = s32[8,1,24]{2,1,0:T(1,128)S(1)} async-done(((s32[8,1,24]{2,1,0:T(1,128)}), s32[8,1,24]{2,1,0:T(1,128)S(1)}, u32[]{:S(2)}, u32[]{:S(2)}) %all-to-all-start) | async-done | bytes 800 | tf_op jit(solution)/shard_map/all_to_all | solution.py:326
  18.9 2.5 %shard_map.119.refs_6_ = f32[256,1024]{1,0:T(8,128)S(1)} custom-call(s32[2]{0:T(128)S(1)} %pad_add_fusion.1.at, bf16[4096,1024]{1,0:T(8,128)(2,1)} %kw_ref.7, bf16[4096,1024]{1,0:T(8,128)(2,1)} %vw_ref.7, bf16[128,1024]{1,0:T(8,128)(2,1)S(1)} %copy-done, bf16[128,1024]{1,0:T(8,128)(2,1)S(1)} %collective-permute-done.refs_1_.refs_4_), custom_call_target="tpu_custom_call" | custom-call | flops 524288 | bytes 2048 | tf_op jit(solution)/shard_map/pallas_call | solution.py:81
  21.5 1.9 %collective-permute-done.3.refs_1_.refs_2_ = bf16[128,1024]{1,0:T(8,128)(2,1)S(1)} collective-permute-done((bf16[128,1024]{1,0:T(8,128)(2,1)}, bf16[128,1024]{1,0:T(8,128)(2,1)S(1)}, u32[]{:S(2)}, u32[]{:S(2)}) %collective-permute-start.3) | collective-permute-done | bytes 262176 | tf_op jit(solution)/shard_map/ppermute | solution.py:357
  23.4 1.9 %collective-permute-done.4.refs_2_.refs_3_ = bf16[128,1024]{1,0:T(8,128)(2,1)S(1)} collective-permute-done((bf16[128,1024]{1,0:T(8,128)(2,1)}, bf16[128,1024]{1,0:T(8,128)(2,1)S(1)}, u32[]{:S(2)}, u32[]{:S(2)}) %collective-permute-start.4) | collective-permute-done | bytes 262176 | tf_op jit(solution)/shard_map/ppermute | solution.py:357
  27.6 3.9 %shard_map.120 = (bf16[256,512]{1,0:T(8,128)(2,1)S(1)}, bf16[256,512]{1,0:T(8,128)(2,1)S(1)}) custom-call(s32[2]{0:T(128)S(1)} %pad_add_fusion.1.at, bf16[4096,1024]{1,0:T(8,128)(2,1)} %kw_ref.7, bf16[4096,1024]{1,0:T(8,128)(2,1)} %vw_ref.7, bf16[128,1024]{1,0:T(8,128)(2,1)S(1)} %collective-permute-done.2.refs_0_.refs_1_, ...), custom_call_target="tpu_custom_call" | custom-call | flops 1572864 | bytes 6144 | tf_op jit(solution)/shard_map/pallas_call | solution.py:81
  31.5 1.6 %collective-permute-start.8 = (bf16[256,512]{1,0:T(8,128)(2,1)S(1)}, bf16[256,512]{1,0:T(8,128)(2,1)S(1)}, u32[]{:S(2)}, u32[]{:S(2)}) collective-permute-start(bf16[256,512]{1,0:T(8,128)(2,1)S(1)} %get-tuple-element.94.refs_0_), channel_id=1, source_target_pairs={{0,8},{4,12},{8,0},{12,4},{16,24},{20,28},{24,16},{28,20},{1,9},{5... | collective-permute-start | bytes 786440 | tf_op jit(solution)/shard_map/ppermute | solution.py:354
  35.7 5.1 %collective-permute-done.8.refs_1_ = bf16[256,512]{1,0:T(8,128)(2,1)S(1)} collective-permute-done((bf16[256,512]{1,0:T(8,128)(2,1)S(1)}, bf16[256,512]{1,0:T(8,128)(2,1)S(1)}, u32[]{:S(2)}, u32[]{:S(2)}) %collective-permute-start.8) | collective-permute-done | bytes 262176 | tf_op jit(solution)/shard_map/ppermute | solution.py:354
  44.8 3.1 %collective-permute-done.9.refs_2_ = bf16[256,512]{1,0:T(8,128)(2,1)S(1)} collective-permute-done((bf16[256,512]{1,0:T(8,128)(2,1)S(1)}, bf16[256,512]{1,0:T(8,128)(2,1)S(1)}, u32[]{:S(2)}, u32[]{:S(2)}) %collective-permute-start.9) | collective-permute-done | bytes 262176 | tf_op jit(solution)/shard_map/ppermute | solution.py:354
  48.0 4.5 %collective-permute-done.10.refs_3_ = bf16[256,512]{1,0:T(8,128)(2,1)S(1)} collective-permute-done((bf16[256,512]{1,0:T(8,128)(2,1)S(1)}, bf16[256,512]{1,0:T(8,128)(2,1)S(1)}, u32[]{:S(2)}, u32[]{:S(2)}) %collective-permute-start.10) | collective-permute-done | bytes 262176 | tf_op jit(solution)/shard_map/ppermute | solution.py:354
  55.9 6.4 %shard_map.122 = (bf16[256,512]{1,0:T(8,128)(2,1)S(1)}, bf16[256,512]{1,0:T(8,128)(2,1)S(1)}, bf16[256,1024]{1,0:T(8,128)(2,1)}, bf16[256,512]{1,0:T(8,128)(2,1)...) custom-call(s32[2]{0:T(128)S(1)} %pad_add_fusion.1.at, ...), custom_call_target="tpu_custom_call" | custom-call | flops 1966080 | bytes 4608 | tf_op jit(solution)/shard_map/pallas_call | solution.py:201
  62.4 2.3 %collective-permute-done.15 = bf16[512,256]{1,0:T(8,128)(2,1)S(1)} collective-permute-done((bf16[512,256]{1,0:T(8,128)(2,1)S(1)}, bf16[512,256]{1,0:T(8,128)(2,1)S(1)}, u32[]{:S(2)}, u32[]{:S(2)}) %collective-permute-start.15) | collective-permute-done | bytes 262176 | tf_op jit(solution)/shard_map/ppermute | solution.py:354
  67.1 1.8 %collective-permute-start.20 = (bf16[256,512]{1,0:T(8,128)(2,1)S(1)}, bf16[256,512]{1,0:T(8,128)(2,1)S(1)}, u32[]{:S(2)}, u32[]{:S(2)}) collective-permute-start(bf16[256,512]{1,0:T(8,128)(2,1)S(1)} %get-tuple-element.120), channel_id=1, source_target_pairs={{0,8},{4,12},{8,0},{12,4},{16,24},{20,28},{24,16},{28,20},{1,9},{5... | collective-permute-start | bytes 786440 | tf_op jit(solution)/shard_map/ppermute | solution.py:354
  69.0 6.4 %collective-permute-done.17 = bf16[256,512]{1,0:T(8,128)(2,1)S(1)} collective-permute-done((bf16[256,512]{1,0:T(8,128)(2,1)S(1)}, bf16[256,512]{1,0:T(8,128)(2,1)S(1)}, u32[]{:S(2)}, u32[]{:S(2)}) %collective-permute-start.17) | collective-permute-done | bytes 262176 | tf_op jit(solution)/shard_map/ppermute | solution.py:354
  78.8 2.1 %collective-permute-done.19 = bf16[256,512]{1,0:T(8,128)(2,1)S(1)} collective-permute-done((bf16[256,512]{1,0:T(8,128)(2,1)S(1)}, bf16[256,512]{1,0:T(8,128)(2,1)S(1)}, u32[]{:S(2)}, u32[]{:S(2)}) %collective-permute-start.19) | collective-permute-done | bytes 262176 | tf_op jit(solution)/shard_map/ppermute | solution.py:354
  82.0 2.7 %collective-permute-done.22 = bf16[256,512]{1,0:T(8,128)(2,1)S(1)} collective-permute-done((bf16[256,512]{1,0:T(8,128)(2,1)S(1)}, bf16[256,512]{1,0:T(8,128)(2,1)S(1)}, u32[]{:S(2)}, u32[]{:S(2)}) %collective-permute-start.22) | collective-permute-done | bytes 262176 | tf_op jit(solution)/shard_map/ppermute | solution.py:354
  86.1 1.6 %collective-permute-start.23 = (bf16[256,1024]{1,0:T(8,128)(2,1)S(1)}, bf16[256,1024]{1,0:T(8,128)(2,1)S(1)}, u32[]{:S(2)}, u32[]{:S(2)}) collective-permute-start(bf16[256,1024]{1,0:T(8,128)(2,1)S(1)} %pad_maximum_fusion.3.own_ref.refs_0_.refs_4_), channel_id=1, source_target_pairs={{0,8},{4,12},{8,0},{12,4},{16,24},{20,28},{24,16},{28,20},{1,9},{5... | collective-permute-start | bytes 1572872 | tf_op jit(solution)/shard_map/ppermute | solution.py:354
  87.7 3.6 %shard_map.123 = bf16[1024,128]{1,0:T(8,128)(2,1)S(1)} custom-call(s32[2]{0:T(128)S(1)} %pad_add_fusion.1.at, bf16[256,1024]{1,0:T(8,128)(2,1)S(1)} %pad_maximum_fusion.3.own_ref.refs_0_.refs_4_, bf16[256,1024]{1,0:T(8,128)(2,1)S(1)} %collective-permute-done.25.other_ref.refs_8_.refs_12_, bf16[4096,1024]{1,0:T(8,128)(2,1)} %kw_ref.7, bf16[4096,1024]{1,0:T(8,128)(2,1)} %vw_ref.7), custom_call_target="tpu_custom_call" | custom-call | flops 524288 | bytes 4096 | tf_op jit(solution)/shard_map/pallas_call | solution.py:255
  91.3 5.5 %collective-permute-start.28 = (bf16[1024,128]{1,0:T(8,128)(2,1)S(1)}, bf16[1024,128]{1,0:T(8,128)(2,1)S(1)}, u32[]{:S(2)}, u32[]{:S(2)}) collective-permute-start(bf16[1024,128]{1,0:T(8,128)(2,1)S(1)} %shard_map.123), channel_id=1, source_target_pairs={{0,2},{1,3},{2,0},{3,1},{4,6},{5,7},{6,4},{7,5},{8,10},{9,11},{10,... | collective-permute-start | bytes 786440 | tf_op jit(solution)/shard_map/ppermute | solution.py:357
  96.8 7.3 %shard_map.124 = (bf16[1024,128]{1,0:T(8,128)(2,1)S(1)}, bf16[1024,128]{1,0:T(8,128)(2,1)S(1)}, bf16[1024,128]{1,0:T(8,128)(2,1)S(1)}) custom-call(s32[2]{0:T(128)S(1)} %pad_add_fusion.1.at, bf16[256,1024]{1,0:T(8,128)(2,1)S(1)} %pad_maximum_fusion.3.own_ref.refs_0_.refs_4_, bf16[256,1024]{1,0:T(8,128)(2,1)S(1)} %collective-permute-done.25.other_ref.refs_8_.refs_12_, ...), custom_call_target="tpu_custom_call" | custom-call | flops 524288 | bytes 4096 | tf_op jit(solution)/shard_map/pallas_call | solution.py:255
  109.0 5.9 %collective-permute-done.28 = bf16[1024,128]{1,0:T(8,128)(2,1)S(1)} collective-permute-done((bf16[1024,128]{1,0:T(8,128)(2,1)S(1)}, bf16[1024,128]{1,0:T(8,128)(2,1)S(1)}, u32[]{:S(2)}, u32[]{:S(2)}) %collective-permute-start.28) | collective-permute-done | bytes 262176 | tf_op jit(solution)/shard_map/ppermute | solution.py:357
  118.5 5.5 %shard_map.125 = (f32[512,1024]{1,0:T(8,128)}, f32[512,1024]{1,0:T(8,128)}) custom-call(s32[2]{0:T(128)S(1)} %pad_add_fusion.1.at, bf16[512,1024]{1,0:T(8,128)(2,1)S(1)} %pad_maximum_fusion.col_ref, bf16[256,1024]{1,0:T(8,128)(2,1)S(1)} %pad_maximum_fusion.3.own_ref.refs_0_.refs_4_, bf16[256,1024]{1,0:T(8,128)(2,1)S(1)} %collective-permute-done.23.refs_1_.refs_5_, ...), custom_call_target="tpu_custom_call" | custom-call | flops 2097152 | bytes 9216 | tf_op jit(solution)/shard_map/pallas_call | solution.py:308
  (91 shorter events, 36.3 us)
Async XLA Ops:
  0.6 22.7 %collective-permute-start.3 = (bf16[128,1024]{1,0:T(8,128)(2,1)}, bf16[128,1024]{1,0:T(8,128)(2,1)S(1)}, u32[]{:S(2)}, u32[]{:S(2)}) collective-permute-start(bf16[128,1024]{1,0:T(8,128)(2,1)} %refs_0_.2), channel_id=1, source_target_pairs={{0,2},{1,3},{2,0},{3,1},{4,6},{5,7},{6,4},{7,5},{8,10},{9,11},{10,... | collective-permute-start | bytes 786440 | tf_op jit(solution)/shard_map/ppermute | solution.py:357
  4.7 18.6 %collective-permute-start.2 = (bf16[128,1024]{1,0:T(8,128)(2,1)}, bf16[128,1024]{1,0:T(8,128)(2,1)S(1)}, u32[]{:S(2)}, u32[]{:S(2)}) collective-permute-start(bf16[128,1024]{1,0:T(8,128)(2,1)} %refs_0_.2), channel_id=1, source_target_pairs={{0,1},{1,2},{2,3},{3,0},{4,5},{5,6},{6,7},{7,4},{8,9},{9,10},{10,1... | collective-permute-start | bytes 786440 | tf_op jit(solution)/shard_map/ppermute | solution.py:357
  6.3 12.6 %collective-permute-start = (bf16[128,1024]{1,0:T(8,128)(2,1)}, bf16[128,1024]{1,0:T(8,128)(2,1)S(1)}, u32[]{:S(2)}, u32[]{:S(2)}) collective-permute-start(bf16[128,1024]{1,0:T(8,128)(2,1)} %refs_0_.2), channel_id=1, source_target_pairs={{0,4},{4,0},{8,12},{12,8},{16,20},{20,16},{24,28},{28,24},{1,5},{5... | collective-permute-start | bytes 786440 | tf_op jit(solution)/shard_map/ppermute | solution.py:354
  6.3 19.0 %collective-permute-start.4 = (bf16[128,1024]{1,0:T(8,128)(2,1)}, bf16[128,1024]{1,0:T(8,128)(2,1)S(1)}, u32[]{:S(2)}, u32[]{:S(2)}) collective-permute-start(bf16[128,1024]{1,0:T(8,128)(2,1)} %refs_0_.2), channel_id=1, source_target_pairs={{0,3},{1,0},{2,1},{3,2},{4,7},{5,4},{6,5},{7,6},{8,11},{9,8},{10,9... | collective-permute-start | bytes 786440 | tf_op jit(solution)/shard_map/ppermute | solution.py:357
  15.0 10.3 %collective-permute-start.1 = (bf16[256,1024]{1,0:T(8,128)(2,1)S(1)}, bf16[256,1024]{1,0:T(8,128)(2,1)S(1)}, u32[]{:S(2)}, u32[]{:S(2)}) collective-permute-start(bf16[256,1024]{1,0:T(8,128)(2,1)S(1)} %pad_maximum_fusion.2), channel_id=1, source_target_pairs={{0,4},{4,0},{8,12},{12,8},{16,20},{20,16},{24,28},{28,24},{1,5},{5... | collective-permute-start | bytes 1572872 | tf_op jit(solution)/shard_map/ppermute | solution.py:354
  31.5 9.2 %collective-permute-start.8 = (bf16[256,512]{1,0:T(8,128)(2,1)S(1)}, bf16[256,512]{1,0:T(8,128)(2,1)S(1)}, u32[]{:S(2)}, u32[]{:S(2)}) collective-permute-start(bf16[256,512]{1,0:T(8,128)(2,1)S(1)} %get-tuple-element.94.refs_0_), channel_id=1, source_target_pairs={{0,8},{4,12},{8,0},{12,4},{16,24},{20,28},{24,16},{28,20},{1,9},{5... | collective-permute-start | bytes 786440 | tf_op jit(solution)/shard_map/ppermute | solution.py:354
  33.1 9.2 %collective-permute-start.12 = (bf16[256,512]{1,0:T(8,128)(2,1)S(1)}, bf16[256,512]{1,0:T(8,128)(2,1)S(1)}, u32[]{:S(2)}, u32[]{:S(2)}) collective-permute-start(bf16[256,512]{1,0:T(8,128)(2,1)S(1)} %get-tuple-element.98.refs_4_), channel_id=1, source_target_pairs={{0,16},{4,20},{8,24},{12,28},{16,0},{20,4},{24,8},{28,12},{1,17},{... | collective-permute-start | bytes 786440 | tf_op jit(solution)/shard_map/ppermute | solution.py:354
  34.7 13.3 %collective-permute-start.9 = (bf16[256,512]{1,0:T(8,128)(2,1)S(1)}, bf16[256,512]{1,0:T(8,128)(2,1)S(1)}, u32[]{:S(2)}, u32[]{:S(2)}) collective-permute-start(bf16[256,512]{1,0:T(8,128)(2,1)S(1)} %get-tuple-element.94.refs_0_), channel_id=1, source_target_pairs={{0,16},{4,20},{8,24},{12,28},{16,0},{20,4},{24,8},{28,12},{1,17},{... | collective-permute-start | bytes 786440 | tf_op jit(solution)/shard_map/ppermute | solution.py:354
  35.2 12.8 %collective-permute-start.11 = (bf16[256,512]{1,0:T(8,128)(2,1)S(1)}, bf16[256,512]{1,0:T(8,128)(2,1)S(1)}, u32[]{:S(2)}, u32[]{:S(2)}) collective-permute-start(bf16[256,512]{1,0:T(8,128)(2,1)S(1)} %get-tuple-element.98.refs_4_), channel_id=1, source_target_pairs={{0,8},{4,12},{8,0},{12,4},{16,24},{20,28},{24,16},{28,20},{1,9},{5... | collective-permute-start | bytes 786440 | tf_op jit(solution)/shard_map/ppermute | solution.py:354
  40.8 11.7 %collective-permute-start.10 = (bf16[256,512]{1,0:T(8,128)(2,1)S(1)}, bf16[256,512]{1,0:T(8,128)(2,1)S(1)}, u32[]{:S(2)}, u32[]{:S(2)}) collective-permute-start(bf16[256,512]{1,0:T(8,128)(2,1)S(1)} %collective-permute-done.8.refs_1_), channel_id=1, source_target_pairs={{0,16},{4,20},{8,24},{12,28},{16,0},{20,4},{24,8},{28,12},{1,17},{... | collective-permute-start | bytes 786440 | tf_op jit(solution)/shard_map/ppermute | solution.py:354
  42.3 10.1 %collective-permute-start.13 = (bf16[256,512]{1,0:T(8,128)(2,1)S(1)}, bf16[256,512]{1,0:T(8,128)(2,1)S(1)}, u32[]{:S(2)}, u32[]{:S(2)}) collective-permute-start(bf16[256,512]{1,0:T(8,128)(2,1)S(1)} %collective-permute-done.12.refs_6_), channel_id=1, source_target_pairs={{0,8},{4,12},{8,0},{12,4},{16,24},{20,28},{24,16},{28,20},{1,9},{5... | collective-permute-start | bytes 786440 | tf_op jit(solution)/shard_map/ppermute | solution.py:354
  52.4 9.9 %collective-permute-start.14 = (bf16[512,256]{1,0:T(8,128)(2,1)S(1)}, bf16[512,256]{1,0:T(8,128)(2,1)S(1)}, u32[]{:S(2)}, u32[]{:S(2)}) collective-permute-start(bf16[512,256]{1,0:T(8,128)(2,1)S(1)} %get-tuple-element.112), channel_id=1, source_target_pairs={{0,8},{4,12},{8,0},{12,4},{16,24},{20,28},{24,16},{28,20},{1,9},{5... | collective-permute-start | bytes 786440 | tf_op jit(solution)/shard_map/ppermute | solution.py:354
  52.9 11.7 %collective-permute-start.15 = (bf16[512,256]{1,0:T(8,128)(2,1)S(1)}, bf16[512,256]{1,0:T(8,128)(2,1)S(1)}, u32[]{:S(2)}, u32[]{:S(2)}) collective-permute-start(bf16[512,256]{1,0:T(8,128)(2,1)S(1)} %get-tuple-element.113), channel_id=1, source_target_pairs={{0,16},{4,20},{8,24},{12,28},{16,0},{20,4},{24,8},{28,12},{1,17},{... | collective-permute-start | bytes 786440 | tf_op jit(solution)/shard_map/ppermute | solution.py:354
  54.5 11.7 %collective-permute-start.16 = (bf16[512,256]{1,0:T(8,128)(2,1)S(1)}, bf16[512,256]{1,0:T(8,128)(2,1)S(1)}, u32[]{:S(2)}, u32[]{:S(2)}) collective-permute-start(bf16[512,256]{1,0:T(8,128)(2,1)S(1)} %get-tuple-element.114), channel_id=1, source_target_pairs={{0,24},{4,28},{8,16},{12,20},{16,8},{20,12},{24,0},{28,4},{1,25},{... | collective-permute-start | bytes 786440 | tf_op jit(solution)/shard_map/ppermute | solution.py:354
  66.2 9.2 %collective-permute-start.17 = (bf16[256,512]{1,0:T(8,128)(2,1)S(1)}, bf16[256,512]{1,0:T(8,128)(2,1)S(1)}, u32[]{:S(2)}, u32[]{:S(2)}) collective-permute-start(bf16[256,512]{1,0:T(8,128)(2,1)S(1)} %get-tuple-element.116), channel_id=1, source_target_pairs={{0,16},{4,20},{8,24},{12,28},{16,0},{20,4},{24,8},{28,12},{1,17},{... | collective-permute-start | bytes 786440 | tf_op jit(solution)/shard_map/ppermute | solution.py:354
  67.1 10.5 %collective-permute-start.20 = (bf16[256,512]{1,0:T(8,128)(2,1)S(1)}, bf16[256,512]{1,0:T(8,128)(2,1)S(1)}, u32[]{:S(2)}, u32[]{:S(2)}) collective-permute-start(bf16[256,512]{1,0:T(8,128)(2,1)S(1)} %get-tuple-element.120), channel_id=1, source_target_pairs={{0,8},{4,12},{8,0},{12,4},{16,24},{20,28},{24,16},{28,20},{1,9},{5... | collective-permute-start | bytes 786440 | tf_op jit(solution)/shard_map/ppermute | solution.py:354
  68.9 12.1 %collective-permute-start.19 = (bf16[256,512]{1,0:T(8,128)(2,1)S(1)}, bf16[256,512]{1,0:T(8,128)(2,1)S(1)}, u32[]{:S(2)}, u32[]{:S(2)}) collective-permute-start(bf16[256,512]{1,0:T(8,128)(2,1)S(1)} %get-tuple-element.118), channel_id=1, source_target_pairs={{0,16},{4,20},{8,24},{12,28},{16,0},{20,4},{24,8},{28,12},{1,17},{... | collective-permute-start | bytes 786440 | tf_op jit(solution)/shard_map/ppermute | solution.py:354
  85.0 19.1 %collective-permute-start.24 = (bf16[256,1024]{1,0:T(8,128)(2,1)S(1)}, bf16[256,1024]{1,0:T(8,128)(2,1)S(1)}, u32[]{:S(2)}, u32[]{:S(2)}) collective-permute-start(bf16[256,1024]{1,0:T(8,128)(2,1)S(1)} %pad_maximum_fusion.3.own_ref.refs_0_.refs_4_), channel_id=1, source_target_pairs={{0,16},{4,20},{8,24},{12,28},{16,0},{20,4},{24,8},{28,12},{1,17},{... | collective-permute-start | bytes 1572872 | tf_op jit(solution)/shard_map/ppermute | solution.py:354
  86.1 18.0 %collective-permute-start.23 = (bf16[256,1024]{1,0:T(8,128)(2,1)S(1)}, bf16[256,1024]{1,0:T(8,128)(2,1)S(1)}, u32[]{:S(2)}, u32[]{:S(2)}) collective-permute-start(bf16[256,1024]{1,0:T(8,128)(2,1)S(1)} %pad_maximum_fusion.3.own_ref.refs_0_.refs_4_), channel_id=1, source_target_pairs={{0,8},{4,12},{8,0},{12,4},{16,24},{20,28},{24,16},{28,20},{1,9},{5... | collective-permute-start | bytes 1572872 | tf_op jit(solution)/shard_map/ppermute | solution.py:354
  87.7 18.4 %collective-permute-start.30 = (bf16[256,1024]{1,0:T(8,128)(2,1)}, bf16[256,1024]{1,0:T(8,128)(2,1)}, u32[]{:S(2)}, u32[]{:S(2)}) collective-permute-start(bf16[256,1024]{1,0:T(8,128)(2,1)} %get-tuple-element.135), channel_id=1, source_target_pairs={{0,4},{4,0},{8,12},{12,8},{16,20},{20,16},{24,28},{28,24},{1,5},{5... | collective-permute-start | bytes 1572872 | tf_op jit(solution)/shard_map/ppermute | solution.py:354
  91.3 23.7 %collective-permute-start.28 = (bf16[1024,128]{1,0:T(8,128)(2,1)S(1)}, bf16[1024,128]{1,0:T(8,128)(2,1)S(1)}, u32[]{:S(2)}, u32[]{:S(2)}) collective-permute-start(bf16[1024,128]{1,0:T(8,128)(2,1)S(1)} %shard_map.123), channel_id=1, source_target_pairs={{0,2},{1,3},{2,0},{3,1},{4,6},{5,7},{6,4},{7,5},{8,10},{9,11},{10,... | collective-permute-start | bytes 786440 | tf_op jit(solution)/shard_map/ppermute | solution.py:357
  104.1 10.9 %collective-permute-start.29 = (bf16[1024,128]{1,0:T(8,128)(2,1)S(1)}, bf16[1024,128]{1,0:T(8,128)(2,1)S(1)}, u32[]{:S(2)}, u32[]{:S(2)}) collective-permute-start(bf16[1024,128]{1,0:T(8,128)(2,1)S(1)} %get-tuple-element.128), channel_id=1, source_target_pairs={{0,1},{1,2},{2,3},{3,0},{4,5},{5,6},{6,7},{7,4},{8,9},{9,10},{10,1... | collective-permute-start | bytes 786440 | tf_op jit(solution)/shard_map/ppermute | solution.py:357
  104.2 10.8 %collective-permute-start.27 = (bf16[256,512]{1,0:T(8,128)(2,1)S(1)}, bf16[256,512]{1,0:T(8,128)(2,1)S(1)}, u32[]{:S(2)}, u32[]{:S(2)}) collective-permute-start(bf16[256,512]{1,0:T(8,128)(2,1)S(1)} %slice.25), channel_id=1, source_target_pairs={{0,8},{4,12},{8,0},{12,4},{16,24},{20,28},{24,16},{28,20},{1,9},{5... | collective-permute-start | bytes 786440 | tf_op jit(solution)/shard_map/ppermute | solution.py:354
  105.1 9.8 %collective-permute-start.26 = (bf16[256,512]{1,0:T(8,128)(2,1)S(1)}, bf16[256,512]{1,0:T(8,128)(2,1)S(1)}, u32[]{:S(2)}, u32[]{:S(2)}) collective-permute-start(bf16[256,512]{1,0:T(8,128)(2,1)S(1)} %slice.24), channel_id=1, source_target_pairs={{0,16},{4,20},{8,24},{12,28},{16,0},{20,4},{24,8},{28,12},{1,17},{... | collective-permute-start | bytes 786440 | tf_op jit(solution)/shard_map/ppermute | solution.py:354
  (16 other events, 86.8 us)

commit v6 on v5

--- a/solution.py
+++ b/solution.py
@@ -394,8 +394,11 @@
     keys, values = project(1, at, key_weight, value_weight, owns[1:], partners[1:], sums)
     keys, values = spread(keys, True), spread(values, False)
     cols = split_columns(chips, at, owns, partners)
+    near = [*lows, *highs]
+    far = [a + b for a in lows for b in highs]
     keys, values, cols = lax.optimization_barrier((keys, values, list(cols)))
-    cols = [cols[0]] + [flip(cols[j], 2 * j) for j in range(1, chips)]
+    far_cols = [cols[j] for j in far]
+    cols = [cols[0]] + [flip(cols[j], 2 * j) for j in near]
     attended, query_grad, back, *parts = attend(window, at, table, mine, pair, keys, values)
     parts, back, cols = lax.optimization_barrier((parts, back, cols))
     own = jnp.concatenate([collect(parts[:chips], False), collect(parts[chips:], True)], axis=1)
@@ -403,7 +406,6 @@
     outs = []
     for here, rest in ((attended, back[:, :gw]), (query_grad, back[:, gw:])):
         outs.append(jnp.where(core == 0, jnp.concatenate([here, rest], 1), jnp.concatenate([rest, here], 1)))
-    cols = jnp.concatenate(cols, axis=1)
     own, cols = lax.optimization_barrier((own, cols))
     other = flip(own, 1)
     owns = {0: own}
@@ -415,12 +417,15 @@
     arrived = [shift(chunks[0], middle)]
     chunks += list(project_back((*rest, 0), peers, at, own, other, key_weight, value_weight))
     arrived += [shift(x, r) for x, r in zip(chunks[1:-1], rest)]
-    owns, _ = lax.optimization_barrier((owns, chunks[:-1]))
+    owns, far_cols, _ = lax.optimization_barrier((owns, far_cols, chunks[:-1]))
+    far_cols = [flip(x, 2 * j) for x, j in zip(far_cols, far)]
     for a in lows:
         for b in highs:
             owns[a + b] = (flip(owns[a][:, :gw], 2 * b), flip(owns[b][:, gw:], 2 * a))
     owns = [owns[j] for j in range(chips)]
-    owns, arrived[:2], chunk, outs = lax.optimization_barrier((owns, arrived[:2], chunks[-1], outs))
+    owns, arrived[:2], far_cols, chunk, outs = lax.optimization_barrier((owns, arrived[:2], far_cols, chunks[-1], outs))
+    held = {j: x for j, x in zip([0] + near + far, cols + far_cols)}
+    cols = jnp.concatenate([held[j] for j in range(chips)], axis=1)
     others = [other] + [tuple(flip(y, 1) for y in x) if isinstance(x, tuple) else flip(x, 1) for x in owns[1:]]
     weight_out = weight_grads(at, cols, owns, others)
     arrived, weight_out = lax.optimization_barrier((arrived, weight_out))

time: 126 us -> 125 us (level)
  waiting for transfers between devices: 44.3 us -> 40.3 us
  starting transfers between devices: 41.9 us -> 44.4 us
    ppermute x6, starting transfers between devices: 14.9 us -> 16.9 us  [shift(): return lax.ppermute(x, 'mp', [(i, (i + r) % peers) for i in range(peers)])]
    ppermute x6, waiting for transfers between devices: 10.2 us -> 8.15 us  [shift(): return lax.ppermute(x, 'mp', [(i, (i + r) % peers) for i in range(peers)])]
  transfers between devices with their start and end apart: 37 -> 37, of which waited for: 19 -> 16; matrix products, arithmetic and copies ran while one was open for 5% -> 6% of each run, Pallas kernels for 21% -> 21%
where the time goes in v6:
time: 125 us
  starting transfers between devices  44.4 us (36%)
  waiting for transfers between devices  40.3 us (32%)
  Pallas kernels  30.3 us (24%)
  other arithmetic  4.85 us (4%)
  local copies, waits for them, and re-layouts  3.95 us (3%)
    ppermute x30, waiting for transfers between devices, flip(): return lax.ppermute(x, 'dp', [(i, i ^ r) for i in range(shards)])  30.5 us
    ppermute x30, starting transfers between devices, flip(): return lax.ppermute(x, 'dp', [(i, i ^ r) for i in range(shards)])  23.7 us
    ppermute x6, starting transfers between devices, shift(): return lax.ppermute(x, 'mp', [(i, (i + r) % peers) for i in range(peers)])  16.9 us
    pallas_call x2, Pallas kernels, project_back(): pl.pallas_call(functools.partial(back_kernel, places, chunks), grid_spec=...  10.8 us
    ppermute x6, waiting for transfers between devices, shift(): return lax.ppermute(x, 'mp', [(i, (i + r) % peers) for i in range(peers)])  8.15 us
    pallas_call x2, Pallas kernels, project(): pl.pallas_call(functools.partial(project_kernel, first, blocks, cuts, fin...  6.47 us
    pallas_call x1, Pallas kernels, attend(): pl.pallas_call(functools.partial(attend_kernel, chips, window), grid_spec...  6.46 us
    pallas_call x1, Pallas kernels, weight_grads(): pl.pallas_call(functools.partial(weight_grad_kernel, chips), grid_spec=pl...  5.5 us
  transfers between devices with their start and end apart: 37, of which 16 were waited for; matrix products, arithmetic and copies ran while one was open for 6% of the time, Pallas kernels for 21%

profile of v6, /device:TPU:0, one launch (start us, length us, event | category | flops | bytes accessed | tf_op | source)
XLA Modules:
  0.0 124.7 jit_solution(3209100290976858951)
XLA Ops:
  0.6 4.1 %collective-permute-start.3 = (bf16[128,1024]{1,0:T(8,128)(2,1)}, bf16[128,1024]{1,0:T(8,128)(2,1)S(1)}, u32[]{:S(2)}, u32[]{:S(2)}) collective-permute-start(bf16[128,1024]{1,0:T(8,128)(2,1)} %refs_0_.2), channel_id=1, source_target_pairs={{0,2},{1,3},{2,0},{3,1},{4,6},{5,7},{6,4},{7,5},{8,10},{9,11},{10,... | collective-permute-start | bytes 786440 | tf_op jit(solution)/shard_map/ppermute | solution.py:357
  6.3 2.2 %collective-permute-start.4 = (bf16[128,1024]{1,0:T(8,128)(2,1)}, bf16[128,1024]{1,0:T(8,128)(2,1)S(1)}, u32[]{:S(2)}, u32[]{:S(2)}) collective-permute-start(bf16[128,1024]{1,0:T(8,128)(2,1)} %refs_0_.2), channel_id=1, source_target_pairs={{0,3},{1,0},{2,1},{3,2},{4,7},{5,4},{6,5},{7,6},{8,11},{9,8},{10,9... | collective-permute-start | bytes 786440 | tf_op jit(solution)/shard_map/ppermute | solution.py:357
  9.9 3.7 %all-to-all-start = ((s32[8,1,24]{2,1,0:T(1,128)}), s32[8,1,24]{2,1,0:T(1,128)S(1)}, u32[]{:S(2)}, u32[]{:S(2)}) async-start(s32[8,1,24]{2,1,0:T(1,128)} %broadcast_in_dim.92), calls=%async_computation | async-start | bytes 8192 | tf_op jit(solution)/shard_map/all_to_all | solution.py:326
  16.5 1.7 %all-to-all-done = s32[8,1,24]{2,1,0:T(1,128)S(1)} async-done(((s32[8,1,24]{2,1,0:T(1,128)}), s32[8,1,24]{2,1,0:T(1,128)S(1)}, u32[]{:S(2)}, u32[]{:S(2)}) %all-to-all-start) | async-done | bytes 800 | tf_op jit(solution)/shard_map/all_to_all | solution.py:326
  18.9 2.5 %shard_map.119.refs_6_ = f32[256,1024]{1,0:T(8,128)S(1)} custom-call(s32[2]{0:T(128)S(1)} %pad_add_fusion.1.at, bf16[4096,1024]{1,0:T(8,128)(2,1)} %kw_ref.7, bf16[4096,1024]{1,0:T(8,128)(2,1)} %vw_ref.7, bf16[128,1024]{1,0:T(8,128)(2,1)S(1)} %copy-done, bf16[128,1024]{1,0:T(8,128)(2,1)S(1)} %collective-permute-done.refs_1_.refs_4_), custom_call_target="tpu_custom_call" | custom-call | flops 524288 | bytes 2048 | tf_op jit(solution)/shard_map/pallas_call | solution.py:81
  21.5 1.9 %collective-permute-done.3.refs_1_.refs_2_ = bf16[128,1024]{1,0:T(8,128)(2,1)S(1)} collective-permute-done((bf16[128,1024]{1,0:T(8,128)(2,1)}, bf16[128,1024]{1,0:T(8,128)(2,1)S(1)}, u32[]{:S(2)}, u32[]{:S(2)}) %collective-permute-start.3) | collective-permute-done | bytes 262176 | tf_op jit(solution)/shard_map/ppermute | solution.py:357
  23.4 1.9 %collective-permute-done.4.refs_2_.refs_3_ = bf16[128,1024]{1,0:T(8,128)(2,1)S(1)} collective-permute-done((bf16[128,1024]{1,0:T(8,128)(2,1)}, bf16[128,1024]{1,0:T(8,128)(2,1)S(1)}, u32[]{:S(2)}, u32[]{:S(2)}) %collective-permute-start.4) | collective-permute-done | bytes 262176 | tf_op jit(solution)/shard_map/ppermute | solution.py:357
  27.6 3.9 %shard_map.120 = (bf16[256,512]{1,0:T(8,128)(2,1)S(1)}, bf16[256,512]{1,0:T(8,128)(2,1)S(1)}) custom-call(s32[2]{0:T(128)S(1)} %pad_add_fusion.1.at, bf16[4096,1024]{1,0:T(8,128)(2,1)} %kw_ref.7, bf16[4096,1024]{1,0:T(8,128)(2,1)} %vw_ref.7, bf16[128,1024]{1,0:T(8,128)(2,1)S(1)} %collective-permute-done.2.refs_0_.refs_1_, ...), custom_call_target="tpu_custom_call" | custom-call | flops 1572864 | bytes 6144 | tf_op jit(solution)/shard_map/pallas_call | solution.py:81
  31.5 1.6 %collective-permute-start.8 = (bf16[256,512]{1,0:T(8,128)(2,1)S(1)}, bf16[256,512]{1,0:T(8,128)(2,1)S(1)}, u32[]{:S(2)}, u32[]{:S(2)}) collective-permute-start(bf16[256,512]{1,0:T(8,128)(2,1)S(1)} %get-tuple-element.97.refs_0_), channel_id=1, source_target_pairs={{0,8},{4,12},{8,0},{12,4},{16,24},{20,28},{24,16},{28,20},{1,9},{5... | collective-permute-start | bytes 786440 | tf_op jit(solution)/shard_map/ppermute | solution.py:354
  35.7 5.1 %collective-permute-done.8.refs_1_ = bf16[256,512]{1,0:T(8,128)(2,1)S(1)} collective-permute-done((bf16[256,512]{1,0:T(8,128)(2,1)S(1)}, bf16[256,512]{1,0:T(8,128)(2,1)S(1)}, u32[]{:S(2)}, u32[]{:S(2)}) %collective-permute-start.8) | collective-permute-done | bytes 262176 | tf_op jit(solution)/shard_map/ppermute | solution.py:354
  44.8 3.1 %collective-permute-done.9.refs_2_ = bf16[256,512]{1,0:T(8,128)(2,1)S(1)} collective-permute-done((bf16[256,512]{1,0:T(8,128)(2,1)S(1)}, bf16[256,512]{1,0:T(8,128)(2,1)S(1)}, u32[]{:S(2)}, u32[]{:S(2)}) %collective-permute-start.9) | collective-permute-done | bytes 262176 | tf_op jit(solution)/shard_map/ppermute | solution.py:354
  48.0 4.5 %collective-permute-done.10.refs_3_ = bf16[256,512]{1,0:T(8,128)(2,1)S(1)} collective-permute-done((bf16[256,512]{1,0:T(8,128)(2,1)S(1)}, bf16[256,512]{1,0:T(8,128)(2,1)S(1)}, u32[]{:S(2)}, u32[]{:S(2)}) %collective-permute-start.10) | collective-permute-done | bytes 262176 | tf_op jit(solution)/shard_map/ppermute | solution.py:354
  54.5 6.5 %shard_map.122 = (bf16[256,512]{1,0:T(8,128)(2,1)S(1)}, bf16[256,512]{1,0:T(8,128)(2,1)S(1)}, bf16[256,1024]{1,0:T(8,128)(2,1)}, bf16[256,512]{1,0:T(8,128)(2,1)...) custom-call(s32[2]{0:T(128)S(1)} %pad_add_fusion.1.at, ...), custom_call_target="tpu_custom_call" | custom-call | flops 1966080 | bytes 4608 | tf_op jit(solution)/shard_map/pallas_call | solution.py:201
  64.6 5.7 %collective-permute-done.16 = bf16[256,512]{1,0:T(8,128)(2,1)S(1)} collective-permute-done((bf16[256,512]{1,0:T(8,128)(2,1)S(1)}, bf16[256,512]{1,0:T(8,128)(2,1)S(1)}, u32[]{:S(2)}, u32[]{:S(2)}) %collective-permute-start.16) | collective-permute-done | bytes 262176 | tf_op jit(solution)/shard_map/ppermute | solution.py:354
  73.1 2.9 %collective-permute-done.18 = bf16[256,512]{1,0:T(8,128)(2,1)S(1)} collective-permute-done((bf16[256,512]{1,0:T(8,128)(2,1)S(1)}, bf16[256,512]{1,0:T(8,128)(2,1)S(1)}, u32[]{:S(2)}, u32[]{:S(2)}) %collective-permute-start.18) | collective-permute-done | bytes 262176 | tf_op jit(solution)/shard_map/ppermute | solution.py:354
  76.8 2.8 %collective-permute-done.21 = bf16[256,512]{1,0:T(8,128)(2,1)S(1)} collective-permute-done((bf16[256,512]{1,0:T(8,128)(2,1)S(1)}, bf16[256,512]{1,0:T(8,128)(2,1)S(1)}, u32[]{:S(2)}, u32[]{:S(2)}) %collective-permute-start.21) | collective-permute-done | bytes 262176 | tf_op jit(solution)/shard_map/ppermute | solution.py:354
  82.5 3.6 %shard_map.123 = bf16[1024,128]{1,0:T(8,128)(2,1)S(1)} custom-call(s32[2]{0:T(128)S(1)} %pad_add_fusion.1.at, bf16[256,1024]{1,0:T(8,128)(2,1)S(1)} %pad_maximum_fusion.3.own_ref.refs_0_.refs_4_, bf16[256,1024]{1,0:T(8,128)(2,1)S(1)} %collective-permute-done.24.other_ref.refs_8_.refs_12_, bf16[4096,1024]{1,0:T(8,128)(2,1)} %kw_ref.7, bf16[4096,1024]{1,0:T(8,128)(2,1)} %vw_ref.7), custom_call_target="tpu_custom_call" | custom-call | flops 524288 | bytes 4096 | tf_op jit(solution)/shard_map/pallas_call | solution.py:255
  86.0 5.4 %collective-permute-start.27 = (bf16[1024,128]{1,0:T(8,128)(2,1)S(1)}, bf16[1024,128]{1,0:T(8,128)(2,1)S(1)}, u32[]{:S(2)}, u32[]{:S(2)}) collective-permute-start(bf16[1024,128]{1,0:T(8,128)(2,1)S(1)} %shard_map.123), channel_id=1, source_target_pairs={{0,2},{1,3},{2,0},{3,1},{4,6},{5,7},{6,4},{7,5},{8,10},{9,11},{10,... | collective-permute-start | bytes 786440 | tf_op jit(solution)/shard_map/ppermute | solution.py:357
  91.5 7.3 %shard_map.124 = (bf16[1024,128]{1,0:T(8,128)(2,1)S(1)}, bf16[1024,128]{1,0:T(8,128)(2,1)S(1)}, bf16[1024,128]{1,0:T(8,128)(2,1)S(1)}) custom-call(s32[2]{0:T(128)S(1)} %pad_add_fusion.1.at, bf16[256,1024]{1,0:T(8,128)(2,1)S(1)} %pad_maximum_fusion.3.own_ref.refs_0_.refs_4_, bf16[256,1024]{1,0:T(8,128)(2,1)S(1)} %collective-permute-done.24.other_ref.refs_8_.refs_12_, ...), custom_call_target="tpu_custom_call" | custom-call | flops 524288 | bytes 4096 | tf_op jit(solution)/shard_map/pallas_call | solution.py:255
  100.8 1.7 %collective-permute-start.29 = (bf16[512,256]{1,0:T(8,128)(2,1)S(1)}, bf16[512,256]{1,0:T(8,128)(2,1)S(1)}, u32[]{:S(2)}, u32[]{:S(2)}) collective-permute-start(bf16[512,256]{1,0:T(8,128)(2,1)S(1)} %get-tuple-element.135), channel_id=1, source_target_pairs={{0,24},{4,28},{8,16},{12,20},{16,8},{20,12},{24,0},{28,4},{1,25},{... | collective-permute-start | bytes 786440 | tf_op jit(solution)/shard_map/ppermute | solution.py:354
  105.4 4.3 %collective-permute-done.27 = bf16[1024,128]{1,0:T(8,128)(2,1)S(1)} collective-permute-done((bf16[1024,128]{1,0:T(8,128)(2,1)S(1)}, bf16[1024,128]{1,0:T(8,128)(2,1)S(1)}, u32[]{:S(2)}, u32[]{:S(2)}) %collective-permute-start.27) | collective-permute-done | bytes 262176 | tf_op jit(solution)/shard_map/ppermute | solution.py:357
  109.7 3.7 %collective-permute-done.29 = bf16[512,256]{1,0:T(8,128)(2,1)S(1)} collective-permute-done((bf16[512,256]{1,0:T(8,128)(2,1)S(1)}, bf16[512,256]{1,0:T(8,128)(2,1)S(1)}, u32[]{:S(2)}, u32[]{:S(2)}) %collective-permute-start.29) | collective-permute-done | bytes 262176 | tf_op jit(solution)/shard_map/ppermute | solution.py:354
  114.5 3.5 %collective-permute-start.31 = (bf16[1024,128]{1,0:T(8,128)(2,1)S(1)}, bf16[1024,128]{1,0:T(8,128)(2,1)S(1)}, u32[]{:S(2)}, u32[]{:S(2)}) collective-permute-start(bf16[1024,128]{1,0:T(8,128)(2,1)S(1)} %get-tuple-element.131), channel_id=1, source_target_pairs={{0,3},{1,0},{2,1},{3,2},{4,7},{5,4},{6,5},{7,6},{8,11},{9,8},{10,9... | collective-permute-start | bytes 786440 | tf_op jit(solution)/shard_map/ppermute | solution.py:357
  118.2 5.5 %shard_map.125 = (f32[512,1024]{1,0:T(8,128)}, f32[512,1024]{1,0:T(8,128)}) custom-call(s32[2]{0:T(128)S(1)} %pad_add_fusion.1.at, bf16[512,1024]{1,0:T(8,128)(2,1)S(1)} %pad_maximum_fusion.col_ref, bf16[256,1024]{1,0:T(8,128)(2,1)S(1)} %pad_maximum_fusion.3.own_ref.refs_0_.refs_4_, bf16[256,1024]{1,0:T(8,128)(2,1)S(1)} %collective-permute-done.22.refs_1_.refs_5_, ...), custom_call_target="tpu_custom_call" | custom-call | flops 2097152 | bytes 9216 | tf_op jit(solution)/shard_map/pallas_call | solution.py:308
  (95 shorter events, 34.7 us)
Async XLA Ops:
  0.6 22.7 %collective-permute-start.3 = (bf16[128,1024]{1,0:T(8,128)(2,1)}, bf16[128,1024]{1,0:T(8,128)(2,1)S(1)}, u32[]{:S(2)}, u32[]{:S(2)}) collective-permute-start(bf16[128,1024]{1,0:T(8,128)(2,1)} %refs_0_.2), channel_id=1, source_target_pairs={{0,2},{1,3},{2,0},{3,1},{4,6},{5,7},{6,4},{7,5},{8,10},{9,11},{10,... | collective-permute-start | bytes 786440 | tf_op jit(solution)/shard_map/ppermute | solution.py:357
  4.7 18.6 %collective-permute-start.2 = (bf16[128,1024]{1,0:T(8,128)(2,1)}, bf16[128,1024]{1,0:T(8,128)(2,1)S(1)}, u32[]{:S(2)}, u32[]{:S(2)}) collective-permute-start(bf16[128,1024]{1,0:T(8,128)(2,1)} %refs_0_.2), channel_id=1, source_target_pairs={{0,1},{1,2},{2,3},{3,0},{4,5},{5,6},{6,7},{7,4},{8,9},{9,10},{10,1... | collective-permute-start | bytes 786440 | tf_op jit(solution)/shard_map/ppermute | solution.py:357
  6.3 12.6 %collective-permute-start = (bf16[128,1024]{1,0:T(8,128)(2,1)}, bf16[128,1024]{1,0:T(8,128)(2,1)S(1)}, u32[]{:S(2)}, u32[]{:S(2)}) collective-permute-start(bf16[128,1024]{1,0:T(8,128)(2,1)} %refs_0_.2), channel_id=1, source_target_pairs={{0,4},{4,0},{8,12},{12,8},{16,20},{20,16},{24,28},{28,24},{1,5},{5... | collective-permute-start | bytes 786440 | tf_op jit(solution)/shard_map/ppermute | solution.py:354
  6.3 19.0 %collective-permute-start.4 = (bf16[128,1024]{1,0:T(8,128)(2,1)}, bf16[128,1024]{1,0:T(8,128)(2,1)S(1)}, u32[]{:S(2)}, u32[]{:S(2)}) collective-permute-start(bf16[128,1024]{1,0:T(8,128)(2,1)} %refs_0_.2), channel_id=1, source_target_pairs={{0,3},{1,0},{2,1},{3,2},{4,7},{5,4},{6,5},{7,6},{8,11},{9,8},{10,9... | collective-permute-start | bytes 786440 | tf_op jit(solution)/shard_map/ppermute | solution.py:357
  15.8 9.5 %collective-permute-start.1 = (bf16[256,1024]{1,0:T(8,128)(2,1)}, bf16[256,1024]{1,0:T(8,128)(2,1)S(1)}, u32[]{:S(2)}, u32[]{:S(2)}) collective-permute-start(bf16[256,1024]{1,0:T(8,128)(2,1)} %pad_maximum_fusion.2), channel_id=1, source_target_pairs={{0,4},{4,0},{8,12},{12,8},{16,20},{20,16},{24,28},{28,24},{1,5},{5... | collective-permute-start | bytes 1572872 | tf_op jit(solution)/shard_map/ppermute | solution.py:354
  31.5 9.2 %collective-permute-start.8 = (bf16[256,512]{1,0:T(8,128)(2,1)S(1)}, bf16[256,512]{1,0:T(8,128)(2,1)S(1)}, u32[]{:S(2)}, u32[]{:S(2)}) collective-permute-start(bf16[256,512]{1,0:T(8,128)(2,1)S(1)} %get-tuple-element.97.refs_0_), channel_id=1, source_target_pairs={{0,8},{4,12},{8,0},{12,4},{16,24},{20,28},{24,16},{28,20},{1,9},{5... | collective-permute-start | bytes 786440 | tf_op jit(solution)/shard_map/ppermute | solution.py:354
  33.1 9.2 %collective-permute-start.12 = (bf16[256,512]{1,0:T(8,128)(2,1)S(1)}, bf16[256,512]{1,0:T(8,128)(2,1)S(1)}, u32[]{:S(2)}, u32[]{:S(2)}) collective-permute-start(bf16[256,512]{1,0:T(8,128)(2,1)S(1)} %get-tuple-element.101.refs_4_), channel_id=1, source_target_pairs={{0,16},{4,20},{8,24},{12,28},{16,0},{20,4},{24,8},{28,12},{1,17},{... | collective-permute-start | bytes 786440 | tf_op jit(solution)/shard_map/ppermute | solution.py:354
  34.7 13.3 %collective-permute-start.9 = (bf16[256,512]{1,0:T(8,128)(2,1)S(1)}, bf16[256,512]{1,0:T(8,128)(2,1)S(1)}, u32[]{:S(2)}, u32[]{:S(2)}) collective-permute-start(bf16[256,512]{1,0:T(8,128)(2,1)S(1)} %get-tuple-element.97.refs_0_), channel_id=1, source_target_pairs={{0,16},{4,20},{8,24},{12,28},{16,0},{20,4},{24,8},{28,12},{1,17},{... | collective-permute-start | bytes 786440 | tf_op jit(solution)/shard_map/ppermute | solution.py:354
  35.2 12.8 %collective-permute-start.11 = (bf16[256,512]{1,0:T(8,128)(2,1)S(1)}, bf16[256,512]{1,0:T(8,128)(2,1)S(1)}, u32[]{:S(2)}, u32[]{:S(2)}) collective-permute-start(bf16[256,512]{1,0:T(8,128)(2,1)S(1)} %get-tuple-element.101.refs_4_), channel_id=1, source_target_pairs={{0,8},{4,12},{8,0},{12,4},{16,24},{20,28},{24,16},{28,20},{1,9},{5... | collective-permute-start | bytes 786440 | tf_op jit(solution)/shard_map/ppermute | solution.py:354
  40.8 11.7 %collective-permute-start.10 = (bf16[256,512]{1,0:T(8,128)(2,1)S(1)}, bf16[256,512]{1,0:T(8,128)(2,1)S(1)}, u32[]{:S(2)}, u32[]{:S(2)}) collective-permute-start(bf16[256,512]{1,0:T(8,128)(2,1)S(1)} %collective-permute-done.8.refs_1_), channel_id=1, source_target_pairs={{0,16},{4,20},{8,24},{12,28},{16,0},{20,4},{24,8},{28,12},{1,17},{... | collective-permute-start | bytes 786440 | tf_op jit(solution)/shard_map/ppermute | solution.py:354
  42.3 10.1 %collective-permute-start.13 = (bf16[256,512]{1,0:T(8,128)(2,1)S(1)}, bf16[256,512]{1,0:T(8,128)(2,1)S(1)}, u32[]{:S(2)}, u32[]{:S(2)}) collective-permute-start(bf16[256,512]{1,0:T(8,128)(2,1)S(1)} %collective-permute-done.12.refs_6_), channel_id=1, source_target_pairs={{0,8},{4,12},{8,0},{12,4},{16,24},{20,28},{24,16},{28,20},{1,9},{5... | collective-permute-start | bytes 786440 | tf_op jit(solution)/shard_map/ppermute | solution.py:354
  52.4 8.5 %collective-permute-start.14 = (bf16[512,256]{1,0:T(8,128)(2,1)S(1)}, bf16[512,256]{1,0:T(8,128)(2,1)S(1)}, u32[]{:S(2)}, u32[]{:S(2)}) collective-permute-start(bf16[512,256]{1,0:T(8,128)(2,1)S(1)} %get-tuple-element.115), channel_id=1, source_target_pairs={{0,8},{4,12},{8,0},{12,4},{16,24},{20,28},{24,16},{28,20},{1,9},{5... | collective-permute-start | bytes 786440 | tf_op jit(solution)/shard_map/ppermute | solution.py:354
  61.0 9.3 %collective-permute-start.16 = (bf16[256,512]{1,0:T(8,128)(2,1)S(1)}, bf16[256,512]{1,0:T(8,128)(2,1)S(1)}, u32[]{:S(2)}, u32[]{:S(2)}) collective-permute-start(bf16[256,512]{1,0:T(8,128)(2,1)S(1)} %get-tuple-element.118), channel_id=1, source_target_pairs={{0,16},{4,20},{8,24},{12,28},{16,0},{20,4},{24,8},{28,12},{1,17},{... | collective-permute-start | bytes 786440 | tf_op jit(solution)/shard_map/ppermute | solution.py:354
  61.5 11.0 %collective-permute-start.19 = (bf16[256,512]{1,0:T(8,128)(2,1)S(1)}, bf16[256,512]{1,0:T(8,128)(2,1)S(1)}, u32[]{:S(2)}, u32[]{:S(2)}) collective-permute-start(bf16[256,512]{1,0:T(8,128)(2,1)S(1)} %get-tuple-element.122), channel_id=1, source_target_pairs={{0,8},{4,12},{8,0},{12,4},{16,24},{20,28},{24,16},{28,20},{1,9},{5... | collective-permute-start | bytes 786440 | tf_op jit(solution)/shard_map/ppermute | solution.py:354
  63.1 12.9 %collective-permute-start.18 = (bf16[256,512]{1,0:T(8,128)(2,1)S(1)}, bf16[256,512]{1,0:T(8,128)(2,1)S(1)}, u32[]{:S(2)}, u32[]{:S(2)}) collective-permute-start(bf16[256,512]{1,0:T(8,128)(2,1)S(1)} %get-tuple-element.120), channel_id=1, source_target_pairs={{0,16},{4,20},{8,24},{12,28},{16,0},{20,4},{24,8},{28,12},{1,17},{... | collective-permute-start | bytes 786440 | tf_op jit(solution)/shard_map/ppermute | solution.py:354
  79.8 19.0 %collective-permute-start.23 = (bf16[256,1024]{1,0:T(8,128)(2,1)S(1)}, bf16[256,1024]{1,0:T(8,128)(2,1)S(1)}, u32[]{:S(2)}, u32[]{:S(2)}) collective-permute-start(bf16[256,1024]{1,0:T(8,128)(2,1)S(1)} %pad_maximum_fusion.3.own_ref.refs_0_.refs_4_), channel_id=1, source_target_pairs={{0,16},{4,20},{8,24},{12,28},{16,0},{20,4},{24,8},{28,12},{1,17},{... | collective-permute-start | bytes 1572872 | tf_op jit(solution)/shard_map/ppermute | solution.py:354
  81.0 17.8 %collective-permute-start.22 = (bf16[256,1024]{1,0:T(8,128)(2,1)S(1)}, bf16[256,1024]{1,0:T(8,128)(2,1)S(1)}, u32[]{:S(2)}, u32[]{:S(2)}) collective-permute-start(bf16[256,1024]{1,0:T(8,128)(2,1)S(1)} %pad_maximum_fusion.3.own_ref.refs_0_.refs_4_), channel_id=1, source_target_pairs={{0,8},{4,12},{8,0},{12,4},{16,24},{20,28},{24,16},{28,20},{1,9},{5... | collective-permute-start | bytes 1572872 | tf_op jit(solution)/shard_map/ppermute | solution.py:354
  82.5 18.4 %collective-permute-start.30 = (bf16[256,1024]{1,0:T(8,128)(2,1)}, bf16[256,1024]{1,0:T(8,128)(2,1)}, u32[]{:S(2)}, u32[]{:S(2)}) collective-permute-start(bf16[256,1024]{1,0:T(8,128)(2,1)} %get-tuple-element.138), channel_id=1, source_target_pairs={{0,4},{4,0},{8,12},{12,8},{16,20},{20,16},{24,28},{28,24},{1,5},{5... | collective-permute-start | bytes 1572872 | tf_op jit(solution)/shard_map/ppermute | solution.py:354
  86.0 23.7 %collective-permute-start.27 = (bf16[1024,128]{1,0:T(8,128)(2,1)S(1)}, bf16[1024,128]{1,0:T(8,128)(2,1)S(1)}, u32[]{:S(2)}, u32[]{:S(2)}) collective-permute-start(bf16[1024,128]{1,0:T(8,128)(2,1)S(1)} %shard_map.123), channel_id=1, source_target_pairs={{0,2},{1,3},{2,0},{3,1},{4,6},{5,7},{6,4},{7,5},{8,10},{9,11},{10,... | collective-permute-start | bytes 786440 | tf_op jit(solution)/shard_map/ppermute | solution.py:357
  98.7 14.7 %collective-permute-start.28 = (bf16[1024,128]{1,0:T(8,128)(2,1)S(1)}, bf16[1024,128]{1,0:T(8,128)(2,1)S(1)}, u32[]{:S(2)}, u32[]{:S(2)}) collective-permute-start(bf16[1024,128]{1,0:T(8,128)(2,1)S(1)} %get-tuple-element.130), channel_id=1, source_target_pairs={{0,1},{1,2},{2,3},{3,0},{4,5},{5,6},{6,7},{7,4},{8,9},{9,10},{10,1... | collective-permute-start | bytes 786440 | tf_op jit(solution)/shard_map/ppermute | solution.py:357
  98.9 10.8 %collective-permute-start.26 = (bf16[256,512]{1,0:T(8,128)(2,1)S(1)}, bf16[256,512]{1,0:T(8,128)(2,1)S(1)}, u32[]{:S(2)}, u32[]{:S(2)}) collective-permute-start(bf16[256,512]{1,0:T(8,128)(2,1)S(1)} %slice.25), channel_id=1, source_target_pairs={{0,8},{4,12},{8,0},{12,4},{16,24},{20,28},{24,16},{28,20},{1,9},{5... | collective-permute-start | bytes 786440 | tf_op jit(solution)/shard_map/ppermute | solution.py:354
  99.7 10.0 %collective-permute-start.25 = (bf16[256,512]{1,0:T(8,128)(2,1)S(1)}, bf16[256,512]{1,0:T(8,128)(2,1)S(1)}, u32[]{:S(2)}, u32[]{:S(2)}) collective-permute-start(bf16[256,512]{1,0:T(8,128)(2,1)S(1)} %slice.24), channel_id=1, source_target_pairs={{0,16},{4,20},{8,24},{12,28},{16,0},{20,4},{24,8},{28,12},{1,17},{... | collective-permute-start | bytes 786440 | tf_op jit(solution)/shard_map/ppermute | solution.py:354
  100.8 12.6 %collective-permute-start.29 = (bf16[512,256]{1,0:T(8,128)(2,1)S(1)}, bf16[512,256]{1,0:T(8,128)(2,1)S(1)}, u32[]{:S(2)}, u32[]{:S(2)}) collective-permute-start(bf16[512,256]{1,0:T(8,128)(2,1)S(1)} %get-tuple-element.135), channel_id=1, source_target_pairs={{0,24},{4,28},{8,16},{12,20},{16,8},{20,12},{24,0},{28,4},{1,25},{... | collective-permute-start | bytes 786440 | tf_op jit(solution)/shard_map/ppermute | solution.py:354
  114.5 9.2 %collective-permute-start.31 = (bf16[1024,128]{1,0:T(8,128)(2,1)S(1)}, bf16[1024,128]{1,0:T(8,128)(2,1)S(1)}, u32[]{:S(2)}, u32[]{:S(2)}) collective-permute-start(bf16[1024,128]{1,0:T(8,128)(2,1)S(1)} %get-tuple-element.131), channel_id=1, source_target_pairs={{0,3},{1,0},{2,1},{3,2},{4,7},{5,4},{6,5},{7,6},{8,11},{9,8},{10,9... | collective-permute-start | bytes 786440 | tf_op jit(solution)/shard_map/ppermute | solution.py:357
  (18 other events, 144.3 us)

commit v7 on v6

--- a/solution.py
+++ b/solution.py
@@ -406,7 +406,8 @@
     outs = []
     for here, rest in ((attended, back[:, :gw]), (query_grad, back[:, gw:])):
         outs.append(jnp.where(core == 0, jnp.concatenate([here, rest], 1), jnp.concatenate([rest, here], 1)))
-    own, cols = lax.optimization_barrier((own, cols))
+    own, cols, far_cols = lax.optimization_barrier((own, cols, far_cols))
+    far_cols = [flip(x, 2 * j) for x, j in zip(far_cols, far)]
     other = flip(own, 1)
     owns = {0: own}
     for j in [*lows, *highs]:
@@ -418,12 +419,11 @@
     chunks += list(project_back((*rest, 0), peers, at, own, other, key_weight, value_weight))
     arrived += [shift(x, r) for x, r in zip(chunks[1:-1], rest)]
     owns, far_cols, _ = lax.optimization_barrier((owns, far_cols, chunks[:-1]))
-    far_cols = [flip(x, 2 * j) for x, j in zip(far_cols, far)]
     for a in lows:
         for b in highs:
             owns[a + b] = (flip(owns[a][:, :gw], 2 * b), flip(owns[b][:, gw:], 2 * a))
     owns = [owns[j] for j in range(chips)]
-    owns, arrived[:2], far_cols, chunk, outs = lax.optimization_barrier((owns, arrived[:2], far_cols, chunks[-1], outs))
+    owns, arrived[:2], chunk, outs = lax.optimization_barrier((owns, arrived[:2], chunks[-1], outs))
     held = {j: x for j, x in zip([0] + near + far, cols + far_cols)}
     cols = jnp.concatenate([held[j] for j in range(chips)], axis=1)
     others = [other] + [tuple(flip(y, 1) for y in x) if isinstance(x, tuple) else flip(x, 1) for x in owns[1:]]

time: 125 us -> 124 us (level)
  waiting for transfers between devices: 40.3 us -> 38.4 us
    ppermute x6, waiting for transfers between devices: 8.15 us -> 4.8 us  [shift(): return lax.ppermute(x, 'mp', [(i, (i + r) % peers) for i in range(peers)])]
    ppermute x30, waiting for transfers between devices: 30.5 us -> 31.9 us  [flip(): return lax.ppermute(x, 'dp', [(i, i ^ r) for i in range(shards)])]
  transfers between devices with their start and end apart: 37 -> 37, of which waited for: 16 -> 19; matrix products, arithmetic and copies ran while one was open for 6% -> 7% of each run, Pallas kernels for 21% -> 21%
where the time goes in v7:
time: 124 us
  starting transfers between devices  44.8 us (36%)
  waiting for transfers between devices  38.4 us (31%)
  Pallas kernels  30.3 us (24%)
  other arithmetic  5.81 us (5%)
  local copies, waits for them, and re-layouts  3.95 us (3%)
    ppermute x30, waiting for transfers between devices, flip(): return lax.ppermute(x, 'dp', [(i, i ^ r) for i in range(shards)])  31.9 us
    ppermute x30, starting transfers between devices, flip(): return lax.ppermute(x, 'dp', [(i, i ^ r) for i in range(shards)])  23.7 us
    ppermute x6, starting transfers between devices, shift(): return lax.ppermute(x, 'mp', [(i, (i + r) % peers) for i in range(peers)])  17.4 us
    pallas_call x2, Pallas kernels, project_back(): pl.pallas_call(functools.partial(back_kernel, places, chunks), grid_spec=...  10.8 us
    pallas_call x2, Pallas kernels, project(): pl.pallas_call(functools.partial(project_kernel, first, blocks, cuts, fin...  6.47 us
    pallas_call x1, Pallas kernels, attend(): pl.pallas_call(functools.partial(attend_kernel, chips, window), grid_spec...  6.46 us
    pallas_call x1, Pallas kernels, weight_grads(): pl.pallas_call(functools.partial(weight_grad_kernel, chips), grid_spec=pl...  5.48 us
    ppermute x6, waiting for transfers between devices, shift(): return lax.ppermute(x, 'mp', [(i, (i + r) % peers) for i in range(peers)])  4.8 us
  transfers between devices with their start and end apart: 37, of which 19 were waited for; matrix products, arithmetic and copies ran while one was open for 7% of the time, Pallas kernels for 21%

profile of v7, /device:TPU:0, one launch (start us, length us, event | category | flops | bytes accessed | tf_op | source)
XLA Modules:
  0.0 124.1 jit_solution(16976717335535106141)
XLA Ops:
  0.6 4.1 %collective-permute-start.3 = (bf16[128,1024]{1,0:T(8,128)(2,1)}, bf16[128,1024]{1,0:T(8,128)(2,1)S(1)}, u32[]{:S(2)}, u32[]{:S(2)}) collective-permute-start(bf16[128,1024]{1,0:T(8,128)(2,1)} %refs_0_.2), channel_id=1, source_target_pairs={{0,2},{1,3},{2,0},{3,1},{4,6},{5,7},{6,4},{7,5},{8,10},{9,11},{10,... | collective-permute-start | bytes 786440 | tf_op jit(solution)/shard_map/ppermute | solution.py:357
  4.7 1.6 %collective-permute-start.2 = (bf16[128,1024]{1,0:T(8,128)(2,1)}, bf16[128,1024]{1,0:T(8,128)(2,1)S(1)}, u32[]{:S(2)}, u32[]{:S(2)}) collective-permute-start(bf16[128,1024]{1,0:T(8,128)(2,1)} %refs_0_.2), channel_id=1, source_target_pairs={{0,1},{1,2},{2,3},{3,0},{4,5},{5,6},{6,7},{7,4},{8,9},{9,10},{10,1... | collective-permute-start | bytes 786440 | tf_op jit(solution)/shard_map/ppermute | solution.py:357
  6.3 2.2 %collective-permute-start.4 = (bf16[128,1024]{1,0:T(8,128)(2,1)}, bf16[128,1024]{1,0:T(8,128)(2,1)S(1)}, u32[]{:S(2)}, u32[]{:S(2)}) collective-permute-start(bf16[128,1024]{1,0:T(8,128)(2,1)} %refs_0_.2), channel_id=1, source_target_pairs={{0,3},{1,0},{2,1},{3,2},{4,7},{5,4},{6,5},{7,6},{8,11},{9,8},{10,9... | collective-permute-start | bytes 786440 | tf_op jit(solution)/shard_map/ppermute | solution.py:357
  9.9 3.7 %all-to-all-start = ((s32[8,1,24]{2,1,0:T(1,128)}), s32[8,1,24]{2,1,0:T(1,128)S(1)}, u32[]{:S(2)}, u32[]{:S(2)}) async-start(s32[8,1,24]{2,1,0:T(1,128)} %broadcast_in_dim.92), calls=%async_computation | async-start | bytes 8192 | tf_op jit(solution)/shard_map/all_to_all | solution.py:326
  16.5 1.7 %all-to-all-done = s32[8,1,24]{2,1,0:T(1,128)S(1)} async-done(((s32[8,1,24]{2,1,0:T(1,128)}), s32[8,1,24]{2,1,0:T(1,128)S(1)}, u32[]{:S(2)}, u32[]{:S(2)}) %all-to-all-start) | async-done | bytes 800 | tf_op jit(solution)/shard_map/all_to_all | solution.py:326
  18.9 2.5 %shard_map.119.refs_6_ = f32[256,1024]{1,0:T(8,128)S(1)} custom-call(s32[2]{0:T(128)S(1)} %pad_add_fusion.1.at, bf16[4096,1024]{1,0:T(8,128)(2,1)} %kw_ref.7, bf16[4096,1024]{1,0:T(8,128)(2,1)} %vw_ref.7, bf16[128,1024]{1,0:T(8,128)(2,1)S(1)} %copy-done, bf16[128,1024]{1,0:T(8,128)(2,1)S(1)} %collective-permute-done.refs_1_.refs_4_), custom_call_target="tpu_custom_call" | custom-call | flops 524288 | bytes 2048 | tf_op jit(solution)/shard_map/pallas_call | solution.py:81
  21.5 1.9 %collective-permute-done.3.refs_1_.refs_2_ = bf16[128,1024]{1,0:T(8,128)(2,1)S(1)} collective-permute-done((bf16[128,1024]{1,0:T(8,128)(2,1)}, bf16[128,1024]{1,0:T(8,128)(2,1)S(1)}, u32[]{:S(2)}, u32[]{:S(2)}) %collective-permute-start.3) | collective-permute-done | bytes 262176 | tf_op jit(solution)/shard_map/ppermute | solution.py:357
  23.4 1.9 %collective-permute-done.4.refs_2_.refs_3_ = bf16[128,1024]{1,0:T(8,128)(2,1)S(1)} collective-permute-done((bf16[128,1024]{1,0:T(8,128)(2,1)}, bf16[128,1024]{1,0:T(8,128)(2,1)S(1)}, u32[]{:S(2)}, u32[]{:S(2)}) %collective-permute-start.4) | collective-permute-done | bytes 262176 | tf_op jit(solution)/shard_map/ppermute | solution.py:357
  27.6 3.9 %shard_map.120 = (bf16[256,512]{1,0:T(8,128)(2,1)S(1)}, bf16[256,512]{1,0:T(8,128)(2,1)S(1)}) custom-call(s32[2]{0:T(128)S(1)} %pad_add_fusion.1.at, bf16[4096,1024]{1,0:T(8,128)(2,1)} %kw_ref.7, bf16[4096,1024]{1,0:T(8,128)(2,1)} %vw_ref.7, bf16[128,1024]{1,0:T(8,128)(2,1)S(1)} %collective-permute-done.2.refs_0_.refs_1_, ...), custom_call_target="tpu_custom_call" | custom-call | flops 1572864 | bytes 6144 | tf_op jit(solution)/shard_map/pallas_call | solution.py:81
  31.5 1.6 %collective-permute-start.8 = (bf16[256,512]{1,0:T(8,128)(2,1)S(1)}, bf16[256,512]{1,0:T(8,128)(2,1)S(1)}, u32[]{:S(2)}, u32[]{:S(2)}) collective-permute-start(bf16[256,512]{1,0:T(8,128)(2,1)S(1)} %get-tuple-element.97.refs_0_), channel_id=1, source_target_pairs={{0,8},{4,12},{8,0},{12,4},{16,24},{20,28},{24,16},{28,20},{1,9},{5... | collective-permute-start | bytes 786440 | tf_op jit(solution)/shard_map/ppermute | solution.py:354
  35.7 5.1 %collective-permute-done.8.refs_1_ = bf16[256,512]{1,0:T(8,128)(2,1)S(1)} collective-permute-done((bf16[256,512]{1,0:T(8,128)(2,1)S(1)}, bf16[256,512]{1,0:T(8,128)(2,1)S(1)}, u32[]{:S(2)}, u32[]{:S(2)}) %collective-permute-start.8) | collective-permute-done | bytes 262176 | tf_op jit(solution)/shard_map/ppermute | solution.py:354
  40.8 1.6 %collective-permute-start.10 = (bf16[256,512]{1,0:T(8,128)(2,1)S(1)}, bf16[256,512]{1,0:T(8,128)(2,1)S(1)}, u32[]{:S(2)}, u32[]{:S(2)}) collective-permute-start(bf16[256,512]{1,0:T(8,128)(2,1)S(1)} %collective-permute-done.8.refs_1_), channel_id=1, source_target_pairs={{0,16},{4,20},{8,24},{12,28},{16,0},{20,4},{24,8},{28,12},{1,17},{... | collective-permute-start | bytes 786440 | tf_op jit(solution)/shard_map/ppermute | solution.py:354
  44.8 3.1 %collective-permute-done.9.refs_2_ = bf16[256,512]{1,0:T(8,128)(2,1)S(1)} collective-permute-done((bf16[256,512]{1,0:T(8,128)(2,1)S(1)}, bf16[256,512]{1,0:T(8,128)(2,1)S(1)}, u32[]{:S(2)}, u32[]{:S(2)}) %collective-permute-start.9) | collective-permute-done | bytes 262176 | tf_op jit(solution)/shard_map/ppermute | solution.py:354
  48.0 4.5 %collective-permute-done.10.refs_3_ = bf16[256,512]{1,0:T(8,128)(2,1)S(1)} collective-permute-done((bf16[256,512]{1,0:T(8,128)(2,1)S(1)}, bf16[256,512]{1,0:T(8,128)(2,1)S(1)}, u32[]{:S(2)}, u32[]{:S(2)}) %collective-permute-start.10) | collective-permute-done | bytes 262176 | tf_op jit(solution)/shard_map/ppermute | solution.py:354
  54.5 6.5 %shard_map.122 = (bf16[256,512]{1,0:T(8,128)(2,1)S(1)}, bf16[256,512]{1,0:T(8,128)(2,1)S(1)}, bf16[256,1024]{1,0:T(8,128)(2,1)}, bf16[256,512]{1,0:T(8,128)(2,1)...) custom-call(s32[2]{0:T(128)S(1)} %pad_add_fusion.1.at, ...), custom_call_target="tpu_custom_call" | custom-call | flops 1966080 | bytes 4608 | tf_op jit(solution)/shard_map/pallas_call | solution.py:201
  64.6 5.7 %collective-permute-done.16 = bf16[256,512]{1,0:T(8,128)(2,1)S(1)} collective-permute-done((bf16[256,512]{1,0:T(8,128)(2,1)S(1)}, bf16[256,512]{1,0:T(8,128)(2,1)S(1)}, u32[]{:S(2)}, u32[]{:S(2)}) %collective-permute-start.16) | collective-permute-done | bytes 262176 | tf_op jit(solution)/shard_map/ppermute | solution.py:354
  73.1 2.9 %collective-permute-done.18 = bf16[256,512]{1,0:T(8,128)(2,1)S(1)} collective-permute-done((bf16[256,512]{1,0:T(8,128)(2,1)S(1)}, bf16[256,512]{1,0:T(8,128)(2,1)S(1)}, u32[]{:S(2)}, u32[]{:S(2)}) %collective-permute-start.18) | collective-permute-done | bytes 262176 | tf_op jit(solution)/shard_map/ppermute | solution.py:354
  76.8 2.8 %collective-permute-done.21 = bf16[256,512]{1,0:T(8,128)(2,1)S(1)} collective-permute-done((bf16[256,512]{1,0:T(8,128)(2,1)S(1)}, bf16[256,512]{1,0:T(8,128)(2,1)S(1)}, u32[]{:S(2)}, u32[]{:S(2)}) %collective-permute-start.21) | collective-permute-done | bytes 262176 | tf_op jit(solution)/shard_map/ppermute | solution.py:354
  83.4 3.6 %shard_map.123 = bf16[1024,128]{1,0:T(8,128)(2,1)S(1)} custom-call(s32[2]{0:T(128)S(1)} %pad_add_fusion.1.at, bf16[256,1024]{1,0:T(8,128)(2,1)S(1)} %pad_maximum_fusion.3.own_ref.refs_0_.refs_4_, bf16[256,1024]{1,0:T(8,128)(2,1)S(1)} %collective-permute-done.25.other_ref.refs_8_.refs_12_, bf16[4096,1024]{1,0:T(8,128)(2,1)} %kw_ref.7, bf16[4096,1024]{1,0:T(8,128)(2,1)} %vw_ref.7), custom_call_target="tpu_custom_call" | custom-call | flops 524288 | bytes 4096 | tf_op jit(solution)/shard_map/pallas_call | solution.py:255
  86.9 5.4 %collective-permute-start.28 = (bf16[1024,128]{1,0:T(8,128)(2,1)S(1)}, bf16[1024,128]{1,0:T(8,128)(2,1)S(1)}, u32[]{:S(2)}, u32[]{:S(2)}) collective-permute-start(bf16[1024,128]{1,0:T(8,128)(2,1)S(1)} %shard_map.123), channel_id=1, source_target_pairs={{0,2},{1,3},{2,0},{3,1},{4,6},{5,7},{6,4},{7,5},{8,10},{9,11},{10,... | collective-permute-start | bytes 786440 | tf_op jit(solution)/shard_map/ppermute | solution.py:357
  92.4 7.3 %shard_map.124 = (bf16[1024,128]{1,0:T(8,128)(2,1)S(1)}, bf16[1024,128]{1,0:T(8,128)(2,1)S(1)}, bf16[1024,128]{1,0:T(8,128)(2,1)S(1)}) custom-call(s32[2]{0:T(128)S(1)} %pad_add_fusion.1.at, bf16[256,1024]{1,0:T(8,128)(2,1)S(1)} %pad_maximum_fusion.3.own_ref.refs_0_.refs_4_, bf16[256,1024]{1,0:T(8,128)(2,1)S(1)} %collective-permute-done.25.other_ref.refs_8_.refs_12_, ...), custom_call_target="tpu_custom_call" | custom-call | flops 524288 | bytes 4096 | tf_op jit(solution)/shard_map/pallas_call | solution.py:255
  101.1 3.6 %collective-permute-start.29 = (bf16[1024,128]{1,0:T(8,128)(2,1)S(1)}, bf16[1024,128]{1,0:T(8,128)(2,1)S(1)}, u32[]{:S(2)}, u32[]{:S(2)}) collective-permute-start(bf16[1024,128]{1,0:T(8,128)(2,1)S(1)} %get-tuple-element.131), channel_id=1, source_target_pairs={{0,1},{1,2},{2,3},{3,0},{4,5},{5,6},{6,7},{7,4},{8,9},{9,10},{10,1... | collective-permute-start | bytes 786440 | tf_op jit(solution)/shard_map/ppermute | solution.py:357
  110.3 1.8 %collective-permute-done.27.refs_7_ = bf16[256,512]{1,0:T(8,128)(2,1)S(1)} collective-permute-done((bf16[256,512]{1,0:T(8,128)(2,1)S(1)}, bf16[256,512]{1,0:T(8,128)(2,1)S(1)}, u32[]{:S(2)}, u32[]{:S(2)}) %collective-permute-start.27) | collective-permute-done | bytes 262176 | tf_op jit(solution)/shard_map/ppermute | solution.py:354
  116.7 5.5 %shard_map.125 = (f32[512,1024]{1,0:T(8,128)}, f32[512,1024]{1,0:T(8,128)}) custom-call(s32[2]{0:T(128)S(1)} %pad_add_fusion.1.at, bf16[512,1024]{1,0:T(8,128)(2,1)S(1)} %pad_maximum_fusion.col_ref, bf16[256,1024]{1,0:T(8,128)(2,1)S(1)} %pad_maximum_fusion.3.own_ref.refs_0_.refs_4_, bf16[256,1024]{1,0:T(8,128)(2,1)S(1)} %collective-permute-done.22.refs_1_.refs_5_, ...), custom_call_target="tpu_custom_call" | custom-call | flops 2097152 | bytes 9216 | tf_op jit(solution)/shard_map/pallas_call | solution.py:308
  (95 shorter events, 38.9 us)
Async XLA Ops:
  0.6 22.7 %collective-permute-start.3 = (bf16[128,1024]{1,0:T(8,128)(2,1)}, bf16[128,1024]{1,0:T(8,128)(2,1)S(1)}, u32[]{:S(2)}, u32[]{:S(2)}) collective-permute-start(bf16[128,1024]{1,0:T(8,128)(2,1)} %refs_0_.2), channel_id=1, source_target_pairs={{0,2},{1,3},{2,0},{3,1},{4,6},{5,7},{6,4},{7,5},{8,10},{9,11},{10,... | collective-permute-start | bytes 786440 | tf_op jit(solution)/shard_map/ppermute | solution.py:357
  4.7 18.6 %collective-permute-start.2 = (bf16[128,1024]{1,0:T(8,128)(2,1)}, bf16[128,1024]{1,0:T(8,128)(2,1)S(1)}, u32[]{:S(2)}, u32[]{:S(2)}) collective-permute-start(bf16[128,1024]{1,0:T(8,128)(2,1)} %refs_0_.2), channel_id=1, source_target_pairs={{0,1},{1,2},{2,3},{3,0},{4,5},{5,6},{6,7},{7,4},{8,9},{9,10},{10,1... | collective-permute-start | bytes 786440 | tf_op jit(solution)/shard_map/ppermute | solution.py:357
  6.3 12.6 %collective-permute-start = (bf16[128,1024]{1,0:T(8,128)(2,1)}, bf16[128,1024]{1,0:T(8,128)(2,1)S(1)}, u32[]{:S(2)}, u32[]{:S(2)}) collective-permute-start(bf16[128,1024]{1,0:T(8,128)(2,1)} %refs_0_.2), channel_id=1, source_target_pairs={{0,4},{4,0},{8,12},{12,8},{16,20},{20,16},{24,28},{28,24},{1,5},{5... | collective-permute-start | bytes 786440 | tf_op jit(solution)/shard_map/ppermute | solution.py:354
  6.3 19.0 %collective-permute-start.4 = (bf16[128,1024]{1,0:T(8,128)(2,1)}, bf16[128,1024]{1,0:T(8,128)(2,1)S(1)}, u32[]{:S(2)}, u32[]{:S(2)}) collective-permute-start(bf16[128,1024]{1,0:T(8,128)(2,1)} %refs_0_.2), channel_id=1, source_target_pairs={{0,3},{1,0},{2,1},{3,2},{4,7},{5,4},{6,5},{7,6},{8,11},{9,8},{10,9... | collective-permute-start | bytes 786440 | tf_op jit(solution)/shard_map/ppermute | solution.py:357
  9.9 8.3 %all-to-all-start = ((s32[8,1,24]{2,1,0:T(1,128)}), s32[8,1,24]{2,1,0:T(1,128)S(1)}, u32[]{:S(2)}, u32[]{:S(2)}) async-start(s32[8,1,24]{2,1,0:T(1,128)} %broadcast_in_dim.92), calls=%async_computation | async-start | bytes 8192 | tf_op jit(solution)/shard_map/all_to_all | solution.py:326
  15.8 9.5 %collective-permute-start.1 = (bf16[256,1024]{1,0:T(8,128)(2,1)}, bf16[256,1024]{1,0:T(8,128)(2,1)S(1)}, u32[]{:S(2)}, u32[]{:S(2)}) collective-permute-start(bf16[256,1024]{1,0:T(8,128)(2,1)} %pad_maximum_fusion.2), channel_id=1, source_target_pairs={{0,4},{4,0},{8,12},{12,8},{16,20},{20,16},{24,28},{28,24},{1,5},{5... | collective-permute-start | bytes 1572872 | tf_op jit(solution)/shard_map/ppermute | solution.py:354
  31.5 9.2 %collective-permute-start.8 = (bf16[256,512]{1,0:T(8,128)(2,1)S(1)}, bf16[256,512]{1,0:T(8,128)(2,1)S(1)}, u32[]{:S(2)}, u32[]{:S(2)}) collective-permute-start(bf16[256,512]{1,0:T(8,128)(2,1)S(1)} %get-tuple-element.97.refs_0_), channel_id=1, source_target_pairs={{0,8},{4,12},{8,0},{12,4},{16,24},{20,28},{24,16},{28,20},{1,9},{5... | collective-permute-start | bytes 786440 | tf_op jit(solution)/shard_map/ppermute | solution.py:354
  33.1 9.2 %collective-permute-start.12 = (bf16[256,512]{1,0:T(8,128)(2,1)S(1)}, bf16[256,512]{1,0:T(8,128)(2,1)S(1)}, u32[]{:S(2)}, u32[]{:S(2)}) collective-permute-start(bf16[256,512]{1,0:T(8,128)(2,1)S(1)} %get-tuple-element.101.refs_4_), channel_id=1, source_target_pairs={{0,16},{4,20},{8,24},{12,28},{16,0},{20,4},{24,8},{28,12},{1,17},{... | collective-permute-start | bytes 786440 | tf_op jit(solution)/shard_map/ppermute | solution.py:354
  34.7 13.3 %collective-permute-start.9 = (bf16[256,512]{1,0:T(8,128)(2,1)S(1)}, bf16[256,512]{1,0:T(8,128)(2,1)S(1)}, u32[]{:S(2)}, u32[]{:S(2)}) collective-permute-start(bf16[256,512]{1,0:T(8,128)(2,1)S(1)} %get-tuple-element.97.refs_0_), channel_id=1, source_target_pairs={{0,16},{4,20},{8,24},{12,28},{16,0},{20,4},{24,8},{28,12},{1,17},{... | collective-permute-start | bytes 786440 | tf_op jit(solution)/shard_map/ppermute | solution.py:354
  35.2 12.8 %collective-permute-start.11 = (bf16[256,512]{1,0:T(8,128)(2,1)S(1)}, bf16[256,512]{1,0:T(8,128)(2,1)S(1)}, u32[]{:S(2)}, u32[]{:S(2)}) collective-permute-start(bf16[256,512]{1,0:T(8,128)(2,1)S(1)} %get-tuple-element.101.refs_4_), channel_id=1, source_target_pairs={{0,8},{4,12},{8,0},{12,4},{16,24},{20,28},{24,16},{28,20},{1,9},{5... | collective-permute-start | bytes 786440 | tf_op jit(solution)/shard_map/ppermute | solution.py:354
  40.8 11.7 %collective-permute-start.10 = (bf16[256,512]{1,0:T(8,128)(2,1)S(1)}, bf16[256,512]{1,0:T(8,128)(2,1)S(1)}, u32[]{:S(2)}, u32[]{:S(2)}) collective-permute-start(bf16[256,512]{1,0:T(8,128)(2,1)S(1)} %collective-permute-done.8.refs_1_), channel_id=1, source_target_pairs={{0,16},{4,20},{8,24},{12,28},{16,0},{20,4},{24,8},{28,12},{1,17},{... | collective-permute-start | bytes 786440 | tf_op jit(solution)/shard_map/ppermute | solution.py:354
  42.3 10.1 %collective-permute-start.13 = (bf16[256,512]{1,0:T(8,128)(2,1)S(1)}, bf16[256,512]{1,0:T(8,128)(2,1)S(1)}, u32[]{:S(2)}, u32[]{:S(2)}) collective-permute-start(bf16[256,512]{1,0:T(8,128)(2,1)S(1)} %collective-permute-done.12.refs_6_), channel_id=1, source_target_pairs={{0,8},{4,12},{8,0},{12,4},{16,24},{20,28},{24,16},{28,20},{1,9},{5... | collective-permute-start | bytes 786440 | tf_op jit(solution)/shard_map/ppermute | solution.py:354
  52.4 8.5 %collective-permute-start.14 = (bf16[512,256]{1,0:T(8,128)(2,1)S(1)}, bf16[512,256]{1,0:T(8,128)(2,1)S(1)}, u32[]{:S(2)}, u32[]{:S(2)}) collective-permute-start(bf16[512,256]{1,0:T(8,128)(2,1)S(1)} %get-tuple-element.115), channel_id=1, source_target_pairs={{0,8},{4,12},{8,0},{12,4},{16,24},{20,28},{24,16},{28,20},{1,9},{5... | collective-permute-start | bytes 786440 | tf_op jit(solution)/shard_map/ppermute | solution.py:354
  52.9 8.0 %collective-permute-start.15 = (bf16[512,256]{1,0:T(8,128)(2,1)S(1)}, bf16[512,256]{1,0:T(8,128)(2,1)S(1)}, u32[]{:S(2)}, u32[]{:S(2)}) collective-permute-start(bf16[512,256]{1,0:T(8,128)(2,1)S(1)} %get-tuple-element.116), channel_id=1, source_target_pairs={{0,16},{4,20},{8,24},{12,28},{16,0},{20,4},{24,8},{28,12},{1,17},{... | collective-permute-start | bytes 786440 | tf_op jit(solution)/shard_map/ppermute | solution.py:354
  61.0 9.3 %collective-permute-start.16 = (bf16[256,512]{1,0:T(8,128)(2,1)S(1)}, bf16[256,512]{1,0:T(8,128)(2,1)S(1)}, u32[]{:S(2)}, u32[]{:S(2)}) collective-permute-start(bf16[256,512]{1,0:T(8,128)(2,1)S(1)} %get-tuple-element.118), channel_id=1, source_target_pairs={{0,16},{4,20},{8,24},{12,28},{16,0},{20,4},{24,8},{28,12},{1,17},{... | collective-permute-start | bytes 786440 | tf_op jit(solution)/shard_map/ppermute | solution.py:354
  61.5 11.0 %collective-permute-start.19 = (bf16[256,512]{1,0:T(8,128)(2,1)S(1)}, bf16[256,512]{1,0:T(8,128)(2,1)S(1)}, u32[]{:S(2)}, u32[]{:S(2)}) collective-permute-start(bf16[256,512]{1,0:T(8,128)(2,1)S(1)} %get-tuple-element.122), channel_id=1, source_target_pairs={{0,8},{4,12},{8,0},{12,4},{16,24},{20,28},{24,16},{28,20},{1,9},{5... | collective-permute-start | bytes 786440 | tf_op jit(solution)/shard_map/ppermute | solution.py:354
  63.1 12.9 %collective-permute-start.18 = (bf16[256,512]{1,0:T(8,128)(2,1)S(1)}, bf16[256,512]{1,0:T(8,128)(2,1)S(1)}, u32[]{:S(2)}, u32[]{:S(2)}) collective-permute-start(bf16[256,512]{1,0:T(8,128)(2,1)S(1)} %get-tuple-element.120), channel_id=1, source_target_pairs={{0,16},{4,20},{8,24},{12,28},{16,0},{20,4},{24,8},{28,12},{1,17},{... | collective-permute-start | bytes 786440 | tf_op jit(solution)/shard_map/ppermute | solution.py:354
  79.8 24.8 %collective-permute-start.23 = (bf16[256,1024]{1,0:T(8,128)(2,1)S(1)}, bf16[256,1024]{1,0:T(8,128)(2,1)S(1)}, u32[]{:S(2)}, u32[]{:S(2)}) collective-permute-start(bf16[256,1024]{1,0:T(8,128)(2,1)S(1)} %pad_maximum_fusion.3.own_ref.refs_0_.refs_4_), channel_id=1, source_target_pairs={{0,16},{4,20},{8,24},{12,28},{16,0},{20,4},{24,8},{28,12},{1,17},{... | collective-permute-start | bytes 1572872 | tf_op jit(solution)/shard_map/ppermute | solution.py:354
  81.0 23.6 %collective-permute-start.22 = (bf16[256,1024]{1,0:T(8,128)(2,1)S(1)}, bf16[256,1024]{1,0:T(8,128)(2,1)S(1)}, u32[]{:S(2)}, u32[]{:S(2)}) collective-permute-start(bf16[256,1024]{1,0:T(8,128)(2,1)S(1)} %pad_maximum_fusion.3.own_ref.refs_0_.refs_4_), channel_id=1, source_target_pairs={{0,8},{4,12},{8,0},{12,4},{16,24},{20,28},{24,16},{28,20},{1,9},{5... | collective-permute-start | bytes 1572872 | tf_op jit(solution)/shard_map/ppermute | solution.py:354
  82.5 24.9 %collective-permute-start.30 = (bf16[256,1024]{1,0:T(8,128)(2,1)}, bf16[256,1024]{1,0:T(8,128)(2,1)}, u32[]{:S(2)}, u32[]{:S(2)}) collective-permute-start(bf16[256,1024]{1,0:T(8,128)(2,1)} %get-tuple-element.138), channel_id=1, source_target_pairs={{0,4},{4,0},{8,12},{12,8},{16,20},{20,16},{24,28},{28,24},{1,5},{5... | collective-permute-start | bytes 1572872 | tf_op jit(solution)/shard_map/ppermute | solution.py:354
  82.5 18.6 %collective-permute-start.24 = (bf16[512,256]{1,0:T(8,128)(2,1)S(1)}, bf16[512,256]{1,0:T(8,128)(2,1)}, u32[]{:S(2)}, u32[]{:S(2)}) collective-permute-start(bf16[512,256]{1,0:T(8,128)(2,1)S(1)} %get-tuple-element.130), channel_id=1, source_target_pairs={{0,24},{4,28},{8,16},{12,20},{16,8},{20,12},{24,0},{28,4},{1,25},{... | collective-permute-start | bytes 786440 | tf_op jit(solution)/shard_map/ppermute | solution.py:354
  86.9 23.3 %collective-permute-start.28 = (bf16[1024,128]{1,0:T(8,128)(2,1)S(1)}, bf16[1024,128]{1,0:T(8,128)(2,1)S(1)}, u32[]{:S(2)}, u32[]{:S(2)}) collective-permute-start(bf16[1024,128]{1,0:T(8,128)(2,1)S(1)} %shard_map.123), channel_id=1, source_target_pairs={{0,2},{1,3},{2,0},{3,1},{4,6},{5,7},{6,4},{7,5},{8,10},{9,11},{10,... | collective-permute-start | bytes 786440 | tf_op jit(solution)/shard_map/ppermute | solution.py:357
  101.1 12.2 %collective-permute-start.29 = (bf16[1024,128]{1,0:T(8,128)(2,1)S(1)}, bf16[1024,128]{1,0:T(8,128)(2,1)S(1)}, u32[]{:S(2)}, u32[]{:S(2)}) collective-permute-start(bf16[1024,128]{1,0:T(8,128)(2,1)S(1)} %get-tuple-element.131), channel_id=1, source_target_pairs={{0,1},{1,2},{2,3},{3,0},{4,5},{5,6},{6,7},{7,4},{8,9},{9,10},{10,1... | collective-permute-start | bytes 786440 | tf_op jit(solution)/shard_map/ppermute | solution.py:357
  114.3 8.9 %collective-permute-start.31 = (bf16[1024,128]{1,0:T(8,128)(2,1)S(1)}, bf16[1024,128]{1,0:T(8,128)(2,1)S(1)}, u32[]{:S(2)}, u32[]{:S(2)}) collective-permute-start(bf16[1024,128]{1,0:T(8,128)(2,1)S(1)} %get-tuple-element.132), channel_id=1, source_target_pairs={{0,3},{1,0},{2,1},{3,2},{4,7},{5,4},{6,5},{7,6},{8,11},{9,8},{10,9... | collective-permute-start | bytes 786440 | tf_op jit(solution)/shard_map/ppermute | solution.py:357
  (18 other events, 119.7 us)
